TPU v7x, 512 devices: a whole 4x8x8 slice. The times are simulated.
512 devices in a mesh: gx: 64 (over z, x, core), gy: 8 (over y).
Axes of the slice: x: 4, y: 8, z: 8, core: 2. Of those that a mesh axis runs over, the one named last changes fastest.
Arguments:
- material_fraction: float32 [256, 128, 256], P('gx', 'gy'), may hold values from 0.02 to 0.98
- primal_warmth: float32 [256, 128, 256], P('gx', 'gy'), may hold values from 0 to 7, as said below
- empty_region_flags: int32 [256, 128, 256], P('gx', 'gy'), may hold values 0 or 1
- dirichlet_flags: int32 [256, 128, 256], P('gx', 'gy'), may hold values 0 or 1
Outputs:
- dual_field_final: float32 [256, 128, 256], P('gx', 'gy')
- sensitivity: float32 [256, 128, 256], P('gx', 'gy')
Inputs may be any that keep to these rules, and one draw needn't show every extreme that they name: `primal_warmth`: positive temperatures.
All inputs are finite; a program needn't handle non-finite values. No bound on the sum of `empty_region_flags` or of `dirichlet_flags` on one device may be relied on, other than what follows from the above.
Results may differ from a plain program's by a relative error of at most 0.003.
Values sent between devices are 32-bit elements; how exact they have to be, the bound alone decides.
No kernel may reach another device: no remote copies, remote signals or barrier semaphores. Data moves between devices by JAX's collectives and lax.ppermute only.
A program may use at most 64 MiB of HBM per device.

v0:
```python
import math

import jax
import jax.numpy as jnp
from jax import lax
from jax.sharding import PartitionSpec as P

ITERS = 3


KMIN = 0.05
QZERO = 1.0


def extended(cells, sides, width):
    for axis, dim in sides:
        count = lax.axis_size(axis)
        ends = count - 1
        head = lax.slice_in_dim(cells, 0, width, axis=dim)
        tail = lax.slice_in_dim(cells, cells.shape[dim] - width, cells.shape[dim], axis=dim)
        cells = jnp.concatenate(
            [
                lax.ppermute(tail, axis, [(i, (i + 1) % count) for i in range(ends)]),
                cells,
                lax.ppermute(head, axis, [((i + 1) % count, i) for i in range(ends)]),
            ],
            axis=dim,
        )
    return cells


def filter_taps():
    taps = []
    for dx in (-1, 0, 1):
        for dy in (-1, 0, 1):
            for dz in (-1, 0, 1):
                count = abs(dx) + abs(dy) + abs(dz)
                if count < 3:
                    weight = 1.5 if count == 0 else 0.5 if count == 1 else 1.5 - math.sqrt(2.0)
                    taps.append((dx, dy, dz, weight))
    return taps


def lift(arr):
    return jnp.concatenate([arr[..., 1:], jnp.zeros_like(arr[..., :1])], axis=-1)


def lower_z(arr):
    return jnp.concatenate([jnp.zeros_like(arr[..., :1]), arr[..., :-1]], axis=-1)


def along_z(arr, step):
    if step == 1:
        return lift(arr)
    if step == -1:
        return lower_z(arr)
    return arr


def filter_sum(padded, start, element_columns, element_row_count):
    total = None
    for dx, dy, dz, weight in filter_taps():
        piece = along_z(
            padded[
                start + dx : start + dx + element_columns,
                start + dy : start + dy + element_row_count,
            ],
            dz,
        )
        total = weight * piece if total is None else total + weight * piece
    return total


def vertex_values(padded, start, element_columns, element_row_count):
    corners = {}
    for a in (0, 1):
        for b in (0, 1):
            base = padded[
                start + a : start + a + element_columns, start + b : start + b + element_row_count
            ]
            corners[a, b, 0] = base
            corners[a, b, 1] = lift(base)
    return corners


def conductance_operator(corners):
    total = sum(corners.values())
    result = {}
    for (a, b, c), value in corners.items():
        near = corners[1 - a, b, c] + corners[a, 1 - b, c] + corners[a, b, 1 - c]
        result[a, b, c] = (5.0 * value + near - total) / 12.0
    return result


def assemble(weight, parts, element_columns, element_row_count):
    total = None
    for (a, b, c), value in parts.items():
        piece = along_z(
            (weight * value)[1 - a : 1 - a + element_columns, 1 - b : 1 - b + element_row_count], -c
        )
        total = piece if total is None else total + piece
    return total


def within(first, limit):
    return ((first >= 0) & (first < limit)).astype(jnp.float32)


def inside_rows(count):
    first = lax.axis_index("gx") * count + jnp.arange(count + 4, dtype=jnp.int32) - 2
    return within(first, count * lax.axis_size("gx"))


def inside_cols(count):
    first = lax.axis_index("gy") * count + jnp.arange(count + 4, dtype=jnp.int32) - 2
    return within(first, count * lax.axis_size("gy"))


def body(material_fraction, primal_warmth, empty_region_flags, dirichlet_flags):
    cx, cy, cz = material_fraction.shape
    movable_points = (1 - dirichlet_flags).astype(jnp.float32)
    fixed = dirichlet_flags.astype(jnp.float32)
    thermal_forcing = empty_region_flags.astype(jnp.float32)
    movable_warmth = movable_points * primal_warmth
    design_pad = extended(material_fraction, (("gx", 0), ("gy", 1)), 2)
    valid_pad = (
        inside_rows(cx)[:, None, None]
        * inside_cols(cy)[None, :, None]
        * jnp.ones((1, 1, cz), jnp.float32)
    )
    hs_ext = filter_sum(valid_pad, 1, cx + 2, cy + 2)
    rho_ext = filter_sum(design_pad, 1, cx + 2, cy + 2) / hs_ext
    valid_elem = valid_pad[1:-1, 1:-1]
    solid = 1.0 - rho_ext
    conduct_ext = valid_elem * (KMIN + (1.0 - KMIN) * solid**3)
    slope_k = valid_elem * (-3.0 * (1.0 - KMIN) * solid**2)
    slope_q = valid_elem * (-3.0 * QZERO * solid**2)
    conduct = conduct_ext[: cx + 1, : cy + 1]
    ones = {(a, b, c): jnp.ones_like(conduct) for a in (0, 1) for b in (0, 1) for c in (0, 1)}
    diag = movable_points * assemble(conduct / 3.0, ones, cx, cy) + fixed

    def precond_product(residual, precond):
        return lax.psum(jnp.sum(residual * precond), ("gx", "gy"))

    forcing_vector = thermal_forcing * movable_warmth
    dual_field_final = jnp.zeros_like(forcing_vector)
    residual = forcing_vector
    precond = residual / diag
    direction = precond
    rz_now = precond_product(residual, precond)
    for step in range(ITERS):
        padded = extended(movable_points * direction, (("gx", 0), ("gy", 1)), 1)
        local = conductance_operator(vertex_values(padded, 0, cx + 1, cy + 1))
        image = movable_points * assemble(conduct, local, cx, cy) + fixed * direction
        alpha = rz_now / lax.psum(jnp.sum(direction * image), ("gx", "gy"))
        dual_field_final = dual_field_final + alpha * direction
        residual = residual - alpha * image
        if step + 1 < ITERS:
            precond = residual / diag
            rz_next = precond_product(residual, precond)
            direction = precond + rz_next / rz_now * direction
            rz_now = rz_next
    state_arrays = extended(
        jnp.stack([movable_warmth, dual_field_final]), (("gx", 1), ("gy", 2)), 2
    )
    temp_pad = state_arrays[0]
    adjoint_pad = state_arrays[1]
    thermal_load = conductance_operator(vertex_values(temp_pad, 1, cx + 2, cy + 2))
    adj_corners = vertex_values(adjoint_pad, 1, cx + 2, cy + 2)
    energy = sum((adj_corners[key] * thermal_load[key] for key in thermal_load))
    adj_total = sum(adj_corners.values())
    srho = valid_elem * (-slope_k * energy + slope_q / 8.0 * adj_total)
    sensitivity = filter_sum(srho / hs_ext, 1, cx, cy)
    return (dual_field_final, sensitivity)


def solution(mesh):
    placed = (P("gx", "gy", None), P("gx", "gy", None), P("gx", "gy", None), P("gx", "gy", None))
    return jax.shard_map(
        body,
        mesh=mesh,
        in_specs=placed,
        out_specs=(P("gx", "gy", None), P("gx", "gy", None)),
        check_vma=False,
    )
```

profile of v0, /device:TPU:1, one launch (start us, length us, event | category | flops | bytes accessed | tf_op | source)
XLA Modules:
  0.0 602.4 jit_solution(2739071449226996792)
XLA Ops:
  0.6 0.8 fusion.203
  1.4 8.9 %collective-permute-start.1 = (f32[2,16,256]{2,1,0:T(8,128)S(1)}, f32[2,16,256]{2,1,0:T(8,128)S(1)}, u32[]{:S(2)}, u32[]{:S(2)}) collective-permute-start(f32[2,16,256]{2,1,0:T(8,128)S(1)} %get-tuple-element.127), channel_id=1, source_target_pairs={{8,0},{16,8},{24,16},{32,24},{40,32},{48,40},{56,48},{64,56},{72,6... | collective-permute-start | bytes 98312 | tf_op jit(solution)/shard_map/ppermute | solution.py:25
  10.3 1.9 collective-permute-start
  12.4 1.1 collective-permute-done
  13.5 1.3 collective-permute-start.2
  14.8 1.3 collective-permute-start.3
  16.2 3.0 collective-permute-done.3
  19.3 0.3 fusion.28
  19.6 0.1 slice.611
  20.0 0.8 fusion.186
  20.8 0.1 broadcast_multiply_fusion
  21.0 0.8 copy-done
  21.8 0.1 convert_multiply_fusion.2
  22.0 5.2 collective-permute-start.4
  27.2 1.9 collective-permute-start.5
  29.1 3.1 collective-permute-done.5
  32.3 1.4 collective-permute-start.6
  33.6 1.3 collective-permute-start.7
  34.9 3.4 collective-permute-done.7
  38.4 0.1 fusion.196
  38.5 0.1 fusion.197
  38.7 0.1 slice_add_fusion.15
  38.8 0.1 fusion.48
  38.9 0.8 multiply_reduce_fusion.3
  39.7 110.8 %all-reduce.66 = (f32[]{:T(128)}, f32[]{:T(128)}) all-reduce(f32[]{:T(128)} %get-tuple-element.3, f32[]{:T(128)} %get-tuple-element.2), channel_id=1, replica_groups=mesh['gx'=64,'gy'=8] {'gx','gy'}, use_global_device_ids=true, to_apply=%region_1.0 | all-reduce | flops 2 | bytes 16 | tf_op jit(solution)/shard_map/psum | solution.py:143
  151.9 0.6 multiply_reduce_fusion.2
  152.5 95.0 %psum.44 = f32[]{:T(128)} all-reduce(f32[]{:T(128)} %get-tuple-element.12), channel_id=1, replica_groups=mesh['gx'=64,'gy'=8] {'gx','gy'}, use_global_device_ids=true, to_apply=%region_5.0 | all-reduce | flops 1 | bytes 8 | tf_op jit(solution)/shard_map/psum | solution.py:143
  248.9 4.2 collective-permute-start.8
  253.2 1.9 collective-permute-start.9
  255.1 3.1 collective-permute-done.9
  258.2 3.3 collective-permute-start.10
  261.6 1.3 collective-permute-start.11
  262.9 3.1 collective-permute-done.11
  266.0 0.1 fusion.194
  266.1 0.1 fusion.195
  266.2 0.1 slice_add_fusion.13
  266.4 0.1 fusion.60
  266.5 0.8 multiply_reduce_fusion.1
  267.3 99.7 %psum.45 = f32[]{:T(128)} all-reduce(f32[]{:T(128)} %get-tuple-element.8), channel_id=1, replica_groups=mesh['gx'=64,'gy'=8] {'gx','gy'}, use_global_device_ids=true, to_apply=%region_7.0 | all-reduce | flops 1 | bytes 8 | tf_op jit(solution)/shard_map/psum | solution.py:155
  368.4 0.6 multiply_reduce_fusion
  369.0 95.0 %psum.46 = f32[]{:T(128)} all-reduce(f32[]{:T(128)} %multiply_reduce_fusion), channel_id=1, replica_groups=mesh['gx'=64,'gy'=8] {'gx','gy'}, use_global_device_ids=true, to_apply=%region_9.0 | all-reduce | flops 1 | bytes 8 | tf_op jit(solution)/shard_map/psum | solution.py:143
  465.4 4.6 collective-permute-start.12
  470.0 1.9 collective-permute-start.13
  471.9 3.1 collective-permute-done.13
  475.1 1.8 collective-permute-start.14
  476.9 1.3 collective-permute-start.15
  478.2 3.7 collective-permute-done.15
  482.0 0.1 fusion.192
  482.1 0.1 fusion.193
  482.2 0.1 slice_add_fusion.11
  482.4 0.1 fusion.72
  482.5 0.8 fusion.179
  483.3 100.3 %psum.47 = f32[]{:T(128)} all-reduce(f32[]{:T(128)} %fusion.179), channel_id=1, replica_groups=mesh['gx'=64,'gy'=8] {'gx','gy'}, use_global_device_ids=true, to_apply=%region_11.0 | all-reduce | flops 1 | bytes 8 | tf_op jit(solution)/shard_map/psum | solution.py:155
  585.0 2.6 collective-permute-start.16
  587.5 1.9 collective-permute-start.17
  589.5 3.6 collective-permute-done.17
  593.1 1.4 collective-permute-start.18
  594.5 1.3 collective-permute-start.19
  595.8 4.3 collective-permute-done.19
  600.2 0.2 fusion.188
  600.5 0.2 fusion.189
  600.7 0.8 multiply_divide_fusion
  601.4 0.2 fusion.191
  601.6 0.8 fusion.74
  (53 shorter events, 1.2 us)
Async XLA Ops:
  1.4 12.0 %copy-start.2 = (f32[4,16,256]{2,1,0:T(8,128)S(1)}, f32[4,16,256]{2,1,0:T(8,128)}, u32[]{:S(2)}) copy-start(f32[4,16,256]{2,1,0:T(8,128)} %param.4) | copy-start | bytes 196612
  1.4 12.0 %collective-permute-start.1 = (f32[2,16,256]{2,1,0:T(8,128)S(1)}, f32[2,16,256]{2,1,0:T(8,128)S(1)}, u32[]{:S(2)}, u32[]{:S(2)}) collective-permute-start(f32[2,16,256]{2,1,0:T(8,128)S(1)} %get-tuple-element.127), channel_id=1, source_target_pairs={{8,0},{16,8},{24,16},{32,24},{40,32},{48,40},{56,48},{64,56},{72,6... | collective-permute-start | bytes 98312 | tf_op jit(solution)/shard_map/ppermute | solution.py:25
  10.3 3.1 collective-permute-start
  13.5 2.8 collective-permute-start.2
  14.8 4.5 collective-permute-start.3
  20.9 0.8 copy-start
  20.9 0.9 copy-start.3
  20.9 0.9 copy-start.4
  22.0 7.1 %collective-permute-start.4 = (f32[1,16,256]{2,1,0:T(8,128)S(1)}, f32[1,16,256]{2,1,0:T(8,128)S(1)}, u32[]{:S(2)}, u32[]{:S(2)}) collective-permute-start(f32[1,16,256]{2,1,0:T(8,128)S(1)} %get-tuple-element.125), channel_id=1, source_target_pairs={{0,8},{8,16},{16,24},{24,32},{32,40},{40,48},{48,56},{56,64},{64,7... | collective-permute-start | bytes 49160 | tf_op jit(solution)/shard_map/ppermute | solution.py:23
  27.2 5.1 collective-permute-start.5
  32.3 2.7 collective-permute-start.6
  33.6 4.8 collective-permute-start.7
  248.9 6.2 %collective-permute-start.8 = (f32[1,16,256]{2,1,0:T(8,128)S(1)}, f32[1,16,256]{2,1,0:T(8,128)S(1)}, u32[]{:S(2)}, u32[]{:S(2)}) collective-permute-start(f32[1,16,256]{2,1,0:T(8,128)S(1)} %get-tuple-element.123), channel_id=1, source_target_pairs={{0,8},{8,16},{16,24},{24,32},{32,40},{40,48},{48,56},{56,64},{64,7... | collective-permute-start | bytes 49160 | tf_op jit(solution)/shard_map/ppermute | solution.py:23
  253.2 5.1 collective-permute-start.9
  258.2 4.7 collective-permute-start.10
  261.6 4.4 collective-permute-start.11
  465.4 6.5 %collective-permute-start.12 = (f32[1,16,256]{2,1,0:T(8,128)S(1)}, f32[1,16,256]{2,1,0:T(8,128)S(1)}, u32[]{:S(2)}, u32[]{:S(2)}) collective-permute-start(f32[1,16,256]{2,1,0:T(8,128)S(1)} %get-tuple-element.121), channel_id=1, source_target_pairs={{0,8},{8,16},{16,24},{24,32},{32,40},{40,48},{48,56},{56,64},{64,7... | collective-permute-start | bytes 49160 | tf_op jit(solution)/shard_map/ppermute | solution.py:23
  470.0 5.1 collective-permute-start.13
  475.1 3.2 collective-permute-start.14
  476.9 5.0 collective-permute-start.15
  584.9 15.2 %copy-start.1 = (f32[4,16,256]{2,1,0:T(8,128)}, f32[4,16,256]{2,1,0:T(8,128)S(1)}, u32[]{:S(2)}) copy-start(f32[4,16,256]{2,1,0:T(8,128)S(1)} %multiply_add_fusion) | copy-start | bytes 196612
  585.0 4.5 collective-permute-start.16
  587.5 5.6 collective-permute-start.17
  593.1 2.7 collective-permute-start.18
  594.5 5.6 collective-permute-start.19
where the time goes:
time: 608 us; the launch traced here: 602 us
  blocking collectives  501 us (82%)
  starting transfers between devices  50.7 us (8%)
  waiting for transfers between devices  31.6 us (5%)
  between operations  7.91 us (1%)
  other arithmetic  7.73 us (1%)
    psum x3, blocking collectives, precond_product(): return lax.psum(jnp.sum(residual * precond), ('gx', 'gy'))  301 us
    psum x2, blocking collectives, body(): alpha = rz_now / lax.psum(jnp.sum(direction * image), ('gx', 'gy'))  200 us
    ppermute x10, waiting for transfers between devices, extended(): lax.ppermute(head, axis, [((i + 1) % count, i) for i in range(ends)])  30.6 us
    ppermute x10, starting transfers between devices, extended(): lax.ppermute(tail, axis, [(i, (i + 1) % count) for i in range(ends)])  27.7 us
    ppermute x10, starting transfers between devices, extended(): lax.ppermute(head, axis, [((i + 1) % count, i) for i in range(ends)])  23.1 us
  transfers between devices with their start and end apart: 20, of which 10 were waited for; matrix products, arithmetic and copies ran while one was open for 0% of the time, Pallas kernels for 0%

commit v1 on v0

v1 whole, which is shorter than its diff:
```python
import functools
import math

import jax
import jax.numpy as jnp
from jax import lax
from jax.experimental import pallas as pl
from jax.experimental.pallas import tpu as pltpu
from jax.sharding import PartitionSpec as P

KMIN = 0.05
QZERO = 1.0
EDGE = 0.5
DIAGONAL = 1.5 - math.sqrt(2.0)

WIDE = 8
NEAR = 4
BASIS = 3
MOMENTS = 8


def up(arr, axis):
    return pltpu.roll(arr, arr.shape[axis] - 1, axis)


def down(arr, axis):
    return pltpu.roll(arr, 1, axis)


def z_index(arr):
    return lax.broadcasted_iota(jnp.int32, arr.shape, 1)


def lift(arr):
    return jnp.where(z_index(arr) == arr.shape[1] - 1, 0.0, up(arr, 1))


def lower_z(arr):
    return jnp.where(z_index(arr) == 0, 0.0, down(arr, 1))


def filtered(below, here, above):
    beside = below + above
    rim = up(here, 0) + down(here, 0)
    corner = up(beside, 0) + down(beside, 0)
    flat = 1.5 * here + EDGE * (beside + rim) + DIAGONAL * corner
    slanted = EDGE * here + DIAGONAL * (beside + rim)
    return flat + lift(slanted) + lower_z(slanted)


def grid_flags(layer, layers, first_layer, first_row, rows, shape):
    def inside(at):
        return ((at >= 0) & (at < layers)).astype(jnp.float32)

    at = first_layer + layer
    row = first_row + lax.broadcasted_iota(jnp.int32, shape, 0)

    def row_inside(offset):
        return ((row + offset >= 0) & (row + offset < rows)).astype(jnp.float32)

    return inside(at), inside(at - 1) + inside(at + 1), row_inside(0), row_inside(-1) + row_inside(1)


def filter_weight(layer, layers, first_layer, first_row, rows, shape):
    here, beside, row_here, row_beside = grid_flags(
        layer, layers, first_layer, first_row, rows, shape
    )
    z = lax.broadcasted_iota(jnp.int32, shape, 1)
    z_beside = (z > 0).astype(jnp.float32) + (z < shape[1] - 1).astype(jnp.float32)
    flat = (1.5 + EDGE * beside) * row_here + (EDGE + DIAGONAL * beside) * row_beside
    slanted = (EDGE + DIAGONAL * beside) * row_here + DIAGONAL * row_beside
    valid = here * row_here
    return valid, jnp.where(valid > 0, flat + z_beside * slanted, 1.0)


def yz_modes(node):
    lifted = lift(node)
    plain, slope = node + lifted, lifted - node
    plain_up, slope_up = up(plain, 0), up(slope, 0)
    return plain + plain_up, slope + slope_up, plain_up - plain, slope_up - slope


def element_modes(low, high):
    return {
        "d0": (3.0, high[0] - low[0]),
        "s1": (3.0, high[1] + low[1]),
        "s2": (3.0, high[2] + low[2]),
        "d1": (2.0, high[1] - low[1]),
        "d2": (2.0, high[2] - low[2]),
        "s3": (2.0, high[3] + low[3]),
        "d3": (1.0, high[3] - low[3]),
    }


def apply_layers(node_at, conduct_at, first, count):
    low = yz_modes(node_at(first - 1))
    carried = None
    for element in range(first - 1, first + count):
        high = yz_modes(node_at(element + 1))
        scaled = conduct_at(element) * (1.0 / 48.0)
        flow = {key: (order * value) * scaled for key, (order, value) in element_modes(low, high).items()}
        zero_sum = flow["d0"]
        if carried is not None:
            planes = (
                carried[0] - zero_sum,
                carried[1] + (flow["s1"] - flow["d1"]),
                carried[2] + (flow["s2"] - flow["d2"]),
                carried[3] + (flow["s3"] - flow["d3"]),
            )
            smooth = (planes[0] - planes[2]) + down(planes[0] + planes[2], 0)
            slope = (planes[1] - planes[3]) + down(planes[1] + planes[3], 0)
            yield element, (smooth - slope) + lower_z(smooth + slope)
        carried = (
            zero_sum,
            flow["s1"] + flow["d1"],
            flow["s2"] + flow["d2"],
            flow["s3"] + flow["d3"],
        )
        low = high


def tile_sum(value):
    return functools.reduce(
        jnp.add,
        [
            value[r : r + 8, c : c + 128]
            for r in range(0, value.shape[0], 8)
            for c in range(0, value.shape[1], 128)
        ],
    )


def basis_kernel(
    n, own_rows, layers, rows,
    design_ref, free_ref, rhs_ref, lo_ref, hi_ref, below_ref, above_ref,
    moments_ref, basis_ref, solid_ref,
    conduct_s, diag_s, inv_s, u0_s, u1_s,
):
    first_layer = lax.axis_index("gx") * n
    first_row = lax.axis_index("gy") * own_rows
    wide_rows = own_rows + 2 * WIDE
    near_rows = own_rows + 2 * NEAR
    wide_tiles, near_tiles = wide_rows // 8, near_rows // 8
    z = design_ref.shape[-1]

    def design_at(i):
        if i == -n - 1:
            return below_ref[0]
        if i == 2 * n:
            return above_ref[0]
        if 0 <= i < n:
            return design_ref[i]
        ref, at = (lo_ref, i + n) if i < 0 else (hi_ref, i - n)
        return ref[at * wide_tiles : (at + 1) * wide_tiles].reshape(wide_rows, z)

    def node_at(which, own_ref):
        def at(i):
            if 0 <= i < n:
                return own_ref[i]
            if i < 0:
                start = n * wide_tiles + (which * (n - 1) + i + n - 1) * near_tiles
                return lo_ref[start : start + near_tiles].reshape(near_rows, z)
            start = n * wide_tiles + (which * n + i - n) * near_tiles
            return hi_ref[start : start + near_tiles].reshape(near_rows, z)

        return at

    free_at, rhs_at = node_at(0, free_ref), node_at(1, rhs_ref)

    for i in range(-n, 2 * n):
        valid, weight = filter_weight(i, layers, first_layer, first_row - WIDE, rows, (wide_rows, z))
        solid = 1.0 - filtered(design_at(i - 1), design_at(i), design_at(i + 1)) / weight
        solid = solid[WIDE - NEAR : wide_rows - WIDE + NEAR]
        valid = valid[WIDE - NEAR : wide_rows - WIDE + NEAR]
        conduct_s[i + n] = jnp.where(valid > 0, KMIN + (1.0 - KMIN) * (solid * solid * solid), 0.0)
        if -1 <= i <= n:
            solid_ref[i + 1] = solid

    for i in range(1 - n, 2 * n):
        pair = conduct_s[i + n] + conduct_s[i + n - 1]
        pair = pair + down(pair, 0)
        pair = pair + lower_z(pair)
        free = free_at(i)
        diag = free * (pair * (1.0 / 3.0)) + (1.0 - free)
        inverse = 1.0 / diag
        diag_s[i + n - 1] = diag
        inv_s[i + n - 1] = inverse
        u0_s[i + n - 1] = rhs_at(i) * inverse

    row = lax.broadcasted_iota(jnp.int32, (near_rows, z), 0)
    own = (row >= NEAR) & (row < NEAR + own_rows)
    sums = [jnp.zeros((8, 128), jnp.float32) for _ in range(MOMENTS)]

    def gather(which, product):
        sums[which] = sums[which] + tile_sum(jnp.where(own, product, 0.0))

    def conduct_at(i):
        return conduct_s[i + n]

    for i, image in apply_layers(
        lambda i: free_at(i) * u0_s[i + n - 1], conduct_at, 2 - n, 3 * n - 3
    ):
        free, start = free_at(i), u0_s[i + n - 1]
        image = free * image + (1.0 - free) * start
        later = image * inv_s[i + n - 1] - start
        u1_s[i + n - 2] = later
        if -1 <= i <= n + 1:
            basis_ref[0, i + 1] = start
        if 0 <= i < n:
            gather(0, start * image)
            gather(1, later * image)
            gather(5, rhs_at(i) * start)
            gather(6, rhs_at(i) * later)
    for i, image in apply_layers(
        lambda i: free_at(i) * u1_s[i + n - 2], conduct_at, -1, n + 3
    ):
        free, start = free_at(i), u1_s[i + n - 2]
        image = free * image + (1.0 - free) * start
        later = image * inv_s[i + n - 1] - start
        basis_ref[1, i + 1] = start
        basis_ref[2, i + 1] = later
        if 0 <= i < n:
            gather(2, start * image)
            gather(3, later * image)
            gather(7, rhs_at(i) * later)
    low = yz_modes(free_at(0) * basis_ref[2, 1])
    for i in range(n):
        high = yz_modes(free_at(i + 1) * basis_ref[2, i + 2])
        square = sum(order * value * value for order, value in element_modes(low, high).values())
        last = basis_ref[2, i + 1]
        gather(4, square * (conduct_at(i) * (1.0 / 48.0)) + (1.0 - free_at(i)) * last * last)
        low = high

    lane = lax.broadcasted_iota(jnp.int32, (1, 128), 1)
    total = jnp.zeros((1, 128), jnp.float32)
    for k in range(MOMENTS):
        total = total + jnp.where(lane == k, jnp.sum(sums[k], axis=(0, 1), keepdims=True), 0.0)
    moments_ref[...] = jnp.broadcast_to(total, moments_ref.shape)


def sensitivity_kernel(
    n, own_rows, layers, rows,
    basis_ref, solid_ref, warmth_ref, lo_ref, hi_ref,
    parts_ref,
    scaled_s,
):
    first_layer = lax.axis_index("gx") * n
    first_row = lax.axis_index("gy") * own_rows
    near_rows = own_rows + 2 * NEAR
    near_tiles = near_rows // 8
    z = solid_ref.shape[-1]
    shape = (near_rows, z)

    def warmth_at(i):
        if 0 <= i < n:
            return warmth_ref[i]
        if i < 0:
            return lo_ref[lo_ref.shape[0] - near_tiles :].reshape(shape)
        start = hi_ref.shape[0] - (n + 2 - i) * near_tiles
        return hi_ref[start : start + near_tiles].reshape(shape)

    warm_low = yz_modes(warmth_at(-1))
    lows = [yz_modes(basis_ref[k, 0]) for k in range(BASIS)]
    for i in range(-1, n + 1):
        warm_high = yz_modes(warmth_at(i + 1))
        valid, weight = filter_weight(i, layers, first_layer, first_row - NEAR, rows, shape)
        solid = solid_ref[i + 1]
        share = jnp.where(valid > 0, 3.0 * solid * solid / weight, 0.0)
        load = {
            key: (order / 48.0) * value for key, (order, value) in element_modes(warm_low, warm_high).items()
        }
        for k in range(BASIS):
            high = yz_modes(basis_ref[k, i + 2])
            modes = element_modes(lows[k], high)
            energy = sum(load[key] * value for key, (_, value) in modes.items())
            total = lows[k][0] + high[0]
            scaled_s[k, i + 1] = share * ((1.0 - KMIN) * energy - (QZERO / 8.0) * total)
            lows[k] = high
        warm_low = warm_high
    for k in range(BASIS):
        for i in range(n):
            result = filtered(scaled_s[k, i], scaled_s[k, i + 1], scaled_s[k, i + 2])
            parts_ref[k, i] = result[NEAR : NEAR + own_rows]


def final_kernel(n, own_rows, moments_ref, basis_ref, parts_ref, dual_ref, sens_ref):
    total = jnp.sum(moments_ref[...], axis=0, keepdims=True)
    a0, a1, a2, a3, a4, b0, b1, b2 = (
        jnp.broadcast_to(total[:, k : k + 1], (1, 128)) for k in range(MOMENTS)
    )
    l10 = a1 / a0
    l20 = a2 / a0
    d1 = a2 - l10 * a1
    t21 = a3 - l20 * a1
    l21 = t21 / d1
    d2 = a4 - l20 * a2 - l21 * t21
    z1 = b1 - l10 * b0
    z2 = b2 - l20 * b0 - l21 * z1
    y2 = z2 / d2
    y1 = z1 / d1 - l21 * y2
    y0 = b0 / a0 - l10 * y1 - l20 * y2
    z = dual_ref.shape[-1]
    coefs = [jnp.concatenate([y] * (z // 128), axis=1) for y in (y0, y1, y2)]
    for i in range(n):
        dual = sum(coefs[k] * basis_ref[k, i + 1] for k in range(BASIS))
        dual_ref[i] = dual[NEAR : NEAR + own_rows]
        sens_ref[i] = sum(coefs[k] * parts_ref[k, i] for k in range(BASIS))


def shifted(arr, axis, step):
    count = lax.axis_size(axis)
    return lax.ppermute(arr, axis, [(i, i + step) for i in range(count) if 0 <= i + step < count])


def body(gx, gy, material_fraction, primal_warmth, empty_region_flags, dirichlet_flags):
    n, own_rows, z = material_fraction.shape
    layers, rows = gx * n, gy * own_rows
    free = (1 - dirichlet_flags).astype(jnp.float32)
    warmth = free * primal_warmth
    rhs = empty_region_flags.astype(jnp.float32) * warmth
    design = material_fraction

    from_low = shifted(
        jnp.concatenate(
            [design[:, -5:], free[:, -3:], rhs[:, -3:], warmth[:, -1:]], axis=1
        ),
        "gy", 1,
    )
    from_high = shifted(
        jnp.concatenate([design[:, :5], free[:, :4], rhs[:, :4], warmth[:, :2]], axis=1),
        "gy", -1,
    )

    def blank(count):
        return jnp.zeros((n, count, z), jnp.float32)

    design = jnp.concatenate([blank(3), from_low[:, :5], design, from_high[:, :5], blank(3)], axis=1)
    free = jnp.concatenate([blank(1), from_low[:, 5:8], free, from_high[:, 5:9]], axis=1)
    rhs = jnp.concatenate([blank(1), from_low[:, 8:11], rhs, from_high[:, 9:13]], axis=1)
    warmth = jnp.concatenate([blank(3), from_low[:, 11:12], warmth, from_high[:, 13:15], blank(2)], axis=1)

    def tiles(*pieces):
        return jnp.concatenate([p.reshape(-1, 8, z) for p in pieces], axis=0)

    lo = shifted(tiles(design, free[1:], rhs[1:], warmth[n - 1 :]), "gx", 1)
    hi = shifted(tiles(design, free, rhs, warmth[:2]), "gx", -1)
    below = shifted(design[n - 1 :], "gx", 2)
    above = shifted(design[:1], "gx", -2)

    near = own_rows + 2 * NEAR
    f32 = jnp.float32
    inner = min(16, gx)
    outer = gx * gy // inner
    sizes = (n, own_rows, layers, rows)
    moments, basis, solid = pl.pallas_call(
        functools.partial(basis_kernel, *sizes),
        out_shape=(
            jax.ShapeDtypeStruct((inner, 128), f32),
            jax.ShapeDtypeStruct((BASIS, n + 3, near, z), f32),
            jax.ShapeDtypeStruct((n + 2, near, z), f32),
        ),
        scratch_shapes=[
            pltpu.VMEM((3 * n, near, z), f32),
            pltpu.VMEM((3 * n - 1, near, z), f32),
            pltpu.VMEM((3 * n - 1, near, z), f32),
            pltpu.VMEM((3 * n - 1, near, z), f32),
            pltpu.VMEM((3 * n - 3, near, z), f32),
        ],
        name="basis",
    )(design, free, rhs, lo, hi, below, above)

    parts = pl.pallas_call(
        functools.partial(sensitivity_kernel, *sizes),
        out_shape=jax.ShapeDtypeStruct((BASIS, n, own_rows, z), f32),
        scratch_shapes=[pltpu.VMEM((BASIS, n + 2, near, z), f32)],
        name="sensitivity_parts",
        cost_estimate=pl.CostEstimate(flops=40000000, bytes_accessed=2000000, transcendentals=0),
    )(basis, solid, warmth, lo, hi)

    first = [[g * inner + j for j in range(inner)] for g in range(gx // inner)]
    first = [[d * gy + y for d in group] for group in first for y in range(gy)]
    second = [
        [(g * inner + j) * gy + y for g in range(gx // inner) for y in range(gy)]
        for j in range(inner)
    ]
    moments = lax.all_to_all(moments, ("gx", "gy"), 0, 0, axis_index_groups=first, tiled=True)
    moments = jnp.broadcast_to(jnp.sum(moments, axis=0, keepdims=True), (outer, 128))
    moments = lax.all_to_all(moments, ("gx", "gy"), 0, 0, axis_index_groups=second, tiled=True)

    return pl.pallas_call(
        functools.partial(final_kernel, n, own_rows),
        out_shape=(
            jax.ShapeDtypeStruct((n, own_rows, z), f32),
            jax.ShapeDtypeStruct((n, own_rows, z), f32),
        ),
        name="combine",
    )(moments, basis, parts)


def solution(mesh):
    placed = P("gx", "gy", None)
    return jax.shard_map(
        functools.partial(body, mesh.shape["gx"], mesh.shape["gy"]),
        mesh=mesh,
        in_specs=(placed,) * 4,
        out_specs=(placed, placed),
        check_vma=False,
    )
```

time: 608 us -> 78.7 us (0.13)
  blocking collectives: 501 us -> 12.3 us
  waiting for transfers between devices: 31.6 us -> 11.8 us
  starting transfers between devices: 50.7 us -> 36 us
  Pallas kernels: 0 us -> 9.23 us
  between operations: 7.91 us -> 1.01 us
  other arithmetic: 7.73 us -> 1.12 us
    psum x5 -> x0, blocking collectives: 501 us -> none  [the longest x3 301 us: precond_product(): return lax.psum(jnp.sum(residual * precond), ('gx', 'gy'))]
    ppermute x20 -> x6, starting transfers between devices: 50.7 us -> 19.7 us  [shifted(): lax.ppermute(arr, axis, [(i, i + step) for i in range(count) if 0 <= i +...]
    ppermute x20 -> x6, waiting for transfers between devices: 31.6 us -> 4.05 us  [shifted(): lax.ppermute(arr, axis, [(i, i + step) for i in range(count) if 0 <= i +...]
    all_to_all x0 -> x1, starting transfers between devices: none -> 16.3 us  [body(): lax.all_to_all(moments, ('gx', 'gy'), 0, 0, axis_index_groups=second, til...]
    all_to_all x0 -> x1, blocking collectives: none -> 12.3 us  [body(): lax.all_to_all(moments, ('gx', 'gy'), 0, 0, axis_index_groups=first, tile...]
    pallas_call x0 -> x3, Pallas kernels: none -> 9.23 us  [the longest x1 4.17 us: body(): pl.pallas_call(functools.partial(basis_kernel, *sizes), out_shape=(jax.Sh...]
    all_to_all x0 -> x1, waiting for transfers between devices: none -> 7.78 us  [body(): lax.all_to_all(moments, ('gx', 'gy'), 0, 0, axis_index_groups=second, til...]
  transfers between devices with their start and end apart: 20 -> 7, of which waited for: 10 -> 3; matrix products, arithmetic and copies ran while one was open for 0% -> 0% of each run, Pallas kernels for 0% -> 4%
where the time goes in v1:
time: 78.7 us; the launch traced here: 78.1 us
  starting transfers between devices  36 us (46%)
  blocking collectives  12.3 us (16%)
  waiting for transfers between devices  11.8 us (15%)
  Pallas kernels  9.23 us (12%)
  local copies, waits for them, and re-layouts  6.63 us (8%)
  other arithmetic  1.12 us (1%)
  between operations  1.01 us (1%)
    ppermute x6, starting transfers between devices, shifted(): lax.ppermute(arr, axis, [(i, i + step) for i in range(count) if 0 <= i +...  19.7 us
    all_to_all x1, starting transfers between devices, body(): lax.all_to_all(moments, ('gx', 'gy'), 0, 0, axis_index_groups=second, til...  16.3 us
    all_to_all x1, blocking collectives, body(): lax.all_to_all(moments, ('gx', 'gy'), 0, 0, axis_index_groups=first, tile...  12.3 us
    all_to_all x1, waiting for transfers between devices, body(): lax.all_to_all(moments, ('gx', 'gy'), 0, 0, axis_index_groups=second, til...  7.78 us
    pallas_call x1, Pallas kernels, body(): pl.pallas_call(functools.partial(basis_kernel, *sizes), out_shape=(jax.Sh...  4.17 us
    unnamed x28, local copies, waits for them, and re-layouts  4.15 us
    ppermute x6, waiting for transfers between devices, shifted(): lax.ppermute(arr, axis, [(i, i + step) for i in range(count) if 0 <= i +...  4.05 us
    pallas_call x1, Pallas kernels, body(): pl.pallas_call(functools.partial(sensitivity_kernel, *sizes), out_shape=j...  3.19 us
  transfers between devices with their start and end apart: 7, of which 3 were waited for; matrix products, arithmetic and copies ran while one was open for 0% of the time, Pallas kernels for 4%

profile of v1, /device:TPU:1, one launch (start us, length us, event | category | flops | bytes accessed | tf_op | source)
XLA Modules:
  0.0 78.1 jit_solution(9358613937127390503)
XLA Ops:
  0.6 0.0 copy-start.7
  0.6 0.0 copy-start.10
  0.6 0.9 %subtract_convert_fusion = f32[4,16,256]{2,1,0:T(8,128)S(1)} fusion(s32[4,16,256]{2,1,0:T(8,128)} %param.7), kind=kLoop, calls=%fused_computation.7 | loop fusion | flops 32768 | bytes 131072 | tf_op jit(solution)/shard_map/convert_element_type | solution.py:318
  1.5 0.0 copy-done.7
  1.6 0.0 copy-start.6
  1.6 0.0 copy-start.9
  1.6 0.0 copy-done.10
  1.6 0.8 %copy-done.6 = s32[4,16,256]{2,1,0:T(8,128)S(1)} copy-done((s32[4,16,256]{2,1,0:T(8,128)S(1)}, s32[4,16,256]{2,1,0:T(8,128)}, u32[]{:S(2)}) %copy-start.6) | copy-done | bytes 65560
  2.4 0.0 copy-done.9
  2.5 4.0 %collective-permute-start = (f32[4,12,256]{2,1,0:T(8,128)S(1)}, f32[4,12,256]{2,1,0:T(8,128)S(1)}, u32[]{:S(2)}, u32[]{:S(2)}) collective-permute-start(f32[4,12,256]{2,1,0:T(8,128)S(1)} %pad_maximum_fusion.4), channel_id=1, source_target_pairs={{0,1},{1,2},{2,3},{3,4},{4,5},{5,6},{6,7},{8,9},{9,10},{10,11},{11... | collective-permute-start | bytes 147464 | tf_op jit(solution)/shard_map/ppermute | solution.py:312
  6.6 1.3 %collective-permute-start.1 = (f32[4,15,256]{2,1,0:T(8,128)S(1)}, f32[4,15,256]{2,1,0:T(8,128)S(1)}, u32[]{:S(2)}, u32[]{:S(2)}) collective-permute-start(f32[4,15,256]{2,1,0:T(8,128)S(1)} %pad_maximum_fusion.5), channel_id=1, source_target_pairs={{1,0},{2,1},{3,2},{4,3},{5,4},{6,5},{7,6},{9,8},{10,9},{11,10},{12... | collective-permute-start | bytes 184328 | tf_op jit(solution)/shard_map/ppermute | solution.py:312
  7.9 0.0 collective-permute-done
  7.9 0.0 copy-start.8
  8.0 0.6 copy-done.8
  8.6 3.1 %collective-permute-done.1 = f32[4,15,256]{2,1,0:T(8,128)S(1)} collective-permute-done((f32[4,15,256]{2,1,0:T(8,128)S(1)}, f32[4,15,256]{2,1,0:T(8,128)S(1)}, u32[]{:S(2)}, u32[]{:S(2)}) %collective-permute-start.1) | collective-permute-done | bytes 61472 | tf_op jit(solution)/shard_map/ppermute | solution.py:312
  11.6 0.2 concatenate.29.warmth_ref
  11.9 0.0 copy-start.5
  11.9 0.6 copy-done.5
  12.5 0.1 pad_maximum_fusion.3
  12.6 0.0 copy-start.2
  12.6 0.0 copy-start.3
  12.7 0.0 slice-start.1
  12.7 0.8 slice-done.1
  13.5 0.0 slice-start
  13.5 0.0 copy-start
  13.5 0.0 copy-done.2
  13.5 0.0 copy-done.3
  13.5 0.7 slice-done
  14.3 7.2 %collective-permute-start.3 = (f32[46,8,256]{2,1,0:T(8,128)S(1)}, f32[46,8,256]{2,1,0:T(8,128)S(1)}, u32[]{:S(2)}, u32[]{:S(2)}) collective-permute-start(f32[46,8,256]{2,1,0:T(8,128)S(1)} %pad_maximum_fusion), channel_id=1, source_target_pairs={{8,0},{16,8},{24,16},{32,24},{40,32},{48,40},{56,48},{64,56},{72,6... | collective-permute-start | bytes 1130504 | tf_op jit(solution)/shard_map/ppermute | solution.py:312
  21.5 1.9 %collective-permute-start.2 = (f32[37,8,256]{2,1,0:T(8,128)S(1)}, f32[37,8,256]{2,1,0:T(8,128)S(1)}, u32[]{:S(2)}, u32[]{:S(2)}) collective-permute-start(f32[37,8,256]{2,1,0:T(8,128)S(1)} %pad_maximum_fusion.1), channel_id=1, source_target_pairs={{0,8},{8,16},{16,24},{24,32},{32,40},{40,48},{48,56},{56,64},{64,7... | collective-permute-start | bytes 909320 | tf_op jit(solution)/shard_map/ppermute | solution.py:312
  23.4 0.0 copy-done
  23.5 1.3 %collective-permute-start.5 = (f32[1,32,256]{2,1,0:T(8,128)S(1)}, f32[1,32,256]{2,1,0:T(8,128)S(1)}, u32[]{:S(2)}, u32[]{:S(2)}) collective-permute-start(f32[1,32,256]{2,1,0:T(8,128)S(1)} %get-tuple-element.10), channel_id=1, source_target_pairs={{16,0},{24,8},{32,16},{40,24},{48,32},{56,40},{64,48},{72,56},{80,... | collective-permute-start | bytes 98312 | tf_op jit(solution)/shard_map/ppermute | solution.py:312
  24.8 4.0 %collective-permute-start.4 = (f32[1,32,256]{2,1,0:T(8,128)S(1)}, f32[1,32,256]{2,1,0:T(8,128)S(1)}, u32[]{:S(2)}, u32[]{:S(2)}) collective-permute-start(f32[1,32,256]{2,1,0:T(8,128)S(1)} %get-tuple-element.11), channel_id=1, source_target_pairs={{0,16},{8,24},{16,32},{24,40},{32,48},{40,56},{48,64},{56,72},{64,... | collective-permute-start | bytes 98312 | tf_op jit(solution)/shard_map/ppermute | solution.py:312
  28.8 0.0 collective-permute-done.5.above_ref
  28.8 0.0 copy-start.12
  28.8 1.0 %collective-permute-done.4.below_ref = f32[1,32,256]{2,1,0:T(8,128)S(1)} collective-permute-done((f32[1,32,256]{2,1,0:T(8,128)S(1)}, f32[1,32,256]{2,1,0:T(8,128)S(1)}, u32[]{:S(2)}, u32[]{:S(2)}) %collective-permute-start.4) | collective-permute-done | bytes 32800 | tf_op jit(solution)/shard_map/ppermute | solution.py:312
  29.8 0.0 copy-start.13
  29.8 0.0 collective-permute-done.2.lo_ref
  29.8 0.0 copy-start.4
  29.8 0.0 collective-permute-done.3.hi_ref
  29.8 0.0 copy-done.12
  29.8 0.6 copy-done.13
  30.4 0.1 copy-done.4
  30.5 0.0 copy-start.1
  30.5 0.7 copy-done.1
  31.3 4.2 %basis.1 = (f32[16,128]{1,0:T(8,128)}, f32[3,7,24,256]{3,2,1,0:T(8,128)}, f32[6,24,256]{2,1,0:T(8,128)}) custom-call(f32[4,32,256]{2,1,0:T(8,128)} %copy-done, f32[4,24,256]{2,1,0:T(8,128)} %copy-done.3, f32[4,24,256]{2,1,0:T(8,128)} %copy-done.2, f32[37,8,256]{2,1,0:T(8,128)} %copy-done.4, f32[46,8,256]{2,1,0:T(8,128)} %copy-done.1, ...), custom_call_target="tpu_custom_call" | custom-call | tf_op jit(solution)/shard_map/basis/pallas_call | solution.py:355
  35.4 12.3 %all_to_all.17 = f32[16,1,128]{2,1,0:T(1,128)S(1)} all-to-all(f32[16,1,128]{2,1,0:T(1,128)} %bitcast.21), channel_id=1, replica_groups={{0,8,16,24,32,40,48,56,64,72,80,88,96,104,112,120},{1,9,17,25,33,41,49,..., dimensions={0} | all-to-all | bytes 16384 | tf_op jit(solution)/shard_map/all_to_all | solution.py:386
  47.7 0.6 broadcast_in_dim.10
  48.3 16.3 %all-to-all-start.1 = ((f32[32,1,128]{2,1,0:T(1,128)}), f32[32,1,128]{2,1,0:T(1,128)S(1)}, u32[]{:S(2)}, u32[]{:S(2)}) async-start(f32[32,1,128]{2,1,0:T(1,128)} %broadcast_in_dim.10), calls=%async_computation.1 | async-start | bytes 32768 | tf_op jit(solution)/shard_map/all_to_all | solution.py:388
  64.7 3.2 %sensitivity_parts.1.parts_ref = f32[3,4,16,256]{3,2,1,0:T(8,128)} custom-call(f32[3,7,24,256]{3,2,1,0:T(8,128)} %get-tuple-element.6.basis_ref, f32[6,24,256]{2,1,0:T(8,128)} %get-tuple-element.7.solid_ref, f32[4,24,256]{2,1,0:T(8,128)} %copy-done.5, f32[37,8,256]{2,1,0:T(8,128)} %copy-done.4, f32[46,8,256]{2,1,0:T(8,128)} %copy-done.1), custom_call_target="tpu_custom_call" | custom-call | flops 40000000 | bytes 2000000 | tf_op jit(solution)/shard_map/sensitivity_parts/pallas_call | solution.py:372
  67.8 7.8 %all-to-all-done.1 = f32[32,1,128]{2,1,0:T(1,128)S(1)} async-done(((f32[32,1,128]{2,1,0:T(1,128)}), f32[32,1,128]{2,1,0:T(1,128)S(1)}, u32[]{:S(2)}, u32[]{:S(2)}) %all-to-all-start.1) | async-done | bytes 16416 | tf_op jit(solution)/shard_map/all_to_all | solution.py:388
  75.6 0.0 copy-start.11
  75.6 0.6 copy-done.11
  76.2 1.9 %combine.1 = (f32[4,16,256]{2,1,0:T(8,128)}, f32[4,16,256]{2,1,0:T(8,128)}) custom-call(f32[32,128]{1,0:T(8,128)} %bitcast.20, f32[3,7,24,256]{3,2,1,0:T(8,128)} %get-tuple-element.6.basis_ref, f32[3,4,16,256]{3,2,1,0:T(8,128)} %sensitivity_parts.1.parts_ref), custom_call_target="tpu_custom_call" | custom-call | tf_op jit(solution)/shard_map/combine/pallas_call | solution.py:390
  (26 shorter events, 0.3 us)
Async XLA Ops:
  0.6 0.9 %copy-start.7 = (f32[4,16,256]{2,1,0:T(8,128)S(1)}, f32[4,16,256]{2,1,0:T(8,128)}, u32[]{:S(2)}) copy-start(f32[4,16,256]{2,1,0:T(8,128)} %param.4) | copy-start | bytes 196612
  0.6 1.0 %copy-start.10 = (f32[4,16,256]{2,1,0:T(8,128)S(1)}, f32[4,16,256]{2,1,0:T(8,128)}, u32[]{:S(2)}) copy-start(f32[4,16,256]{2,1,0:T(8,128)} %param.5) | copy-start | bytes 196612
  1.6 0.8 %copy-start.6 = (s32[4,16,256]{2,1,0:T(8,128)S(1)}, s32[4,16,256]{2,1,0:T(8,128)}, u32[]{:S(2)}) copy-start(s32[4,16,256]{2,1,0:T(8,128)} %param.7) | copy-start | bytes 196612
  1.6 0.9 %copy-start.9 = (s32[4,16,256]{2,1,0:T(8,128)S(1)}, s32[4,16,256]{2,1,0:T(8,128)}, u32[]{:S(2)}) copy-start(s32[4,16,256]{2,1,0:T(8,128)} %param.6) | copy-start | bytes 196612
  2.5 5.4 %collective-permute-start = (f32[4,12,256]{2,1,0:T(8,128)S(1)}, f32[4,12,256]{2,1,0:T(8,128)S(1)}, u32[]{:S(2)}, u32[]{:S(2)}) collective-permute-start(f32[4,12,256]{2,1,0:T(8,128)S(1)} %pad_maximum_fusion.4), channel_id=1, source_target_pairs={{0,1},{1,2},{2,3},{3,4},{4,5},{5,6},{6,7},{8,9},{9,10},{10,11},{11... | collective-permute-start | bytes 147464 | tf_op jit(solution)/shard_map/ppermute | solution.py:312
  6.6 5.0 %collective-permute-start.1 = (f32[4,15,256]{2,1,0:T(8,128)S(1)}, f32[4,15,256]{2,1,0:T(8,128)S(1)}, u32[]{:S(2)}, u32[]{:S(2)}) collective-permute-start(f32[4,15,256]{2,1,0:T(8,128)S(1)} %pad_maximum_fusion.5), channel_id=1, source_target_pairs={{1,0},{2,1},{3,2},{4,3},{5,4},{6,5},{7,6},{9,8},{10,9},{11,10},{12... | collective-permute-start | bytes 184328 | tf_op jit(solution)/shard_map/ppermute | solution.py:312
  7.9 0.6 copy-start.8
  11.9 0.6 copy-start.5
  12.6 0.9 %copy-start.2 = (f32[4,24,256]{2,1,0:T(8,128)}, f32[4,24,256]{2,1,0:T(8,128)S(1)}, u32[]{:S(2)}) copy-start(f32[4,24,256]{2,1,0:T(8,128)S(1)} %get-tuple-element.18.rhs_ref) | copy-start | bytes 294916
  12.6 0.9 %copy-start.3 = (f32[4,24,256]{2,1,0:T(8,128)}, f32[4,24,256]{2,1,0:T(8,128)S(1)}, u32[]{:S(2)}) copy-start(f32[4,24,256]{2,1,0:T(8,128)S(1)} %get-tuple-element.19.free_ref) | copy-start | bytes 294916
  12.7 0.8 %slice-start.1 = ((f32[4,12,256]{2,1,0:T(8,128)}), f32[4,5,256]{2,1,0:T(8,128)S(1)}, s32[]{:S(2)}) async-start(f32[4,12,256]{2,1,0:T(8,128)} %copy-done.8), calls=%async_computation.3 | async-start | bytes 65536 | tf_op jit(solution)/shard_map/slice | solution.py:337
  13.5 0.8 %slice-start = ((f32[4,24,256]{2,1,0:T(8,128)}), f32[2,24,256]{2,1,0:T(8,128)S(1)}, s32[]{:S(2)}) async-start(f32[4,24,256]{2,1,0:T(8,128)} %copy-done.5), calls=%async_computation.2 | async-start | bytes 98304 | tf_op jit(solution)/shard_map/slice | solution.py:346
  13.5 9.9 %copy-start = (f32[4,32,256]{2,1,0:T(8,128)}, f32[4,32,256]{2,1,0:T(8,128)S(1)}, u32[]{:S(2)}) copy-start(f32[4,32,256]{2,1,0:T(8,128)S(1)} %concatenate.26.design_ref) | copy-start | bytes 393220
  14.3 15.5 %collective-permute-start.3 = (f32[46,8,256]{2,1,0:T(8,128)S(1)}, f32[46,8,256]{2,1,0:T(8,128)S(1)}, u32[]{:S(2)}, u32[]{:S(2)}) collective-permute-start(f32[46,8,256]{2,1,0:T(8,128)S(1)} %pad_maximum_fusion), channel_id=1, source_target_pairs={{8,0},{16,8},{24,16},{32,24},{40,32},{48,40},{56,48},{64,56},{72,6... | collective-permute-start | bytes 1130504 | tf_op jit(solution)/shard_map/ppermute | solution.py:312
  21.5 8.3 %collective-permute-start.2 = (f32[37,8,256]{2,1,0:T(8,128)S(1)}, f32[37,8,256]{2,1,0:T(8,128)S(1)}, u32[]{:S(2)}, u32[]{:S(2)}) collective-permute-start(f32[37,8,256]{2,1,0:T(8,128)S(1)} %pad_maximum_fusion.1), channel_id=1, source_target_pairs={{0,8},{8,16},{16,24},{24,32},{32,40},{40,48},{48,56},{56,64},{64,7... | collective-permute-start | bytes 909320 | tf_op jit(solution)/shard_map/ppermute | solution.py:312
  23.5 5.3 %collective-permute-start.5 = (f32[1,32,256]{2,1,0:T(8,128)S(1)}, f32[1,32,256]{2,1,0:T(8,128)S(1)}, u32[]{:S(2)}, u32[]{:S(2)}) collective-permute-start(f32[1,32,256]{2,1,0:T(8,128)S(1)} %get-tuple-element.10), channel_id=1, source_target_pairs={{16,0},{24,8},{32,16},{40,24},{48,32},{56,40},{64,48},{72,56},{80,... | collective-permute-start | bytes 98312 | tf_op jit(solution)/shard_map/ppermute | solution.py:312
  24.8 5.0 %collective-permute-start.4 = (f32[1,32,256]{2,1,0:T(8,128)S(1)}, f32[1,32,256]{2,1,0:T(8,128)S(1)}, u32[]{:S(2)}, u32[]{:S(2)}) collective-permute-start(f32[1,32,256]{2,1,0:T(8,128)S(1)} %get-tuple-element.11), channel_id=1, source_target_pairs={{0,16},{8,24},{16,32},{24,40},{32,48},{40,56},{48,64},{56,72},{64,... | collective-permute-start | bytes 98312 | tf_op jit(solution)/shard_map/ppermute | solution.py:312
  28.8 1.0 %copy-start.12 = (f32[1,32,256]{2,1,0:T(8,128)}, f32[1,32,256]{2,1,0:T(8,128)S(1)}, u32[]{:S(2)}) copy-start(f32[1,32,256]{2,1,0:T(8,128)S(1)} %collective-permute-done.5.above_ref) | copy-start | bytes 98308
  29.8 0.6 copy-start.13
  29.8 0.7 copy-start.4
  30.5 0.8 copy-start.1
  48.3 27.3 %all-to-all-start.1 = ((f32[32,1,128]{2,1,0:T(1,128)}), f32[32,1,128]{2,1,0:T(1,128)S(1)}, u32[]{:S(2)}, u32[]{:S(2)}) async-start(f32[32,1,128]{2,1,0:T(1,128)} %broadcast_in_dim.10), calls=%async_computation.1 | async-start | bytes 32768 | tf_op jit(solution)/shard_map/all_to_all | solution.py:388
  75.6 0.6 copy-start.11

commit v2 on v1

v2 whole, which is shorter than its diff:
```python
import functools
import math

import jax
import jax.numpy as jnp
from jax import lax
from jax.experimental import pallas as pl
from jax.experimental.pallas import tpu as pltpu
from jax.sharding import PartitionSpec as P

KMIN = 0.05
QZERO = 1.0
EDGE = 0.5
DIAGONAL = 1.5 - math.sqrt(2.0)

WIDE = 8
NEAR = 4
BASIS = 3
MOMENTS = 8


def up(arr, axis):
    return pltpu.roll(arr, arr.shape[axis] - 1, axis)


def down(arr, axis):
    return pltpu.roll(arr, 1, axis)


def z_index(arr):
    return lax.broadcasted_iota(jnp.int32, arr.shape, 1)


def lift(arr):
    return jnp.where(z_index(arr) == arr.shape[1] - 1, 0.0, up(arr, 1))


def lower_z(arr):
    return jnp.where(z_index(arr) == 0, 0.0, down(arr, 1))


def filtered(below, here, above):
    beside = below + above
    rim = up(here, 0) + down(here, 0)
    corner = up(beside, 0) + down(beside, 0)
    flat = 1.5 * here + EDGE * (beside + rim) + DIAGONAL * corner
    slanted = EDGE * here + DIAGONAL * (beside + rim)
    return flat + lift(slanted) + lower_z(slanted)


def grid_flags(layer, layers, first_layer, first_row, rows, shape):
    def inside(at):
        return ((at >= 0) & (at < layers)).astype(jnp.float32)

    at = first_layer + layer
    row = first_row + lax.broadcasted_iota(jnp.int32, shape, 0)

    def row_inside(offset):
        return ((row + offset >= 0) & (row + offset < rows)).astype(jnp.float32)

    return inside(at), inside(at - 1) + inside(at + 1), row_inside(0), row_inside(-1) + row_inside(1)


def filter_weight(layer, layers, first_layer, first_row, rows, shape):
    here, beside, row_here, row_beside = grid_flags(
        layer, layers, first_layer, first_row, rows, shape
    )
    z = lax.broadcasted_iota(jnp.int32, shape, 1)
    z_beside = (z > 0).astype(jnp.float32) + (z < shape[1] - 1).astype(jnp.float32)
    flat = (1.5 + EDGE * beside) * row_here + (EDGE + DIAGONAL * beside) * row_beside
    slanted = (EDGE + DIAGONAL * beside) * row_here + DIAGONAL * row_beside
    valid = here * row_here
    return valid, jnp.where(valid > 0, flat + z_beside * slanted, 1.0)


def yz_modes(node):
    lifted = lift(node)
    plain, slope = node + lifted, lifted - node
    plain_up, slope_up = up(plain, 0), up(slope, 0)
    return plain + plain_up, slope + slope_up, plain_up - plain, slope_up - slope


def element_modes(low, high):
    return {
        "d0": (3.0, high[0] - low[0]),
        "s1": (3.0, high[1] + low[1]),
        "s2": (3.0, high[2] + low[2]),
        "d1": (2.0, high[1] - low[1]),
        "d2": (2.0, high[2] - low[2]),
        "s3": (2.0, high[3] + low[3]),
        "d3": (1.0, high[3] - low[3]),
    }


def apply_layers(node_at, conduct_at, first, count):
    low = yz_modes(node_at(first - 1))
    carried = None
    for element in range(first - 1, first + count):
        high = yz_modes(node_at(element + 1))
        scaled = conduct_at(element) * (1.0 / 48.0)
        flow = {key: (order * value) * scaled for key, (order, value) in element_modes(low, high).items()}
        zero_sum = flow["d0"]
        if carried is not None:
            planes = (
                carried[0] - zero_sum,
                carried[1] + (flow["s1"] - flow["d1"]),
                carried[2] + (flow["s2"] - flow["d2"]),
                carried[3] + (flow["s3"] - flow["d3"]),
            )
            smooth = (planes[0] - planes[2]) + down(planes[0] + planes[2], 0)
            slope = (planes[1] - planes[3]) + down(planes[1] + planes[3], 0)
            yield element, (smooth - slope) + lower_z(smooth + slope)
        carried = (
            zero_sum,
            flow["s1"] + flow["d1"],
            flow["s2"] + flow["d2"],
            flow["s3"] + flow["d3"],
        )
        low = high


def tile_sum(value):
    return functools.reduce(
        jnp.add,
        [
            value[r : r + 8, c : c + 128]
            for r in range(0, value.shape[0], 8)
            for c in range(0, value.shape[1], 128)
        ],
    )


def roll_rows(tile, step):
    return pltpu.roll(tile, step % tile.shape[0], 0)


def tiles_of(ref, layer):
    return [ref[layer, r : r + 8] for r in range(0, ref.shape[1], 8)]


def pack_kernel(
    n, material_ref, primal_ref, source_ref, fixed_ref,
    free_ref, rhs_ref, warmth_ref, y_up_ref, y_down_ref, x_up_ref, x_down_ref,
):
    row = lax.broadcasted_iota(jnp.int32, (8, material_ref.shape[-1]), 0)
    for i in range(n):
        free = (1 - fixed_ref[i]).astype(jnp.float32)
        warmth = free * primal_ref[i]
        free_ref[i] = free
        warmth_ref[i] = warmth
        rhs_ref[i] = source_ref[i].astype(jnp.float32) * warmth
        design, free, rhs, warmth = (
            tiles_of(ref, i) for ref in (material_ref, free_ref, rhs_ref, warmth_ref)
        )
        y_up_ref[i] = jnp.where(row >= 3, design[-1], roll_rows(free[-1], 3))
        y_up_ref[n + i] = jnp.where(row >= 5, rhs[-1], roll_rows(warmth[-1], 1))
        y_down_ref[i] = jnp.where(row < 5, design[0], roll_rows(warmth[0], 5))
        y_down_ref[n + i] = jnp.where(row < 4, rhs[0], roll_rows(free[0], 4))
        for ref in (x_up_ref, x_down_ref):
            for t, tile in enumerate(design):
                ref[len(design) * i + t] = tile
    per = material_ref.shape[1] // 8
    spot = per * n
    for ref in (free_ref, rhs_ref):
        for i in range(2, n):
            for tile in tiles_of(ref, i):
                x_up_ref[spot] = tile
                spot += 1
    spot = per * n
    for ref, count in ((free_ref, n - 1), (rhs_ref, n - 1), (warmth_ref, 1)):
        for i in range(count):
            for tile in tiles_of(ref, i):
                x_down_ref[spot] = tile
                spot += 1


def corner_kernel(n, low_ref, high_ref, up_ref, down_ref):
    half = up_ref.shape[0] // 2
    up_ref[:n] = low_ref[:n]
    up_ref[n:half] = low_ref[n + 2 :]
    up_ref[half : half + n] = high_ref[:n]
    up_ref[half + n :] = high_ref[n + 2 :]
    half = down_ref.shape[0] // 2
    down_ref[:n] = low_ref[:n]
    down_ref[n:half] = low_ref[n : 2 * n - 1]
    down_ref[half : half + n] = high_ref[:n]
    down_ref[half + n :] = high_ref[n : 2 * n - 1]


def brick(n, own_rows, own, y_low, y_high, x_low, x_high, corner_low, corner_high):
    design_ref, free_ref, rhs_ref, warmth_ref = own
    per = own_rows // 8

    def rows_of(ref, start):
        return ref[start : start + per].reshape(own_rows, ref.shape[-1])

    def own_part(which, i):
        if 0 <= i < n:
            return own[which][i]
        if i < 0:
            return rows_of(x_low, per * ((i + n) if which == 0 else n + (which - 1) * (n - 2) + i + n - 2))
        return rows_of(x_high, per * ((i - n) if which == 0 else n + (which - 1) * (n - 1) + i - n))

    def y_tile(first, high, i):
        if 0 <= i < n:
            return (y_high if high else y_low)[i if first else n + i]
        ref, at, count = (corner_low, i + n, n - 2) if i < 0 else (corner_high, i - n, n - 1)
        start = (n + count) if high else 0
        if first:
            return ref[start + at]
        return ref[start + n + (i + n - 2 if i < 0 else at)]

    def joined(low, middle, high):
        return jnp.concatenate([low, middle, high], axis=0)

    def near(value):
        return value[WIDE - NEAR : own_rows + WIDE + NEAR]

    def design_at(i):
        return joined(y_tile(True, False, i), own_part(0, i), y_tile(True, True, i))

    def free_at(i):
        return near(
            joined(roll_rows(y_tile(True, False, i), -3), own_part(1, i), roll_rows(y_tile(False, True, i), -4))
        )

    def rhs_at(i):
        return near(joined(y_tile(False, False, i), own_part(2, i), y_tile(False, True, i)))

    def warmth_at(i):
        return near(
            joined(roll_rows(y_tile(False, False, i), -1), own_part(3, i), roll_rows(y_tile(True, True, i), -5))
        )

    return design_at, free_at, rhs_at, warmth_at


def basis_kernel(
    n, own_rows, layers, rows,
    design_ref, free_ref, rhs_ref, y_low, y_high, x_low, x_high, corner_low, corner_high,
    moments_ref, basis_ref, solid_ref,
    conduct_s, free_s, diag_inverse_s, u0_s, u1_s,
):
    first_layer = lax.axis_index("gx") * n
    first_row = lax.axis_index("gy") * own_rows
    wide_rows = own_rows + 2 * WIDE
    near_rows = own_rows + 2 * NEAR
    z = design_ref.shape[-1]
    design_at, free_from, rhs_at, _ = brick(
        n, own_rows, (design_ref, free_ref, rhs_ref, None),
        y_low, y_high, x_low, x_high, corner_low, corner_high,
    )

    for i in range(1 - n, 2 * n - 1):
        valid, weight = filter_weight(i, layers, first_layer, first_row - WIDE, rows, (wide_rows, z))
        solid = 1.0 - filtered(design_at(i - 1), design_at(i), design_at(i + 1)) / weight
        solid = solid[WIDE - NEAR : wide_rows - WIDE + NEAR]
        valid = valid[WIDE - NEAR : wide_rows - WIDE + NEAR]
        conduct_s[i + n - 1] = jnp.where(valid > 0, KMIN + (1.0 - KMIN) * (solid * solid * solid), 0.0)
        if 0 <= i < n:
            solid_ref[i] = solid

    def conduct_at(i):
        return conduct_s[i + n - 1]

    def free_at(i):
        return free_s[i + n - 2]

    for i in range(2 - n, 2 * n - 1):
        pair = conduct_at(i) + conduct_at(i - 1)
        pair = pair + down(pair, 0)
        pair = pair + lower_z(pair)
        free = free_from(i)
        inverse = 1.0 / (free * (pair * (1.0 / 3.0)) + (1.0 - free))
        free_s[i + n - 2] = free
        diag_inverse_s[i + n - 2] = inverse
        u0_s[i + n - 2] = rhs_at(i) * inverse

    row = lax.broadcasted_iota(jnp.int32, (near_rows, z), 0)
    own = (row >= NEAR) & (row < NEAR + own_rows)
    sums = [jnp.zeros((8, 128), jnp.float32) for _ in range(MOMENTS)]

    def gather(which, product):
        sums[which] = sums[which] + tile_sum(jnp.where(own, product, 0.0))

    def step(previous, first, count):
        for i, image in apply_layers(lambda i: free_at(i) * previous(i), conduct_at, first, count):
            free, start = free_at(i), previous(i)
            image = free * image + (1.0 - free) * start
            yield i, start, image, image * diag_inverse_s[i + n - 2] - start

    for i, start, image, later in step(lambda i: u0_s[i + n - 2], 3 - n, 3 * n - 5):
        u1_s[i + n - 3] = later
        if 0 <= i <= n:
            basis_ref[0, i] = start
        if 0 <= i < n:
            rhs = rhs_at(i)
            gather(0, start * image)
            gather(1, later * image)
            gather(5, rhs * start)
            gather(6, rhs * later)
    for i, start, image, later in step(lambda i: u1_s[i + n - 3], 0, n + 1):
        basis_ref[1, i] = start
        basis_ref[2, i] = later
        if i < n:
            gather(2, start * image)
            gather(3, later * image)
            gather(7, rhs_at(i) * later)
    low = yz_modes(free_at(0) * basis_ref[2, 0])
    for i in range(n):
        high = yz_modes(free_at(i + 1) * basis_ref[2, i + 1])
        square = sum(order * value * value for order, value in element_modes(low, high).values())
        last = basis_ref[2, i]
        gather(4, square * (conduct_at(i) * (1.0 / 48.0)) + (1.0 - free_at(i)) * last * last)
        low = high

    lane = lax.broadcasted_iota(jnp.int32, (1, 128), 1)
    total = jnp.zeros((1, 128), jnp.float32)
    for k in range(MOMENTS):
        total = total + jnp.where(lane == k, jnp.sum(sums[k], axis=(0, 1), keepdims=True), 0.0)
    moments_ref[...] = jnp.broadcast_to(total, moments_ref.shape)


def integrand_kernel(
    n, own_rows, layers, rows,
    basis_ref, solid_ref, warmth_ref, y_low, y_high, x_low, x_high, corner_low, corner_high,
    scaled_ref, first_ref, last_ref,
):
    first_layer = lax.axis_index("gx") * n
    first_row = lax.axis_index("gy") * own_rows
    shape = solid_ref.shape[1:]
    *_, warmth_at = brick(
        n, own_rows, (None, None, None, warmth_ref),
        y_low, y_high, x_low, x_high, corner_low, corner_high,
    )
    warm_low = yz_modes(warmth_at(0))
    lows = [yz_modes(basis_ref[k, 0]) for k in range(BASIS)]
    for i in range(n):
        warm_high = yz_modes(warmth_at(i + 1))
        valid, weight = filter_weight(i, layers, first_layer, first_row - NEAR, rows, shape)
        solid = solid_ref[i]
        share = jnp.where(valid > 0, 3.0 * solid * solid / weight, 0.0)
        load = {
            key: (order / 48.0) * value for key, (order, value) in element_modes(warm_low, warm_high).items()
        }
        for k in range(BASIS):
            high = yz_modes(basis_ref[k, i + 1])
            modes = element_modes(lows[k], high)
            energy = sum(load[key] * value for key, (_, value) in modes.items())
            total = lows[k][0] + high[0]
            result = share * ((1.0 - KMIN) * energy - (QZERO / 8.0) * total)
            scaled_ref[k, i] = result
            if i == 0:
                first_ref[k] = result
            if i == n - 1:
                last_ref[k] = result
            lows[k] = high
        warm_low = warm_high


def filter_kernel(n, own_rows, scaled_ref, below_ref, above_ref, parts_ref):
    for k in range(BASIS):
        for i in range(n):
            below = scaled_ref[k, i - 1] if i > 0 else below_ref[k]
            above = scaled_ref[k, i + 1] if i < n - 1 else above_ref[k]
            parts_ref[k, i] = filtered(below, scaled_ref[k, i], above)[NEAR : NEAR + own_rows]


def final_kernel(n, own_rows, moments_ref, basis_ref, parts_ref, dual_ref, sens_ref):
    total = jnp.sum(moments_ref[...], axis=0, keepdims=True)
    a0, a1, a2, a3, a4, b0, b1, b2 = (
        jnp.broadcast_to(total[:, k : k + 1], (1, 128)) for k in range(MOMENTS)
    )
    l10 = a1 / a0
    l20 = a2 / a0
    d1 = a2 - l10 * a1
    t21 = a3 - l20 * a1
    l21 = t21 / d1
    d2 = a4 - l20 * a2 - l21 * t21
    z1 = b1 - l10 * b0
    z2 = b2 - l20 * b0 - l21 * z1
    y2 = z2 / d2
    y1 = z1 / d1 - l21 * y2
    y0 = b0 / a0 - l10 * y1 - l20 * y2
    z = dual_ref.shape[-1]
    coefs = [jnp.concatenate([y] * (z // 128), axis=1) for y in (y0, y1, y2)]
    for i in range(n):
        dual = sum(coefs[k] * basis_ref[k, i] for k in range(BASIS))
        dual_ref[i] = dual[NEAR : NEAR + own_rows]
        sens_ref[i] = sum(coefs[k] * parts_ref[k, i] for k in range(BASIS))


def shifted(arr, axis, step):
    count = lax.axis_size(axis)
    return lax.ppermute(arr, axis, [(i, i + step) for i in range(count) if 0 <= i + step < count])


def in_vmem(count):
    return [pl.BlockSpec(memory_space=pltpu.VMEM)] * count


def body(gx, gy, material_fraction, primal_warmth, empty_region_flags, dirichlet_flags):
    n, own_rows, z = material_fraction.shape
    sizes = (n, own_rows, gx * n, gy * own_rows)
    near = own_rows + 2 * NEAR
    per = own_rows // 8

    def arrays(*shapes):
        return [jax.ShapeDtypeStruct(shape, jnp.float32) for shape in shapes]

    def call(name, kernel, outs, *operands, scratch=(), resident=True, flops=0):
        return pl.pallas_call(
            kernel,
            out_shape=arrays(*outs),
            in_specs=in_vmem(len(operands)) if resident else None,
            out_specs=in_vmem(len(outs)) if resident else None,
            scratch_shapes=[pltpu.VMEM(shape, jnp.float32) for shape in scratch],
            cost_estimate=pl.CostEstimate(flops=flops, bytes_accessed=1 << 20, transcendentals=0),
            name=name,
        )(*operands)

    brick_shape = (n, own_rows, z)
    free, rhs, warmth, y_up, y_down, x_up, x_down = call(
        "pack",
        functools.partial(pack_kernel, n),
        [brick_shape] * 3
        + [(2 * n, 8, z)] * 2
        + [(per * (n + 2 * (n - 2)), 8, z), (per * (n + 2 * (n - 1) + 1), 8, z)],
        material_fraction, primal_warmth, empty_region_flags, dirichlet_flags,
    )
    y_low = shifted(y_up, "gy", 1)
    y_high = shifted(y_down, "gy", -1)
    x_low = shifted(x_up, "gx", 1)
    x_high = shifted(x_down, "gx", -1)
    corner_up, corner_down = call(
        "corners",
        functools.partial(corner_kernel, n),
        [(2 * (2 * n - 2), 8, z), (2 * (2 * n - 1), 8, z)],
        y_low, y_high,
    )
    corner_low = shifted(corner_up, "gx", 1)
    corner_high = shifted(corner_down, "gx", -1)
    halo = (y_low, y_high, x_low, x_high, corner_low, corner_high)

    pairs = 2 if gx % 2 == 0 else 1
    inner, outer = pairs * gy, gx // pairs
    moments, basis, solid = call(
        "basis",
        functools.partial(basis_kernel, *sizes),
        [(inner, 128), (BASIS, n + 1, near, z), (n, near, z)],
        material_fraction, free, rhs, *halo,
        scratch=[
            (3 * n - 2, near, z),
            (3 * n - 3, near, z),
            (3 * n - 3, near, z),
            (3 * n - 3, near, z),
            (3 * n - 5, near, z),
        ],
    )
    scaled, first, last = call(
        "integrand",
        functools.partial(integrand_kernel, *sizes),
        [(BASIS, n, near, z), (BASIS, near, z), (BASIS, near, z)],
        basis, solid, warmth, *halo,
        flops=40000000,
    )
    below = shifted(last, "gx", 1)
    above = shifted(first, "gx", -1)
    (parts,) = call(
        "filter",
        functools.partial(filter_kernel, n, own_rows),
        [(BASIS,) + brick_shape],
        scaled, below, above,
        flops=40000000,
    )

    near_groups = [
        [(g * pairs + c) * gy + y for c in range(pairs) for y in range(gy)] for g in range(outer)
    ]
    far_groups = [
        [(g * pairs + c) * gy + y for g in range(outer)] for c in range(pairs) for y in range(gy)
    ]
    moments = lax.all_to_all(moments, ("gx", "gy"), 0, 0, axis_index_groups=near_groups, tiled=True)
    moments = jnp.broadcast_to(jnp.sum(moments, axis=0, keepdims=True), (outer, 128))
    moments = lax.all_to_all(moments, ("gx", "gy"), 0, 0, axis_index_groups=far_groups, tiled=True)
    return tuple(
        call(
            "combine",
            functools.partial(final_kernel, n, own_rows),
            [brick_shape, brick_shape],
            moments, basis, parts,
        )
    )


def solution(mesh):
    placed = P("gx", "gy", None)
    return jax.shard_map(
        functools.partial(body, mesh.shape["gx"], mesh.shape["gy"]),
        mesh=mesh,
        in_specs=(placed,) * 4,
        out_specs=(placed, placed),
        check_vma=False,
    )
```

time: 78.7 us -> 87.6 us (1.11)
  starting transfers between devices: 36 us -> 46.5 us
  Pallas kernels: 9.23 us -> 13.8 us
  waiting for transfers between devices: 11.8 us -> 7.82 us
  local copies, waits for them, and re-layouts: 6.63 us -> 3.82 us
  blocking collectives: 12.3 us -> 14.2 us
  other arithmetic: 1.12 us -> 0.03 us
    all_to_all x1, starting transfers between devices: 16.3 us -> 21.6 us  [body(): lax.all_to_all(moments, ('gx', 'gy'), 0, 0, axis_index_groups=far_groups,...]
    ppermute x6 -> x8, starting transfers between devices: 19.7 us -> 24.9 us  [shifted(): lax.ppermute(arr, axis, [(i, i + step) for i in range(count) if 0 <= i +...]
    pallas_call x3 -> x6, Pallas kernels: 9.23 us -> 13.8 us  [call(): pl.pallas_call(kernel, out_shape=arrays(*outs), in_specs=in_vmem(len(oper...]
    ppermute x6 -> x8, waiting for transfers between devices: 4.05 us -> 1.93 us  [shifted(): lax.ppermute(arr, axis, [(i, i + step) for i in range(count) if 0 <= i +...]
    all_to_all x1, blocking collectives: 12.3 us -> 14.2 us  [body(): lax.all_to_all(moments, ('gx', 'gy'), 0, 0, axis_index_groups=near_groups...]
    all_to_all x1, waiting for transfers between devices: 7.78 us -> 5.89 us  [body(): lax.all_to_all(moments, ('gx', 'gy'), 0, 0, axis_index_groups=far_groups,...]
    slice x19 -> x0, local copies, waits for them, and re-layouts: 1.59 us -> none  [the longest x2 0.78 us: body(): from_low[:, :5]]
    unnamed x28 -> x20, local copies, waits for them, and re-layouts: 4.15 us -> 3.2 us
  transfers between devices with their start and end apart: 7 -> 9, of which waited for: 3 -> 2; matrix products, arithmetic and copies ran while one was open for 0% -> 1% of each run, Pallas kernels for 4% -> 4%
where the time goes in v2:
time: 87.6 us; the launch traced here: 87 us
  starting transfers between devices  46.5 us (53%)
  blocking collectives  14.2 us (16%)
  Pallas kernels  13.8 us (16%)
  waiting for transfers between devices  7.82 us (9%)
  local copies, waits for them, and re-layouts  3.82 us (4%)
    ppermute x8, starting transfers between devices, shifted(): lax.ppermute(arr, axis, [(i, i + step) for i in range(count) if 0 <= i +...  24.9 us
    all_to_all x1, starting transfers between devices, body(): lax.all_to_all(moments, ('gx', 'gy'), 0, 0, axis_index_groups=far_groups,...  21.6 us
    all_to_all x1, blocking collectives, body(): lax.all_to_all(moments, ('gx', 'gy'), 0, 0, axis_index_groups=near_groups...  14.2 us
    pallas_call x6, Pallas kernels, call(): pl.pallas_call(kernel, out_shape=arrays(*outs), in_specs=in_vmem(len(oper...  13.8 us
    all_to_all x1, waiting for transfers between devices, body(): lax.all_to_all(moments, ('gx', 'gy'), 0, 0, axis_index_groups=far_groups,...  5.89 us
    unnamed x20, local copies, waits for them, and re-layouts  3.2 us
    ppermute x8, waiting for transfers between devices, shifted(): lax.ppermute(arr, axis, [(i, i + step) for i in range(count) if 0 <= i +...  1.93 us
  transfers between devices with their start and end apart: 9, of which 2 were waited for; matrix products, arithmetic and copies ran while one was open for 1% of the time, Pallas kernels for 4%

profile of v2, /device:TPU:1, one launch (start us, length us, event | category | flops | bytes accessed | tf_op | source)
XLA Modules:
  0.0 87.0 jit_solution(12357224229314376902)
XLA Ops:
  0.6 1.8 %pack.1 = (f32[4,16,256]{2,1,0:T(8,128)}, f32[4,16,256]{2,1,0:T(8,128)}, f32[4,16,256]{2,1,0:T(8,128)}, f32[8,8,256]{2,1,0:T(8,128)}, f32[8,8,256]{2,1,0:T(8,128...) custom-call(f32[4,16,256]{2,1,0:T(8,128)} %design_ref.1, f32[4,16,256]{2,1,0:T(8,128)} %primal_ref.1, ...), custom_call_target="tpu_custom_call" | custom-call | bytes 1048576 | tf_op jit(solution)/shard_map/pack/pallas_call | solution.py:412
  2.4 4.0 %collective-permute-start = (f32[8,8,256]{2,1,0:T(8,128)}, f32[8,8,256]{2,1,0:T(8,128)S(1)}, u32[]{:S(2)}, u32[]{:S(2)}) collective-permute-start(f32[8,8,256]{2,1,0:T(8,128)} %get-tuple-element.19), channel_id=1, source_target_pairs={{0,1},{1,2},{2,3},{3,4},{4,5},{5,6},{6,7},{8,9},{9,10},{10,11},{11... | collective-permute-start | bytes 196616 | tf_op jit(solution)/shard_map/ppermute | solution.py:395
  6.4 1.3 %collective-permute-start.1 = (f32[8,8,256]{2,1,0:T(8,128)}, f32[8,8,256]{2,1,0:T(8,128)S(1)}, u32[]{:S(2)}, u32[]{:S(2)}) collective-permute-start(f32[8,8,256]{2,1,0:T(8,128)} %get-tuple-element.20), channel_id=1, source_target_pairs={{1,0},{2,1},{3,2},{4,3},{5,4},{6,5},{7,6},{9,8},{10,9},{11,10},{12... | collective-permute-start | bytes 196616 | tf_op jit(solution)/shard_map/ppermute | solution.py:395
  7.7 6.0 %collective-permute-start.3 = (f32[22,8,256]{2,1,0:T(8,128)}, f32[22,8,256]{2,1,0:T(8,128)S(1)}, u32[]{:S(2)}, u32[]{:S(2)}) collective-permute-start(f32[22,8,256]{2,1,0:T(8,128)} %get-tuple-element.22), channel_id=1, source_target_pairs={{8,0},{16,8},{24,16},{32,24},{40,32},{48,40},{56,48},{64,56},{72,6... | collective-permute-start | bytes 540680 | tf_op jit(solution)/shard_map/ppermute | solution.py:395
  13.8 1.9 %collective-permute-start.2 = (f32[16,8,256]{2,1,0:T(8,128)}, f32[16,8,256]{2,1,0:T(8,128)S(1)}, u32[]{:S(2)}, u32[]{:S(2)}) collective-permute-start(f32[16,8,256]{2,1,0:T(8,128)} %get-tuple-element.21), channel_id=1, source_target_pairs={{0,8},{8,16},{16,24},{24,32},{32,40},{40,48},{48,56},{56,64},{64,7... | collective-permute-start | bytes 393224 | tf_op jit(solution)/shard_map/ppermute | solution.py:395
  15.7 0.0 collective-permute-done.low_ref.y_low
  15.7 0.0 copy-start.1
  15.7 0.0 collective-permute-done.1.high_ref.y_high
  15.7 0.6 copy-done.1
  16.4 0.0 copy-start.2
  16.4 0.6 copy-done.2
  17.0 1.6 %corners.1 = (f32[12,8,256]{2,1,0:T(8,128)}, f32[14,8,256]{2,1,0:T(8,128)}) custom-call(f32[8,8,256]{2,1,0:T(8,128)} %copy-done.1, f32[8,8,256]{2,1,0:T(8,128)} %copy-done.2), custom_call_target="tpu_custom_call" | custom-call | bytes 1048576 | tf_op jit(solution)/shard_map/corners/pallas_call | solution.py:412
  18.6 2.5 %collective-permute-start.5 = (f32[14,8,256]{2,1,0:T(8,128)}, f32[14,8,256]{2,1,0:T(8,128)S(1)}, u32[]{:S(2)}, u32[]{:S(2)}) collective-permute-start(f32[14,8,256]{2,1,0:T(8,128)} %get-tuple-element.24), channel_id=1, source_target_pairs={{8,0},{16,8},{24,16},{32,24},{40,32},{48,40},{56,48},{64,56},{72,6... | collective-permute-start | bytes 344072 | tf_op jit(solution)/shard_map/ppermute | solution.py:395
  21.0 3.1 %collective-permute-start.4 = (f32[12,8,256]{2,1,0:T(8,128)}, f32[12,8,256]{2,1,0:T(8,128)S(1)}, u32[]{:S(2)}, u32[]{:S(2)}) collective-permute-start(f32[12,8,256]{2,1,0:T(8,128)} %get-tuple-element.23), channel_id=1, source_target_pairs={{0,8},{8,16},{16,24},{24,32},{32,40},{40,48},{48,56},{56,64},{64,7... | collective-permute-start | bytes 294920 | tf_op jit(solution)/shard_map/ppermute | solution.py:395
  24.1 0.0 collective-permute-done.2.x_low
  24.1 0.0 copy-start.3
  24.1 1.9 %collective-permute-done.4.corner_low = f32[12,8,256]{2,1,0:T(8,128)S(1)} collective-permute-done((f32[12,8,256]{2,1,0:T(8,128)}, f32[12,8,256]{2,1,0:T(8,128)S(1)}, u32[]{:S(2)}, u32[]{:S(2)}) %collective-permute-start.4) | collective-permute-done | bytes 98336 | tf_op jit(solution)/shard_map/ppermute | solution.py:395
  26.1 0.0 copy-start.5
  26.1 0.0 collective-permute-done.3.x_high
  26.1 0.0 copy-start
  26.1 0.0 collective-permute-done.5.corner_high
  26.1 0.0 copy-start.4
  26.1 0.0 copy-done.3
  26.1 0.6 copy-done.5
  26.7 0.1 copy-done
  26.8 0.0 copy-done.4
  26.8 3.7 %basis.1 = (f32[16,128]{1,0:T(8,128)}, f32[3,5,24,256]{3,2,1,0:T(8,128)}, f32[4,24,256]{2,1,0:T(8,128)}) custom-call(f32[4,16,256]{2,1,0:T(8,128)} %design_ref.1, f32[4,16,256]{2,1,0:T(8,128)} %get-tuple-element.17.free_ref, f32[4,16,256]{2,1,0:T(8,128)} %get-tuple-element.18.rhs_ref, f32[8,8,256]{2,1,0:T(8,128)} %copy-done.1, f32[8,8,256]{2,1,0:T(8,128)} %copy-done.2, ...), custom_call_target="tpu_custom_call" | custom-call | bytes 1048576 | tf_op jit(solution)/shard_map/basis/pallas_call | solution.py:412
  30.5 0.0 copy-start.9
  30.5 3.0 %integrand.1 = (f32[3,4,24,256]{3,2,1,0:T(8,128)}, f32[3,24,256]{2,1,0:T(8,128)}, f32[3,24,256]{2,1,0:T(8,128)}) custom-call(f32[3,5,24,256]{3,2,1,0:T(8,128)} %get-tuple-element.26.basis_ref, f32[4,24,256]{2,1,0:T(8,128)} %get-tuple-element.27.solid_ref, f32[4,16,256]{2,1,0:T(8,128)} %get-tuple-element.28.warmth_ref, f32[8,8,256]{2,1,0:T(8,128)} %copy-done.1, ...), custom_call_target="tpu_custom_call" | custom-call | flops 40000000 | bytes 1048576 | tf_op jit(solution)/shard_map/integrand/pallas_call | solution.py:412
  33.5 4.2 %collective-permute-start.6 = (f32[3,24,256]{2,1,0:T(8,128)}, f32[3,24,256]{2,1,0:T(8,128)S(1)}, u32[]{:S(2)}, u32[]{:S(2)}) collective-permute-start(f32[3,24,256]{2,1,0:T(8,128)} %get-tuple-element.30), channel_id=1, source_target_pairs={{0,8},{8,16},{16,24},{24,32},{32,40},{40,48},{48,56},{56,64},{64,7... | collective-permute-start | bytes 221192 | tf_op jit(solution)/shard_map/ppermute | solution.py:395
  37.7 1.9 %collective-permute-start.7 = (f32[3,24,256]{2,1,0:T(8,128)}, f32[3,24,256]{2,1,0:T(8,128)S(1)}, u32[]{:S(2)}, u32[]{:S(2)}) collective-permute-start(f32[3,24,256]{2,1,0:T(8,128)} %get-tuple-element.31), channel_id=1, source_target_pairs={{8,0},{16,8},{24,16},{32,24},{40,32},{48,40},{56,48},{64,56},{72,6... | collective-permute-start | bytes 221192 | tf_op jit(solution)/shard_map/ppermute | solution.py:395
  39.6 0.0 copy-done.9
  39.6 14.2 %all_to_all.17 = f32[16,1,128]{2,1,0:T(1,128)S(1)} all-to-all(f32[16,1,128]{2,1,0:T(1,128)S(1)} %bitcast.5), channel_id=1, replica_groups={{0,1,2,3,4,5,6,7,8,9,10,11,12,13,14,15},{16,17,18,19,20,21,22,23,24,25,..., dimensions={0} | all-to-all | bytes 16384 | tf_op jit(solution)/shard_map/all_to_all | solution.py:483
  53.9 0.6 broadcast_in_dim.2
  54.5 21.6 %all-to-all-start.1 = ((f32[32,1,128]{2,1,0:T(1,128)}), f32[32,1,128]{2,1,0:T(1,128)S(1)}, u32[]{:S(2)}, u32[]{:S(2)}) async-start(f32[32,1,128]{2,1,0:T(1,128)} %broadcast_in_dim.2), calls=%async_computation.1 | async-start | bytes 32768 | tf_op jit(solution)/shard_map/all_to_all | solution.py:485
  76.1 0.0 collective-permute-done.6.below_ref
  76.1 0.0 copy-start.6
  76.1 0.0 collective-permute-done.7.above_ref
  76.1 0.0 copy-start.7
  76.1 0.6 copy-done.6
  76.7 0.0 copy-done.7
  76.7 1.9 %filter.1.parts_ref = f32[3,4,16,256]{3,2,1,0:T(8,128)} custom-call(f32[3,4,24,256]{3,2,1,0:T(8,128)} %get-tuple-element.29.scaled_ref, f32[3,24,256]{2,1,0:T(8,128)} %copy-done.6, f32[3,24,256]{2,1,0:T(8,128)} %copy-done.7), custom_call_target="tpu_custom_call" | custom-call | flops 40000000 | bytes 1048576 | tf_op jit(solution)/shard_map/filter/pallas_call | solution.py:412
  78.7 5.9 %all-to-all-done.1 = f32[32,1,128]{2,1,0:T(1,128)S(1)} async-done(((f32[32,1,128]{2,1,0:T(1,128)}), f32[32,1,128]{2,1,0:T(1,128)S(1)}, u32[]{:S(2)}, u32[]{:S(2)}) %all-to-all-start.1) | async-done | bytes 16416 | tf_op jit(solution)/shard_map/all_to_all | solution.py:485
  84.6 0.0 copy-start.8
  84.6 0.6 copy-done.8
  85.2 1.8 %combine.1 = (f32[4,16,256]{2,1,0:T(8,128)}, f32[4,16,256]{2,1,0:T(8,128)}) custom-call(f32[32,128]{1,0:T(8,128)} %bitcast.4, f32[3,5,24,256]{3,2,1,0:T(8,128)} %get-tuple-element.26.basis_ref, f32[3,4,16,256]{3,2,1,0:T(8,128)} %filter.1.parts_ref), custom_call_target="tpu_custom_call" | custom-call | bytes 1048576 | tf_op jit(solution)/shard_map/combine/pallas_call | solution.py:412
  (1 shorter events, 0.0 us)
Async XLA Ops:
  2.4 13.3 %collective-permute-start = (f32[8,8,256]{2,1,0:T(8,128)}, f32[8,8,256]{2,1,0:T(8,128)S(1)}, u32[]{:S(2)}, u32[]{:S(2)}) collective-permute-start(f32[8,8,256]{2,1,0:T(8,128)} %get-tuple-element.19), channel_id=1, source_target_pairs={{0,1},{1,2},{2,3},{3,4},{4,5},{5,6},{6,7},{8,9},{9,10},{10,11},{11... | collective-permute-start | bytes 196616 | tf_op jit(solution)/shard_map/ppermute | solution.py:395
  6.4 9.3 %collective-permute-start.1 = (f32[8,8,256]{2,1,0:T(8,128)}, f32[8,8,256]{2,1,0:T(8,128)S(1)}, u32[]{:S(2)}, u32[]{:S(2)}) collective-permute-start(f32[8,8,256]{2,1,0:T(8,128)} %get-tuple-element.20), channel_id=1, source_target_pairs={{1,0},{2,1},{3,2},{4,3},{5,4},{6,5},{7,6},{9,8},{10,9},{11,10},{12... | collective-permute-start | bytes 196616 | tf_op jit(solution)/shard_map/ppermute | solution.py:395
  7.7 18.3 %collective-permute-start.3 = (f32[22,8,256]{2,1,0:T(8,128)}, f32[22,8,256]{2,1,0:T(8,128)S(1)}, u32[]{:S(2)}, u32[]{:S(2)}) collective-permute-start(f32[22,8,256]{2,1,0:T(8,128)} %get-tuple-element.22), channel_id=1, source_target_pairs={{8,0},{16,8},{24,16},{32,24},{40,32},{48,40},{56,48},{64,56},{72,6... | collective-permute-start | bytes 540680 | tf_op jit(solution)/shard_map/ppermute | solution.py:395
  13.8 10.3 %collective-permute-start.2 = (f32[16,8,256]{2,1,0:T(8,128)}, f32[16,8,256]{2,1,0:T(8,128)S(1)}, u32[]{:S(2)}, u32[]{:S(2)}) collective-permute-start(f32[16,8,256]{2,1,0:T(8,128)} %get-tuple-element.21), channel_id=1, source_target_pairs={{0,8},{8,16},{16,24},{24,32},{32,40},{40,48},{48,56},{56,64},{64,7... | collective-permute-start | bytes 393224 | tf_op jit(solution)/shard_map/ppermute | solution.py:395
  15.7 0.6 copy-start.1
  16.4 0.6 copy-start.2
  18.6 7.5 %collective-permute-start.5 = (f32[14,8,256]{2,1,0:T(8,128)}, f32[14,8,256]{2,1,0:T(8,128)S(1)}, u32[]{:S(2)}, u32[]{:S(2)}) collective-permute-start(f32[14,8,256]{2,1,0:T(8,128)} %get-tuple-element.24), channel_id=1, source_target_pairs={{8,0},{16,8},{24,16},{32,24},{40,32},{48,40},{56,48},{64,56},{72,6... | collective-permute-start | bytes 344072 | tf_op jit(solution)/shard_map/ppermute | solution.py:395
  21.0 5.0 %collective-permute-start.4 = (f32[12,8,256]{2,1,0:T(8,128)}, f32[12,8,256]{2,1,0:T(8,128)S(1)}, u32[]{:S(2)}, u32[]{:S(2)}) collective-permute-start(f32[12,8,256]{2,1,0:T(8,128)} %get-tuple-element.23), channel_id=1, source_target_pairs={{0,8},{8,16},{16,24},{24,32},{32,40},{40,48},{48,56},{56,64},{64,7... | collective-permute-start | bytes 294920 | tf_op jit(solution)/shard_map/ppermute | solution.py:395
  24.1 1.9 %copy-start.3 = (f32[16,8,256]{2,1,0:T(8,128)}, f32[16,8,256]{2,1,0:T(8,128)S(1)}, u32[]{:S(2)}) copy-start(f32[16,8,256]{2,1,0:T(8,128)S(1)} %collective-permute-done.2.x_low) | copy-start | bytes 393220
  26.1 0.6 copy-start.5
  26.1 0.7 copy-start
  26.1 0.7 copy-start.4
  30.5 9.1 %copy-start.9 = (f32[16,128]{1,0:T(8,128)S(1)}, f32[16,128]{1,0:T(8,128)}, u32[]{:S(2)}) copy-start(f32[16,128]{1,0:T(8,128)} %get-tuple-element.25) | copy-start | bytes 24580
  33.5 42.6 %collective-permute-start.6 = (f32[3,24,256]{2,1,0:T(8,128)}, f32[3,24,256]{2,1,0:T(8,128)S(1)}, u32[]{:S(2)}, u32[]{:S(2)}) collective-permute-start(f32[3,24,256]{2,1,0:T(8,128)} %get-tuple-element.30), channel_id=1, source_target_pairs={{0,8},{8,16},{16,24},{24,32},{32,40},{40,48},{48,56},{56,64},{64,7... | collective-permute-start | bytes 221192 | tf_op jit(solution)/shard_map/ppermute | solution.py:395
  37.7 38.4 %collective-permute-start.7 = (f32[3,24,256]{2,1,0:T(8,128)}, f32[3,24,256]{2,1,0:T(8,128)S(1)}, u32[]{:S(2)}, u32[]{:S(2)}) collective-permute-start(f32[3,24,256]{2,1,0:T(8,128)} %get-tuple-element.31), channel_id=1, source_target_pairs={{8,0},{16,8},{24,16},{32,24},{40,32},{48,40},{56,48},{64,56},{72,6... | collective-permute-start | bytes 221192 | tf_op jit(solution)/shard_map/ppermute | solution.py:395
  54.5 30.1 %all-to-all-start.1 = ((f32[32,1,128]{2,1,0:T(1,128)}), f32[32,1,128]{2,1,0:T(1,128)S(1)}, u32[]{:S(2)}, u32[]{:S(2)}) async-start(f32[32,1,128]{2,1,0:T(1,128)} %broadcast_in_dim.2), calls=%async_computation.1 | async-start | bytes 32768 | tf_op jit(solution)/shard_map/all_to_all | solution.py:485
  76.1 0.6 copy-start.6
  76.1 0.6 copy-start.7
  84.6 0.6 copy-start.8

commit v3 on v2

--- a/solution.py
+++ b/solution.py
@@ -17,6 +17,7 @@
 NEAR = 4
 BASIS = 3
 MOMENTS = 8
+VMEM_LIMIT = 12 << 20
 
 
 def up(arr, axis):
@@ -415,6 +416,7 @@
             in_specs=in_vmem(len(operands)) if resident else None,
             out_specs=in_vmem(len(outs)) if resident else None,
             scratch_shapes=[pltpu.VMEM(shape, jnp.float32) for shape in scratch],
+            compiler_params=pltpu.CompilerParams(vmem_limit_bytes=VMEM_LIMIT),
             cost_estimate=pl.CostEstimate(flops=flops, bytes_accessed=1 << 20, transcendentals=0),
             name=name,
         )(*operands)
@@ -464,6 +466,16 @@
         basis, solid, warmth, *halo,
         flops=40000000,
     )
+    near_groups = [
+        [(g * pairs + c) * gy + y for c in range(pairs) for y in range(gy)] for g in range(outer)
+    ]
+    far_groups = [
+        [(g * pairs + c) * gy + y for g in range(outer)] for c in range(pairs) for y in range(gy)
+    ]
+    moments = lax.all_to_all(moments, ("gx", "gy"), 0, 0, axis_index_groups=near_groups, tiled=True)
+    near_total = jnp.sum(moments, axis=0, keepdims=True)
+    near_total, first, last = lax.optimization_barrier((near_total, first, last))
+    moments = jnp.broadcast_to(near_total, (outer, 128))
     below = shifted(last, "gx", 1)
     above = shifted(first, "gx", -1)
     (parts,) = call(
@@ -471,17 +483,8 @@
         functools.partial(filter_kernel, n, own_rows),
         [(BASIS,) + brick_shape],
         scaled, below, above,
-        flops=40000000,
-    )
-
-    near_groups = [
-        [(g * pairs + c) * gy + y for c in range(pairs) for y in range(gy)] for g in range(outer)
-    ]
-    far_groups = [
-        [(g * pairs + c) * gy + y for g in range(outer)] for c in range(pairs) for y in range(gy)
-    ]
-    moments = lax.all_to_all(moments, ("gx", "gy"), 0, 0, axis_index_groups=near_groups, tiled=True)
-    moments = jnp.broadcast_to(jnp.sum(moments, axis=0, keepdims=True), (outer, 128))
+        flops=1000000,
+    )
     moments = lax.all_to_all(moments, ("gx", "gy"), 0, 0, axis_index_groups=far_groups, tiled=True)
     return tuple(
         call(

time: 87.6 us -> 79.5 us (0.908)
  the two profiles are of different devices: /device:TPU:1 before, /device:TPU:2 now
where the time goes in v3:
time: 79.5 us; the launch traced here: 78.9 us
  starting transfers between devices  50.4 us (63%)
  waiting for transfers between devices  19.3 us (24%)
  Pallas kernels  4.51 us (6%)
  local copies, waits for them, and re-layouts  3.96 us (5%)
    all_to_all x1, starting transfers between devices, body(): lax.all_to_all(moments, ('gx', 'gy'), 0, 0, axis_index_groups=far_groups,...  21.6 us
    ppermute x8, starting transfers between devices, shifted(): lax.ppermute(arr, axis, [(i, i + step) for i in range(count) if 0 <= i +...  21.3 us
    all_to_all x1, waiting for transfers between devices, body(): lax.all_to_all(moments, ('gx', 'gy'), 0, 0, axis_index_groups=far_groups,...  8.15 us
    all_to_all x1, starting transfers between devices, body(): lax.all_to_all(moments, ('gx', 'gy'), 0, 0, axis_index_groups=near_groups...  7.4 us
    all_to_all x1, waiting for transfers between devices, body(): lax.all_to_all(moments, ('gx', 'gy'), 0, 0, axis_index_groups=near_groups...  6.61 us
    ppermute x8, waiting for transfers between devices, shifted(): lax.ppermute(arr, axis, [(i, i + step) for i in range(count) if 0 <= i +...  4.52 us
    pallas_call x6, Pallas kernels, call(): pl.pallas_call(kernel, out_shape=arrays(*outs), in_specs=in_vmem(len(oper...  4.51 us
    unnamed x8, local copies, waits for them, and re-layouts  3.35 us
  transfers between devices with their start and end apart: 10, of which 4 were waited for; matrix products, arithmetic and copies ran while one was open for 1% of the time, Pallas kernels for 1%

profile of v3, /device:TPU:2, one launch (start us, length us, event | category | flops | bytes accessed | tf_op | source)
XLA Modules:
  0.0 78.9 jit_solution(5405764565839688772)
XLA Ops:
  0.6 0.0 copy-start
  0.6 0.8 %copy-done = f32[4,16,256]{2,1,0:T(8,128)S(1)} copy-done((f32[4,16,256]{2,1,0:T(8,128)S(1)}, f32[4,16,256]{2,1,0:T(8,128)}, u32[]{:S(2)}) %copy-start) | copy-done | bytes 65560
  1.5 0.0 copy-start.1
  1.5 0.8 %copy-done.1 = f32[4,16,256]{2,1,0:T(8,128)S(1)} copy-done((f32[4,16,256]{2,1,0:T(8,128)S(1)}, f32[4,16,256]{2,1,0:T(8,128)}, u32[]{:S(2)}) %copy-start.1) | copy-done | bytes 65560
  2.3 0.0 copy-start.2
  2.3 0.8 %copy-done.2 = s32[4,16,256]{2,1,0:T(8,128)S(1)} copy-done((s32[4,16,256]{2,1,0:T(8,128)S(1)}, s32[4,16,256]{2,1,0:T(8,128)}, u32[]{:S(2)}) %copy-start.2) | copy-done | bytes 65560
  3.2 0.0 copy-start.3
  3.2 0.8 %copy-done.3 = s32[4,16,256]{2,1,0:T(8,128)S(1)} copy-done((s32[4,16,256]{2,1,0:T(8,128)S(1)}, s32[4,16,256]{2,1,0:T(8,128)}, u32[]{:S(2)}) %copy-start.3) | copy-done | bytes 65560
  4.0 3.5 %collective-permute-start = (f32[8,8,256]{2,1,0:T(8,128)S(1)}, f32[8,8,256]{2,1,0:T(8,128)S(1)}, u32[]{:S(2)}, u32[]{:S(2)}) collective-permute-start(f32[8,8,256]{2,1,0:T(8,128)S(1)} %get-tuple-element.22), channel_id=1, source_target_pairs={{0,1},{1,2},{2,3},{3,4},{4,5},{5,6},{6,7},{8,9},{9,10},{10,11},{11... | collective-permute-start | bytes 196616 | tf_op jit(solution)/shard_map/ppermute | solution.py:396
  7.5 1.3 %collective-permute-start.1 = (f32[8,8,256]{2,1,0:T(8,128)S(1)}, f32[8,8,256]{2,1,0:T(8,128)S(1)}, u32[]{:S(2)}, u32[]{:S(2)}) collective-permute-start(f32[8,8,256]{2,1,0:T(8,128)S(1)} %get-tuple-element.23), channel_id=1, source_target_pairs={{1,0},{2,1},{3,2},{4,3},{5,4},{6,5},{7,6},{9,8},{10,9},{11,10},{12... | collective-permute-start | bytes 196616 | tf_op jit(solution)/shard_map/ppermute | solution.py:396
  8.8 1.9 %collective-permute-start.3 = (f32[22,8,256]{2,1,0:T(8,128)S(1)}, f32[22,8,256]{2,1,0:T(8,128)S(1)}, u32[]{:S(2)}, u32[]{:S(2)}) collective-permute-start(f32[22,8,256]{2,1,0:T(8,128)S(1)} %get-tuple-element.25), channel_id=1, source_target_pairs={{8,0},{16,8},{24,16},{32,24},{40,32},{48,40},{56,48},{64,56},{72,6... | collective-permute-start | bytes 540680 | tf_op jit(solution)/shard_map/ppermute | solution.py:396
  10.8 2.4 %collective-permute-start.2 = (f32[16,8,256]{2,1,0:T(8,128)S(1)}, f32[16,8,256]{2,1,0:T(8,128)S(1)}, u32[]{:S(2)}, u32[]{:S(2)}) collective-permute-start(f32[16,8,256]{2,1,0:T(8,128)S(1)} %get-tuple-element.24), channel_id=1, source_target_pairs={{0,8},{8,16},{16,24},{24,32},{32,40},{40,48},{48,56},{56,64},{64,7... | collective-permute-start | bytes 393224 | tf_op jit(solution)/shard_map/ppermute | solution.py:396
  13.2 0.0 collective-permute-done.low_ref.y_low
  13.2 0.5 collective-permute-done.1.high_ref.y_high
  13.7 4.8 %collective-permute-start.5 = (f32[14,8,256]{2,1,0:T(8,128)S(1)}, f32[14,8,256]{2,1,0:T(8,128)S(1)}, u32[]{:S(2)}, u32[]{:S(2)}) collective-permute-start(f32[14,8,256]{2,1,0:T(8,128)S(1)} %get-tuple-element.27), channel_id=1, source_target_pairs={{8,0},{16,8},{24,16},{32,24},{40,32},{48,40},{56,48},{64,56},{72,6... | collective-permute-start | bytes 344072 | tf_op jit(solution)/shard_map/ppermute | solution.py:396
  18.5 1.9 %collective-permute-start.4 = (f32[12,8,256]{2,1,0:T(8,128)S(1)}, f32[12,8,256]{2,1,0:T(8,128)S(1)}, u32[]{:S(2)}, u32[]{:S(2)}) collective-permute-start(f32[12,8,256]{2,1,0:T(8,128)S(1)} %get-tuple-element.26), channel_id=1, source_target_pairs={{0,8},{8,16},{16,24},{24,32},{32,40},{40,48},{48,56},{56,64},{64,7... | collective-permute-start | bytes 294920 | tf_op jit(solution)/shard_map/ppermute | solution.py:396
  20.4 0.0 collective-permute-done.2.x_low
  20.4 4.0 %collective-permute-done.4.corner_low = f32[12,8,256]{2,1,0:T(8,128)S(1)} collective-permute-done((f32[12,8,256]{2,1,0:T(8,128)S(1)}, f32[12,8,256]{2,1,0:T(8,128)S(1)}, u32[]{:S(2)}, u32[]{:S(2)}) %collective-permute-start.4) | collective-permute-done | bytes 98336 | tf_op jit(solution)/shard_map/ppermute | solution.py:396
  24.4 0.0 collective-permute-done.3.x_high
  24.4 0.0 collective-permute-done.5.corner_high
  24.4 2.5 %basis.1 = (f32[16,128]{1,0:T(8,128)}, f32[3,5,24,256]{3,2,1,0:T(8,128)S(1)}, f32[4,24,256]{2,1,0:T(8,128)S(1)}) custom-call(f32[4,16,256]{2,1,0:T(8,128)S(1)} %copy-done, f32[4,16,256]{2,1,0:T(8,128)S(1)} %get-tuple-element.20.free_ref, f32[4,16,256]{2,1,0:T(8,128)S(1)} %get-tuple-element.21.rhs_ref, f32[8,8,256]{2,1,0:T(8,128)S(1)} %collective-permute-done.low_ref.y_low, ...), custom_call_target="tpu_custom_call" | custom-call | bytes 1048576 | tf_op jit(solution)/shard_map/basis/pallas_call | solution.py:413
  26.9 7.4 %all-to-all-start = ((f32[16,1,128]{2,1,0:T(1,128)}), f32[16,1,128]{2,1,0:T(1,128)S(1)}, u32[]{:S(2)}, u32[]{:S(2)}) async-start(f32[16,1,128]{2,1,0:T(1,128)} %bitcast.1), calls=%async_computation | async-start | bytes 16384 | tf_op jit(solution)/shard_map/all_to_all | solution.py:475
  34.3 0.9 %integrand.1 = (f32[3,4,24,256]{3,2,1,0:T(8,128)S(1)}, f32[3,24,256]{2,1,0:T(8,128)S(1)}, f32[3,24,256]{2,1,0:T(8,128)S(1)}) custom-call(f32[3,5,24,256]{3,2,1,0:T(8,128)S(1)} %get-tuple-element.29.basis_ref, f32[4,24,256]{2,1,0:T(8,128)S(1)} %get-tuple-element.30.solid_ref, f32[4,16,256]{2,1,0:T(8,128)S(1)} %get-tuple-element.31.warmth_ref, ...), custom_call_target="tpu_custom_call" | custom-call | flops 40000000 | bytes 1048576 | tf_op jit(solution)/shard_map/integrand/pallas_call | solution.py:413
  35.2 6.6 %all-to-all-done = f32[16,1,128]{2,1,0:T(1,128)S(1)} async-done(((f32[16,1,128]{2,1,0:T(1,128)}), f32[16,1,128]{2,1,0:T(1,128)S(1)}, u32[]{:S(2)}, u32[]{:S(2)}) %all-to-all-start) | async-done | bytes 8224 | tf_op jit(solution)/shard_map/all_to_all | solution.py:475
  41.9 1.9 %collective-permute-start.6 = (f32[3,24,256]{2,1,0:T(8,128)S(1)}, f32[3,24,256]{2,1,0:T(8,128)S(1)}, u32[]{:S(2)}, u32[]{:S(2)}) collective-permute-start(f32[3,24,256]{2,1,0:T(8,128)S(1)} %get-tuple-element.36), channel_id=1, source_target_pairs={{0,8},{8,16},{16,24},{24,32},{32,40},{40,48},{48,56},{56,64},{64,7... | collective-permute-start | bytes 221192 | tf_op jit(solution)/shard_map/ppermute | solution.py:396
  43.8 3.6 %collective-permute-start.7 = (f32[3,24,256]{2,1,0:T(8,128)S(1)}, f32[3,24,256]{2,1,0:T(8,128)S(1)}, u32[]{:S(2)}, u32[]{:S(2)}) collective-permute-start(f32[3,24,256]{2,1,0:T(8,128)S(1)} %get-tuple-element.37), channel_id=1, source_target_pairs={{8,0},{16,8},{24,16},{32,24},{40,32},{48,40},{56,48},{64,56},{72,6... | collective-permute-start | bytes 221192 | tf_op jit(solution)/shard_map/ppermute | solution.py:396
  47.4 0.6 broadcast_in_dim.9
  48.1 21.6 %all-to-all-start.1 = ((f32[32,1,128]{2,1,0:T(1,128)}), f32[32,1,128]{2,1,0:T(1,128)S(1)}, u32[]{:S(2)}, u32[]{:S(2)}) async-start(f32[32,1,128]{2,1,0:T(1,128)} %broadcast_in_dim.9), calls=%async_computation.1 | async-start | bytes 32768 | tf_op jit(solution)/shard_map/all_to_all | solution.py:488
  69.7 0.0 collective-permute-done.6.below_ref
  69.7 0.0 collective-permute-done.7.above_ref
  69.7 0.3 filter.1.parts_ref
  70.0 8.2 %all-to-all-done.1 = f32[32,1,128]{2,1,0:T(1,128)S(1)} async-done(((f32[32,1,128]{2,1,0:T(1,128)}), f32[32,1,128]{2,1,0:T(1,128)S(1)}, u32[]{:S(2)}, u32[]{:S(2)}) %all-to-all-start.1) | async-done | bytes 16416 | tf_op jit(solution)/shard_map/all_to_all | solution.py:488
  78.2 0.8 combine.1
  (3 shorter events, 0.1 us)
Async XLA Ops:
  0.6 0.8 %copy-start = (f32[4,16,256]{2,1,0:T(8,128)S(1)}, f32[4,16,256]{2,1,0:T(8,128)}, u32[]{:S(2)}) copy-start(f32[4,16,256]{2,1,0:T(8,128)} %design_ref.1) | copy-start | bytes 196612
  1.5 0.8 %copy-start.1 = (f32[4,16,256]{2,1,0:T(8,128)S(1)}, f32[4,16,256]{2,1,0:T(8,128)}, u32[]{:S(2)}) copy-start(f32[4,16,256]{2,1,0:T(8,128)} %primal_ref.1) | copy-start | bytes 196612
  2.3 0.8 %copy-start.2 = (s32[4,16,256]{2,1,0:T(8,128)S(1)}, s32[4,16,256]{2,1,0:T(8,128)}, u32[]{:S(2)}) copy-start(s32[4,16,256]{2,1,0:T(8,128)} %source_ref.1) | copy-start | bytes 196612
  3.2 0.8 %copy-start.3 = (s32[4,16,256]{2,1,0:T(8,128)S(1)}, s32[4,16,256]{2,1,0:T(8,128)}, u32[]{:S(2)}) copy-start(s32[4,16,256]{2,1,0:T(8,128)} %fixed_ref.1) | copy-start | bytes 196612
  4.0 9.1 %collective-permute-start = (f32[8,8,256]{2,1,0:T(8,128)S(1)}, f32[8,8,256]{2,1,0:T(8,128)S(1)}, u32[]{:S(2)}, u32[]{:S(2)}) collective-permute-start(f32[8,8,256]{2,1,0:T(8,128)S(1)} %get-tuple-element.22), channel_id=1, source_target_pairs={{0,1},{1,2},{2,3},{3,4},{4,5},{5,6},{6,7},{8,9},{9,10},{10,11},{11... | collective-permute-start | bytes 196616 | tf_op jit(solution)/shard_map/ppermute | solution.py:396
  7.5 6.2 %collective-permute-start.1 = (f32[8,8,256]{2,1,0:T(8,128)S(1)}, f32[8,8,256]{2,1,0:T(8,128)S(1)}, u32[]{:S(2)}, u32[]{:S(2)}) collective-permute-start(f32[8,8,256]{2,1,0:T(8,128)S(1)} %get-tuple-element.23), channel_id=1, source_target_pairs={{1,0},{2,1},{3,2},{4,3},{5,4},{6,5},{7,6},{9,8},{10,9},{11,10},{12... | collective-permute-start | bytes 196616 | tf_op jit(solution)/shard_map/ppermute | solution.py:396
  8.8 15.6 %collective-permute-start.3 = (f32[22,8,256]{2,1,0:T(8,128)S(1)}, f32[22,8,256]{2,1,0:T(8,128)S(1)}, u32[]{:S(2)}, u32[]{:S(2)}) collective-permute-start(f32[22,8,256]{2,1,0:T(8,128)S(1)} %get-tuple-element.25), channel_id=1, source_target_pairs={{8,0},{16,8},{24,16},{32,24},{40,32},{48,40},{56,48},{64,56},{72,6... | collective-permute-start | bytes 540680 | tf_op jit(solution)/shard_map/ppermute | solution.py:396
  10.8 9.6 %collective-permute-start.2 = (f32[16,8,256]{2,1,0:T(8,128)S(1)}, f32[16,8,256]{2,1,0:T(8,128)S(1)}, u32[]{:S(2)}, u32[]{:S(2)}) collective-permute-start(f32[16,8,256]{2,1,0:T(8,128)S(1)} %get-tuple-element.24), channel_id=1, source_target_pairs={{0,8},{8,16},{16,24},{24,32},{32,40},{40,48},{48,56},{56,64},{64,7... | collective-permute-start | bytes 393224 | tf_op jit(solution)/shard_map/ppermute | solution.py:396
  13.7 10.7 %collective-permute-start.5 = (f32[14,8,256]{2,1,0:T(8,128)S(1)}, f32[14,8,256]{2,1,0:T(8,128)S(1)}, u32[]{:S(2)}, u32[]{:S(2)}) collective-permute-start(f32[14,8,256]{2,1,0:T(8,128)S(1)} %get-tuple-element.27), channel_id=1, source_target_pairs={{8,0},{16,8},{24,16},{32,24},{40,32},{48,40},{56,48},{64,56},{72,6... | collective-permute-start | bytes 344072 | tf_op jit(solution)/shard_map/ppermute | solution.py:396
  18.5 5.9 %collective-permute-start.4 = (f32[12,8,256]{2,1,0:T(8,128)S(1)}, f32[12,8,256]{2,1,0:T(8,128)S(1)}, u32[]{:S(2)}, u32[]{:S(2)}) collective-permute-start(f32[12,8,256]{2,1,0:T(8,128)S(1)} %get-tuple-element.26), channel_id=1, source_target_pairs={{0,8},{8,16},{16,24},{24,32},{32,40},{40,48},{48,56},{56,64},{64,7... | collective-permute-start | bytes 294920 | tf_op jit(solution)/shard_map/ppermute | solution.py:396
  26.9 14.9 %all-to-all-start = ((f32[16,1,128]{2,1,0:T(1,128)}), f32[16,1,128]{2,1,0:T(1,128)S(1)}, u32[]{:S(2)}, u32[]{:S(2)}) async-start(f32[16,1,128]{2,1,0:T(1,128)} %bitcast.1), calls=%async_computation | async-start | bytes 16384 | tf_op jit(solution)/shard_map/all_to_all | solution.py:475
  41.9 27.8 %collective-permute-start.6 = (f32[3,24,256]{2,1,0:T(8,128)S(1)}, f32[3,24,256]{2,1,0:T(8,128)S(1)}, u32[]{:S(2)}, u32[]{:S(2)}) collective-permute-start(f32[3,24,256]{2,1,0:T(8,128)S(1)} %get-tuple-element.36), channel_id=1, source_target_pairs={{0,8},{8,16},{16,24},{24,32},{32,40},{40,48},{48,56},{56,64},{64,7... | collective-permute-start | bytes 221192 | tf_op jit(solution)/shard_map/ppermute | solution.py:396
  43.8 25.9 %collective-permute-start.7 = (f32[3,24,256]{2,1,0:T(8,128)S(1)}, f32[3,24,256]{2,1,0:T(8,128)S(1)}, u32[]{:S(2)}, u32[]{:S(2)}) collective-permute-start(f32[3,24,256]{2,1,0:T(8,128)S(1)} %get-tuple-element.37), channel_id=1, source_target_pairs={{8,0},{16,8},{24,16},{32,24},{40,32},{48,40},{56,48},{64,56},{72,6... | collective-permute-start | bytes 221192 | tf_op jit(solution)/shard_map/ppermute | solution.py:396
  48.1 30.1 %all-to-all-start.1 = ((f32[32,1,128]{2,1,0:T(1,128)}), f32[32,1,128]{2,1,0:T(1,128)S(1)}, u32[]{:S(2)}, u32[]{:S(2)}) async-start(f32[32,1,128]{2,1,0:T(1,128)} %broadcast_in_dim.9), calls=%async_computation.1 | async-start | bytes 32768 | tf_op jit(solution)/shard_map/all_to_all | solution.py:488

commit v4 on v1

--- a/solution.py
+++ b/solution.py
@@ -17,6 +17,8 @@
 NEAR = 4
 BASIS = 3
 MOMENTS = 8
+VMEM_LIMIT = 12 << 20
+LOAD_LIMIT = 857 << 16
 
 
 def up(arr, axis):
@@ -130,11 +132,100 @@
     )
 
 
+def roll_rows(tile, step):
+    return pltpu.roll(tile, step % tile.shape[0], 0)
+
+
+def load_kernel(
+    n, material_hbm, primal_hbm, source_hbm, fixed_hbm,
+    design_ref, free_ref, rhs_ref, warmth_ref, y_up_ref, y_down_ref,
+    primal_ref, source_ref, fixed_ref, arrived,
+):
+    copies = [
+        pltpu.make_async_copy(source, target, arrived.at[k])
+        for k, (source, target) in enumerate(
+            (
+                (material_hbm, design_ref),
+                (primal_hbm, primal_ref),
+                (source_hbm, source_ref),
+                (fixed_hbm, fixed_ref),
+            )
+        )
+    ]
+    for copy in copies:
+        copy.start()
+    for copy in copies:
+        copy.wait()
+    row = lax.broadcasted_iota(jnp.int32, (8, design_ref.shape[-1]), 0)
+    for i in range(n):
+        free = (1 - fixed_ref[i]).astype(jnp.float32)
+        warmth = free * primal_ref[i]
+        rhs = source_ref[i].astype(jnp.float32) * warmth
+        design = design_ref[i]
+        free_ref[i] = free
+        warmth_ref[i] = warmth
+        rhs_ref[i] = rhs
+        y_up_ref[i] = jnp.where(row >= 3, design[-8:], roll_rows(free[-8:], 3))
+        y_up_ref[n + i] = jnp.where(row >= 5, rhs[-8:], roll_rows(warmth[-8:], 1))
+        y_down_ref[i] = jnp.where(row < 5, design[:8], roll_rows(warmth[:8], 5))
+        y_down_ref[n + i] = jnp.where(row < 4, rhs[:8], roll_rows(free[:8], 4))
+
+
+def extend_kernel(
+    n, own_rows, design_in, free_in, rhs_in, warmth_in, low_ref, high_ref,
+    design_ref, free_ref, rhs_ref, warmth_ref, up_ref, down_ref, far_up_ref, far_down_ref,
+):
+    z = design_in.shape[-1]
+
+    def joined(low, middle, high):
+        return jnp.concatenate([low, middle, high], axis=0)
+
+    def near(low, middle, high):
+        return joined(low, middle, high)[WIDE - NEAR : own_rows + WIDE + NEAR]
+
+    spots = {id(up_ref): 0, id(down_ref): 0}
+
+    def put(ref, value):
+        count = value.shape[0] // 8
+        spot = spots[id(ref)]
+        ref[spot : spot + count] = value.reshape(count, 8, z)
+        spots[id(ref)] = spot + count
+
+    for i in range(n):
+        value = joined(low_ref[i], design_in[i], high_ref[i])
+        design_ref[i] = value
+        put(up_ref, value)
+        put(down_ref, value)
+        if i == 0:
+            far_down_ref[0] = value
+        if i == n - 1:
+            far_up_ref[0] = value
+    for i in range(n):
+        value = near(roll_rows(low_ref[i], -3), free_in[i], roll_rows(high_ref[n + i], -4))
+        free_ref[i] = value
+        put(down_ref, value)
+        if i > 0:
+            put(up_ref, value)
+    for i in range(n):
+        value = near(low_ref[n + i], rhs_in[i], high_ref[n + i])
+        rhs_ref[i] = value
+        put(down_ref, value)
+        if i > 0:
+            put(up_ref, value)
+    for i in range(n):
+        value = near(roll_rows(low_ref[n + i], -1), warmth_in[i], roll_rows(high_ref[i], -5))
+        warmth_ref[i] = value
+        if i < 2:
+            put(down_ref, value)
+        if i == n - 1:
+            put(up_ref, value)
+
+
 def basis_kernel(
     n, own_rows, layers, rows,
     design_ref, free_ref, rhs_ref, lo_ref, hi_ref, below_ref, above_ref,
     moments_ref, basis_ref, solid_ref,
-    conduct_s, diag_s, inv_s, u0_s, u1_s,
+    conduct_s, inv_s, u0_s, u1_s,
 ):
     first_layer = lax.axis_index("gx") * n
     first_row = lax.axis_index("gy") * own_rows
@@ -183,7 +274,6 @@
         free = free_at(i)
         diag = free * (pair * (1.0 / 3.0)) + (1.0 - free)
         inverse = 1.0 / diag
-        diag_s[i + n - 1] = diag
         inv_s[i + n - 1] = inverse
         u0_s[i + n - 1] = rhs_at(i) * inverse
 
@@ -314,68 +404,78 @@
 
 def body(gx, gy, material_fraction, primal_warmth, empty_region_flags, dirichlet_flags):
     n, own_rows, z = material_fraction.shape
-    layers, rows = gx * n, gy * own_rows
-    free = (1 - dirichlet_flags).astype(jnp.float32)
-    warmth = free * primal_warmth
-    rhs = empty_region_flags.astype(jnp.float32) * warmth
-    design = material_fraction
-
-    from_low = shifted(
-        jnp.concatenate(
-            [design[:, -5:], free[:, -3:], rhs[:, -3:], warmth[:, -1:]], axis=1
-        ),
-        "gy", 1,
-    )
-    from_high = shifted(
-        jnp.concatenate([design[:, :5], free[:, :4], rhs[:, :4], warmth[:, :2]], axis=1),
-        "gy", -1,
-    )
-
-    def blank(count):
-        return jnp.zeros((n, count, z), jnp.float32)
-
-    design = jnp.concatenate([blank(3), from_low[:, :5], design, from_high[:, :5], blank(3)], axis=1)
-    free = jnp.concatenate([blank(1), from_low[:, 5:8], free, from_high[:, 5:9]], axis=1)
-    rhs = jnp.concatenate([blank(1), from_low[:, 8:11], rhs, from_high[:, 9:13]], axis=1)
-    warmth = jnp.concatenate([blank(3), from_low[:, 11:12], warmth, from_high[:, 13:15], blank(2)], axis=1)
-
-    def tiles(*pieces):
-        return jnp.concatenate([p.reshape(-1, 8, z) for p in pieces], axis=0)
-
-    lo = shifted(tiles(design, free[1:], rhs[1:], warmth[n - 1 :]), "gx", 1)
-    hi = shifted(tiles(design, free, rhs, warmth[:2]), "gx", -1)
-    below = shifted(design[n - 1 :], "gx", 2)
-    above = shifted(design[:1], "gx", -2)
-
-    near = own_rows + 2 * NEAR
-    f32 = jnp.float32
+    sizes = (n, own_rows, gx * n, gy * own_rows)
+    near, wide = own_rows + 2 * NEAR, own_rows + 2 * WIDE
+    near_tiles, wide_tiles = near // 8, wide // 8
+
+    def call(name, kernel, outs, *operands, scratch=(), space=pltpu.VMEM, limit=VMEM_LIMIT, flops=0):
+        return pl.pallas_call(
+            kernel,
+            out_shape=[jax.ShapeDtypeStruct(shape, jnp.float32) for shape in outs],
+            in_specs=[pl.BlockSpec(memory_space=space)] * len(operands),
+            out_specs=[pl.BlockSpec(memory_space=pltpu.VMEM)] * len(outs),
+            scratch_shapes=list(scratch),
+            compiler_params=pltpu.CompilerParams(vmem_limit_bytes=limit),
+            cost_estimate=pl.CostEstimate(flops=flops, bytes_accessed=1 << 20, transcendentals=0),
+            name=name,
+        )(*operands)
+
+    def floats(*shape):
+        return pltpu.VMEM(shape, jnp.float32)
+
+    brick_shape = (n, own_rows, z)
+    *own, y_up, y_down = call(
+        "load",
+        functools.partial(load_kernel, n),
+        [brick_shape] * 4 + [(2 * n, 8, z)] * 2,
+        material_fraction, primal_warmth, empty_region_flags, dirichlet_flags,
+        scratch=[
+            floats(*brick_shape),
+            pltpu.VMEM(brick_shape, jnp.int32),
+            pltpu.VMEM(brick_shape, jnp.int32),
+            pltpu.SemaphoreType.DMA((4,)),
+        ],
+        space=pltpu.HBM,
+        limit=LOAD_LIMIT,
+    )
+    y_low = shifted(y_up, "gy", 1)
+    y_high = shifted(y_down, "gy", -1)
+    up_tiles = n * wide_tiles + (2 * (n - 1) + 1) * near_tiles
+    down_tiles = n * wide_tiles + (2 * n + 2) * near_tiles
+    design, free, rhs, warmth, up, down, far_up, far_down = call(
+        "extend",
+        functools.partial(extend_kernel, n, own_rows),
+        [(n, wide, z)] + [(n, near, z)] * 3
+        + [(up_tiles, 8, z), (down_tiles, 8, z), (1, wide, z), (1, wide, z)],
+        *own, y_low, y_high,
+    )
+    lo = shifted(up, "gx", 1)
+    hi = shifted(down, "gx", -1)
+    below = shifted(far_up, "gx", 2)
+    above = shifted(far_down, "gx", -2)
+
     inner = min(16, gx)
     outer = gx * gy // inner
-    sizes = (n, own_rows, layers, rows)
-    moments, basis, solid = pl.pallas_call(
+    moments, basis, solid = call(
+        "basis",
         functools.partial(basis_kernel, *sizes),
-        out_shape=(
-            jax.ShapeDtypeStruct((inner, 128), f32),
-            jax.ShapeDtypeStruct((BASIS, n + 3, near, z), f32),
-            jax.ShapeDtypeStruct((n + 2, near, z), f32),
-        ),
-        scratch_shapes=[
-            pltpu.VMEM((3 * n, near, z), f32),
-            pltpu.VMEM((3 * n - 1, near, z), f32),
-            pltpu.VMEM((3 * n - 1, near, z), f32),
-            pltpu.VMEM((3 * n - 1, near, z), f32),
-            pltpu.VMEM((3 * n - 3, near, z), f32),
+        [(inner, 128), (BASIS, n + 3, near, z), (n + 2, near, z)],
+        design, free, rhs, lo, hi, below, above,
+        scratch=[
+            floats(3 * n, near, z),
+            floats(3 * n - 1, near, z),
+            floats(3 * n - 1, near, z),
+            floats(3 * n - 3, near, z),
         ],
-        name="basis",
-    )(design, free, rhs, lo, hi, below, above)
-
-    parts = pl.pallas_call(
+    )
+    (parts,) = call(
+        "sensitivity_parts",
         functools.partial(sensitivity_kernel, *sizes),
-        out_shape=jax.ShapeDtypeStruct((BASIS, n, own_rows, z), f32),
-        scratch_shapes=[pltpu.VMEM((BASIS, n + 2, near, z), f32)],
-        name="sensitivity_parts",
-        cost_estimate=pl.CostEstimate(flops=40000000, bytes_accessed=2000000, transcendentals=0),
-    )(basis, solid, warmth, lo, hi)
+        [(BASIS,) + brick_shape],
+        basis, solid, warmth, lo, hi,
+        scratch=[floats(BASIS, n + 2, near, z)],
+        flops=40000000,
+    )
 
     first = [[g * inner + j for j in range(inner)] for g in range(gx // inner)]
     first = [[d * gy + y for d in group] for group in first for y in range(gy)]
@@ -386,15 +486,14 @@
     moments = lax.all_to_all(moments, ("gx", "gy"), 0, 0, axis_index_groups=first, tiled=True)
     moments = jnp.broadcast_to(jnp.sum(moments, axis=0, keepdims=True), (outer, 128))
     moments = lax.all_to_all(moments, ("gx", "gy"), 0, 0, axis_index_groups=second, tiled=True)
-
-    return pl.pallas_call(
-        functools.partial(final_kernel, n, own_rows),
-        out_shape=(
-            jax.ShapeDtypeStruct((n, own_rows, z), f32),
-            jax.ShapeDtypeStruct((n, own_rows, z), f32),
-        ),
-        name="combine",
-    )(moments, basis, parts)
+    return tuple(
+        call(
+            "combine",
+            functools.partial(final_kernel, n, own_rows),
+            [brick_shape, brick_shape],
+            moments, basis, parts,
+        )
+    )
 
 
 def solution(mesh):

time: 78.7 us -> 69.7 us (0.89)
  local copies, waits for them, and re-layouts: 6.63 us -> 0.62 us
  waiting for transfers between devices: 11.8 us -> 16.9 us
  starting transfers between devices: 36 us -> 31.1 us
  Pallas kernels: 9.23 us -> 5.12 us
  blocking collectives: 12.3 us -> 14.8 us
  other arithmetic: 1.12 us -> 0.03 us
    unnamed x28 -> x0, local copies, waits for them, and re-layouts: 4.15 us -> none
    pallas_call x3 -> x5, Pallas kernels: 9.23 us -> 5.12 us  [call(): pl.pallas_call(kernel, out_shape=[jax.ShapeDtypeStruct(shape, jnp.float32...]
    ppermute x6, waiting for transfers between devices: 4.05 us -> 7.07 us  [shifted(): lax.ppermute(arr, axis, [(i, i + step) for i in range(count) if 0 <= i +...]
    ppermute x6, starting transfers between devices: 19.7 us -> 17 us  [shifted(): lax.ppermute(arr, axis, [(i, i + step) for i in range(count) if 0 <= i +...]
    all_to_all x1, blocking collectives: 12.3 us -> 14.8 us  [body(): lax.all_to_all(moments, ('gx', 'gy'), 0, 0, axis_index_groups=first, tile...]
    all_to_all x1, starting transfers between devices: 16.3 us -> 14.1 us  [body(): lax.all_to_all(moments, ('gx', 'gy'), 0, 0, axis_index_groups=second, til...]
    all_to_all x1, waiting for transfers between devices: 7.78 us -> 9.79 us  [body(): lax.all_to_all(moments, ('gx', 'gy'), 0, 0, axis_index_groups=second, til...]
    slice x19 -> x0, local copies, waits for them, and re-layouts: 1.59 us -> none  [the longest x2 0.78 us: body(): from_low[:, :5]]
  transfers between devices with their start and end apart: 7 -> 7, of which waited for: 3 -> 4; matrix products, arithmetic and copies ran while one was open for 0% -> 0% of each run, Pallas kernels for 4% -> 2%
where the time goes in v4:
time: 69.7 us; the launch traced here: 69.3 us
  starting transfers between devices  31.1 us (45%)
  waiting for transfers between devices  16.9 us (24%)
  blocking collectives  14.8 us (21%)
  Pallas kernels  5.12 us (7%)
  between operations  0.71 us (1%)
    ppermute x6, starting transfers between devices, shifted(): lax.ppermute(arr, axis, [(i, i + step) for i in range(count) if 0 <= i +...  17 us
    all_to_all x1, blocking collectives, body(): lax.all_to_all(moments, ('gx', 'gy'), 0, 0, axis_index_groups=first, tile...  14.8 us
    all_to_all x1, starting transfers between devices, body(): lax.all_to_all(moments, ('gx', 'gy'), 0, 0, axis_index_groups=second, til...  14.1 us
    all_to_all x1, waiting for transfers between devices, body(): lax.all_to_all(moments, ('gx', 'gy'), 0, 0, axis_index_groups=second, til...  9.79 us
    ppermute x6, waiting for transfers between devices, shifted(): lax.ppermute(arr, axis, [(i, i + step) for i in range(count) if 0 <= i +...  7.07 us
    pallas_call x5, Pallas kernels, call(): pl.pallas_call(kernel, out_shape=[jax.ShapeDtypeStruct(shape, jnp.float32...  5.12 us
  transfers between devices with their start and end apart: 7, of which 4 were waited for; matrix products, arithmetic and copies ran while one was open for 0% of the time, Pallas kernels for 2%

profile of v4, /device:TPU:1, one launch (start us, length us, event | category | flops | bytes accessed | tf_op | source)
XLA Modules:
  0.0 69.3 jit_solution(10686555729543781290)
XLA Ops:
  0.6 1.0 %load.1 = (f32[4,16,256]{2,1,0:T(8,128)S(1)}, f32[4,16,256]{2,1,0:T(8,128)S(1)}, f32[4,16,256]{2,1,0:T(8,128)S(1)}, f32[4,16,256]{2,1,0:T(8,128)S(1)}, f32[8,8,2...) custom-call(f32[4,16,256]{2,1,0:T(8,128)} %material_hbm.1, f32[4,16,256]{2,1,0:T(8,128)} %primal_hbm.1, ...), custom_call_target="tpu_custom_call" | custom-call | bytes 1048576 | tf_op jit(solution)/shard_map/load/pallas_call | solution.py:412
  1.6 4.0 %collective-permute-start = (f32[8,8,256]{2,1,0:T(8,128)S(1)}, f32[8,8,256]{2,1,0:T(8,128)S(1)}, u32[]{:S(2)}, u32[]{:S(2)}) collective-permute-start(f32[8,8,256]{2,1,0:T(8,128)S(1)} %get-tuple-element.23), channel_id=1, source_target_pairs={{0,1},{1,2},{2,3},{3,4},{4,5},{5,6},{6,7},{8,9},{9,10},{10,11},{11... | collective-permute-start | bytes 196616 | tf_op jit(solution)/shard_map/ppermute | solution.py:402
  5.7 1.3 %collective-permute-start.1 = (f32[8,8,256]{2,1,0:T(8,128)S(1)}, f32[8,8,256]{2,1,0:T(8,128)S(1)}, u32[]{:S(2)}, u32[]{:S(2)}) collective-permute-start(f32[8,8,256]{2,1,0:T(8,128)S(1)} %get-tuple-element.24), channel_id=1, source_target_pairs={{1,0},{2,1},{3,2},{4,3},{5,4},{6,5},{7,6},{9,8},{10,9},{11,10},{12... | collective-permute-start | bytes 196616 | tf_op jit(solution)/shard_map/ppermute | solution.py:402
  7.0 0.0 collective-permute-done.low_ref
  7.0 3.7 %collective-permute-done.1.high_ref = f32[8,8,256]{2,1,0:T(8,128)S(1)} collective-permute-done((f32[8,8,256]{2,1,0:T(8,128)S(1)}, f32[8,8,256]{2,1,0:T(8,128)S(1)}, u32[]{:S(2)}, u32[]{:S(2)}) %collective-permute-start.1) | collective-permute-done | bytes 65568 | tf_op jit(solution)/shard_map/ppermute | solution.py:402
  10.7 0.1 extend.1
  10.8 7.2 %collective-permute-start.3 = (f32[46,8,256]{2,1,0:T(8,128)S(1)}, f32[46,8,256]{2,1,0:T(8,128)S(1)}, u32[]{:S(2)}, u32[]{:S(2)}) collective-permute-start(f32[46,8,256]{2,1,0:T(8,128)S(1)} %get-tuple-element.29), channel_id=1, source_target_pairs={{8,0},{16,8},{24,16},{32,24},{40,32},{48,40},{56,48},{64,56},{72,6... | collective-permute-start | bytes 1130504 | tf_op jit(solution)/shard_map/ppermute | solution.py:402
  18.0 1.9 %collective-permute-start.2 = (f32[37,8,256]{2,1,0:T(8,128)S(1)}, f32[37,8,256]{2,1,0:T(8,128)S(1)}, u32[]{:S(2)}, u32[]{:S(2)}) collective-permute-start(f32[37,8,256]{2,1,0:T(8,128)S(1)} %get-tuple-element.28), channel_id=1, source_target_pairs={{0,8},{8,16},{16,24},{24,32},{32,40},{40,48},{48,56},{56,64},{64,7... | collective-permute-start | bytes 909320 | tf_op jit(solution)/shard_map/ppermute | solution.py:402
  19.9 1.3 %collective-permute-start.4 = (f32[1,32,256]{2,1,0:T(8,128)S(1)}, f32[1,32,256]{2,1,0:T(8,128)S(1)}, u32[]{:S(2)}, u32[]{:S(2)}) collective-permute-start(f32[1,32,256]{2,1,0:T(8,128)S(1)} %get-tuple-element.30), channel_id=1, source_target_pairs={{0,16},{8,24},{16,32},{24,40},{32,48},{40,56},{48,64},{56,72},{64,... | collective-permute-start | bytes 98312 | tf_op jit(solution)/shard_map/ppermute | solution.py:402
  21.2 1.3 %collective-permute-start.5 = (f32[1,32,256]{2,1,0:T(8,128)S(1)}, f32[1,32,256]{2,1,0:T(8,128)S(1)}, u32[]{:S(2)}, u32[]{:S(2)}) collective-permute-start(f32[1,32,256]{2,1,0:T(8,128)S(1)} %get-tuple-element.31), channel_id=1, source_target_pairs={{16,0},{24,8},{32,16},{40,24},{48,32},{56,40},{64,48},{72,56},{80,... | collective-permute-start | bytes 98312 | tf_op jit(solution)/shard_map/ppermute | solution.py:402
  22.5 1.8 %collective-permute-done.4.below_ref = f32[1,32,256]{2,1,0:T(8,128)S(1)} collective-permute-done((f32[1,32,256]{2,1,0:T(8,128)S(1)}, f32[1,32,256]{2,1,0:T(8,128)S(1)}, u32[]{:S(2)}, u32[]{:S(2)}) %collective-permute-start.4) | collective-permute-done | bytes 32800 | tf_op jit(solution)/shard_map/ppermute | solution.py:402
  24.3 1.5 %collective-permute-done.5.above_ref = f32[1,32,256]{2,1,0:T(8,128)S(1)} collective-permute-done((f32[1,32,256]{2,1,0:T(8,128)S(1)}, f32[1,32,256]{2,1,0:T(8,128)S(1)}, u32[]{:S(2)}, u32[]{:S(2)}) %collective-permute-start.5) | collective-permute-done | bytes 32800 | tf_op jit(solution)/shard_map/ppermute | solution.py:402
  25.9 0.0 collective-permute-done.2.lo_ref
  25.9 0.0 collective-permute-done.3.hi_ref
  25.9 2.1 %basis.1 = (f32[16,128]{1,0:T(8,128)S(1)}, f32[3,7,24,256]{3,2,1,0:T(8,128)S(1)}, f32[6,24,256]{2,1,0:T(8,128)S(1)}) custom-call(f32[4,32,256]{2,1,0:T(8,128)S(1)} %get-tuple-element.25.design_ref, f32[4,24,256]{2,1,0:T(8,128)S(1)} %get-tuple-element.26.free_ref, f32[4,24,256]{2,1,0:T(8,128)S(1)} %get-tuple-element.27.rhs_ref, ...), custom_call_target="tpu_custom_call" | custom-call | bytes 1048576 | tf_op jit(solution)/shard_map/basis/pallas_call | solution.py:412
  28.0 14.8 %all_to_all.17 = f32[16,1,128]{2,1,0:T(1,128)S(1)} all-to-all(f32[16,1,128]{2,1,0:T(1,128)S(1)} %bitcast.5), channel_id=1, replica_groups={{0,8,16,24,32,40,48,56,64,72,80,88,96,104,112,120},{1,9,17,25,33,41,49,..., dimensions={0} | all-to-all | bytes 16384 | tf_op jit(solution)/shard_map/all_to_all | solution.py:486
  42.8 0.6 broadcast_in_dim.2
  43.4 14.1 %all-to-all-start.1 = ((f32[32,1,128]{2,1,0:T(1,128)}), f32[32,1,128]{2,1,0:T(1,128)S(1)}, u32[]{:S(2)}, u32[]{:S(2)}) async-start(f32[32,1,128]{2,1,0:T(1,128)} %broadcast_in_dim.2), calls=%async_computation.1 | async-start | bytes 32768 | tf_op jit(solution)/shard_map/all_to_all | solution.py:488
  57.6 1.2 %sensitivity_parts.1.parts_ref = f32[3,4,16,256]{3,2,1,0:T(8,128)S(1)} custom-call(f32[3,7,24,256]{3,2,1,0:T(8,128)S(1)} %get-tuple-element.33.basis_ref, f32[6,24,256]{2,1,0:T(8,128)S(1)} %get-tuple-element.34.solid_ref, f32[4,24,256]{2,1,0:T(8,128)S(1)} %get-tuple-element.35.warmth_ref, f32[37,8,256]{2,1,0:T(8,128)S(1)} %collective-permute-done.2.lo_ref, ...), custom_call_target="tpu_custom_call" | custom-call | flops 40000000 | bytes 1048576 | tf_op jit(solution)/shard_map/sensitivity_parts/pallas_call | solution.py:412
  58.7 9.8 %all-to-all-done.1 = f32[32,1,128]{2,1,0:T(1,128)S(1)} async-done(((f32[32,1,128]{2,1,0:T(1,128)}), f32[32,1,128]{2,1,0:T(1,128)S(1)}, u32[]{:S(2)}, u32[]{:S(2)}) %all-to-all-start.1) | async-done | bytes 16416 | tf_op jit(solution)/shard_map/all_to_all | solution.py:488
  68.5 0.8 %combine.1 = (f32[4,16,256]{2,1,0:T(8,128)}, f32[4,16,256]{2,1,0:T(8,128)}) custom-call(f32[32,128]{1,0:T(8,128)S(1)} %bitcast.4, f32[3,7,24,256]{3,2,1,0:T(8,128)S(1)} %get-tuple-element.33.basis_ref, f32[3,4,16,256]{3,2,1,0:T(8,128)S(1)} %sensitivity_parts.1.parts_ref), custom_call_target="tpu_custom_call" | custom-call | bytes 1048576 | tf_op jit(solution)/shard_map/combine/pallas_call | solution.py:412
  (1 shorter events, 0.0 us)
Async XLA Ops:
  1.6 5.4 %collective-permute-start = (f32[8,8,256]{2,1,0:T(8,128)S(1)}, f32[8,8,256]{2,1,0:T(8,128)S(1)}, u32[]{:S(2)}, u32[]{:S(2)}) collective-permute-start(f32[8,8,256]{2,1,0:T(8,128)S(1)} %get-tuple-element.23), channel_id=1, source_target_pairs={{0,1},{1,2},{2,3},{3,4},{4,5},{5,6},{6,7},{8,9},{9,10},{10,11},{11... | collective-permute-start | bytes 196616 | tf_op jit(solution)/shard_map/ppermute | solution.py:402
  5.7 5.0 %collective-permute-start.1 = (f32[8,8,256]{2,1,0:T(8,128)S(1)}, f32[8,8,256]{2,1,0:T(8,128)S(1)}, u32[]{:S(2)}, u32[]{:S(2)}) collective-permute-start(f32[8,8,256]{2,1,0:T(8,128)S(1)} %get-tuple-element.24), channel_id=1, source_target_pairs={{1,0},{2,1},{3,2},{4,3},{5,4},{6,5},{7,6},{9,8},{10,9},{11,10},{12... | collective-permute-start | bytes 196616 | tf_op jit(solution)/shard_map/ppermute | solution.py:402
  10.8 15.1 %collective-permute-start.3 = (f32[46,8,256]{2,1,0:T(8,128)S(1)}, f32[46,8,256]{2,1,0:T(8,128)S(1)}, u32[]{:S(2)}, u32[]{:S(2)}) collective-permute-start(f32[46,8,256]{2,1,0:T(8,128)S(1)} %get-tuple-element.29), channel_id=1, source_target_pairs={{8,0},{16,8},{24,16},{32,24},{40,32},{48,40},{56,48},{64,56},{72,6... | collective-permute-start | bytes 1130504 | tf_op jit(solution)/shard_map/ppermute | solution.py:402
  18.0 7.9 %collective-permute-start.2 = (f32[37,8,256]{2,1,0:T(8,128)S(1)}, f32[37,8,256]{2,1,0:T(8,128)S(1)}, u32[]{:S(2)}, u32[]{:S(2)}) collective-permute-start(f32[37,8,256]{2,1,0:T(8,128)S(1)} %get-tuple-element.28), channel_id=1, source_target_pairs={{0,8},{8,16},{16,24},{24,32},{32,40},{40,48},{48,56},{56,64},{64,7... | collective-permute-start | bytes 909320 | tf_op jit(solution)/shard_map/ppermute | solution.py:402
  19.9 4.4 %collective-permute-start.4 = (f32[1,32,256]{2,1,0:T(8,128)S(1)}, f32[1,32,256]{2,1,0:T(8,128)S(1)}, u32[]{:S(2)}, u32[]{:S(2)}) collective-permute-start(f32[1,32,256]{2,1,0:T(8,128)S(1)} %get-tuple-element.30), channel_id=1, source_target_pairs={{0,16},{8,24},{16,32},{24,40},{32,48},{40,56},{48,64},{56,72},{64,... | collective-permute-start | bytes 98312 | tf_op jit(solution)/shard_map/ppermute | solution.py:402
  21.2 4.7 %collective-permute-start.5 = (f32[1,32,256]{2,1,0:T(8,128)S(1)}, f32[1,32,256]{2,1,0:T(8,128)S(1)}, u32[]{:S(2)}, u32[]{:S(2)}) collective-permute-start(f32[1,32,256]{2,1,0:T(8,128)S(1)} %get-tuple-element.31), channel_id=1, source_target_pairs={{16,0},{24,8},{32,16},{40,24},{48,32},{56,40},{64,48},{72,56},{80,... | collective-permute-start | bytes 98312 | tf_op jit(solution)/shard_map/ppermute | solution.py:402
  43.4 25.1 %all-to-all-start.1 = ((f32[32,1,128]{2,1,0:T(1,128)}), f32[32,1,128]{2,1,0:T(1,128)S(1)}, u32[]{:S(2)}, u32[]{:S(2)}) async-start(f32[32,1,128]{2,1,0:T(1,128)} %broadcast_in_dim.2), calls=%async_computation.1 | async-start | bytes 32768 | tf_op jit(solution)/shard_map/all_to_all | solution.py:488

commit v5 on v4

v5 whole, which is shorter than its diff:
```python
import functools
import math

import jax
import jax.numpy as jnp
from jax import lax
from jax.experimental import pallas as pl
from jax.experimental.pallas import tpu as pltpu
from jax.sharding import PartitionSpec as P

KMIN = 0.05
QZERO = 1.0
EDGE = 0.5
DIAGONAL = 1.5 - math.sqrt(2.0)

WIDE = 8
NEAR = 4
BASIS = 3
MOMENTS = 8
VMEM_LIMIT = 12 << 20
FAR_WORK = 10**10
LOAD_LIMIT = 857 << 16


def up(arr, axis):
    return pltpu.roll(arr, arr.shape[axis] - 1, axis)


def down(arr, axis):
    return pltpu.roll(arr, 1, axis)


def z_index(arr):
    return lax.broadcasted_iota(jnp.int32, arr.shape, 1)


def lift(arr):
    return jnp.where(z_index(arr) == arr.shape[1] - 1, 0.0, up(arr, 1))


def lower_z(arr):
    return jnp.where(z_index(arr) == 0, 0.0, down(arr, 1))


def filtered(below, here, above):
    beside = below + above
    rim = up(here, 0) + down(here, 0)
    corner = up(beside, 0) + down(beside, 0)
    flat = 1.5 * here + EDGE * (beside + rim) + DIAGONAL * corner
    slanted = EDGE * here + DIAGONAL * (beside + rim)
    return flat + lift(slanted) + lower_z(slanted)


def grid_flags(layer, layers, first_layer, first_row, rows, shape):
    def inside(at):
        return ((at >= 0) & (at < layers)).astype(jnp.float32)

    at = first_layer + layer
    row = first_row + lax.broadcasted_iota(jnp.int32, shape, 0)

    def row_inside(offset):
        return ((row + offset >= 0) & (row + offset < rows)).astype(jnp.float32)

    return inside(at), inside(at - 1) + inside(at + 1), row_inside(0), row_inside(-1) + row_inside(1)


def filter_weight(layer, layers, first_layer, first_row, rows, shape):
    here, beside, row_here, row_beside = grid_flags(
        layer, layers, first_layer, first_row, rows, shape
    )
    z = lax.broadcasted_iota(jnp.int32, shape, 1)
    z_beside = (z > 0).astype(jnp.float32) + (z < shape[1] - 1).astype(jnp.float32)
    flat = (1.5 + EDGE * beside) * row_here + (EDGE + DIAGONAL * beside) * row_beside
    slanted = (EDGE + DIAGONAL * beside) * row_here + DIAGONAL * row_beside
    valid = here * row_here
    return valid, jnp.where(valid > 0, flat + z_beside * slanted, 1.0)


def yz_modes(node):
    lifted = lift(node)
    plain, slope = node + lifted, lifted - node
    plain_up, slope_up = up(plain, 0), up(slope, 0)
    return plain + plain_up, slope + slope_up, plain_up - plain, slope_up - slope


def element_modes(low, high):
    return {
        "d0": (3.0, high[0] - low[0]),
        "s1": (3.0, high[1] + low[1]),
        "s2": (3.0, high[2] + low[2]),
        "d1": (2.0, high[1] - low[1]),
        "d2": (2.0, high[2] - low[2]),
        "s3": (2.0, high[3] + low[3]),
        "d3": (1.0, high[3] - low[3]),
    }


def apply_layers(node_at, conduct_at, first, count):
    low = yz_modes(node_at(first - 1))
    carried = None
    for element in range(first - 1, first + count):
        high = yz_modes(node_at(element + 1))
        scaled = conduct_at(element) * (1.0 / 48.0)
        flow = {key: (order * value) * scaled for key, (order, value) in element_modes(low, high).items()}
        zero_sum = flow["d0"]
        if carried is not None:
            planes = (
                carried[0] - zero_sum,
                carried[1] + (flow["s1"] - flow["d1"]),
                carried[2] + (flow["s2"] - flow["d2"]),
                carried[3] + (flow["s3"] - flow["d3"]),
            )
            smooth = (planes[0] - planes[2]) + down(planes[0] + planes[2], 0)
            slope = (planes[1] - planes[3]) + down(planes[1] + planes[3], 0)
            yield element, (smooth - slope) + lower_z(smooth + slope)
        carried = (
            zero_sum,
            flow["s1"] + flow["d1"],
            flow["s2"] + flow["d2"],
            flow["s3"] + flow["d3"],
        )
        low = high


def tile_sum(value):
    return functools.reduce(
        jnp.add,
        [
            value[r : r + 8, c : c + 128]
            for r in range(0, value.shape[0], 8)
            for c in range(0, value.shape[1], 128)
        ],
    )


def roll_rows(tile, step):
    return pltpu.roll(tile, step % tile.shape[0], 0)


def load_kernel(
    n, material_hbm, primal_hbm, source_hbm, fixed_hbm,
    design_ref, free_ref, rhs_ref, warmth_ref, y_up_ref, y_down_ref,
    primal_ref, source_ref, fixed_ref, arrived,
):
    copies = [
        pltpu.make_async_copy(source, target, arrived.at[k])
        for k, (source, target) in enumerate(
            (
                (material_hbm, design_ref),
                (primal_hbm, primal_ref),
                (source_hbm, source_ref),
                (fixed_hbm, fixed_ref),
            )
        )
    ]
    for copy in copies:
        copy.start()
    for copy in copies:
        copy.wait()
    row = lax.broadcasted_iota(jnp.int32, (8, design_ref.shape[-1]), 0)
    for i in range(n):
        free = (1 - fixed_ref[i]).astype(jnp.float32)
        warmth = free * primal_ref[i]
        rhs = source_ref[i].astype(jnp.float32) * warmth
        design = design_ref[i]
        free_ref[i] = free
        warmth_ref[i] = warmth
        rhs_ref[i] = rhs
        y_up_ref[i] = jnp.where(row >= 3, design[-8:], roll_rows(free[-8:], 3))
        y_up_ref[n + i] = jnp.where(row >= 5, rhs[-8:], roll_rows(warmth[-8:], 1))
        y_down_ref[i] = jnp.where(row < 5, design[:8], roll_rows(warmth[:8], 5))
        y_down_ref[n + i] = jnp.where(row < 4, rhs[:8], roll_rows(free[:8], 4))


class Layers:
    def __init__(self, n, own_rows, z):
        self.n, self.z = n, z
        self.wide, self.near = own_rows + 2 * WIDE, own_rows + 2 * NEAR
        self.tiles = (n * self.wide + (2 * n + 1) * self.near) // 8

    def place(self, which, layer):
        rows = self.near if which else self.wide
        start = layer * rows if which == 0 else self.n * self.wide + ((which - 1) * self.n + layer) * self.near
        return slice(start // 8, (start + rows) // 8), rows

    def put(self, ref, which, layer, value):
        place, rows = self.place(which, layer)
        ref[place] = value.reshape(rows // 8, 8, self.z)

    def get(self, ref, which, layer):
        place, rows = self.place(which, layer)
        return ref[place].reshape(rows, self.z)


def extend_kernel(
    n, own_rows, design_in, free_in, rhs_in, warmth_in, low_ref, high_ref, message_ref, warmth_ref
):
    layers = Layers(n, own_rows, design_in.shape[-1])

    def joined(low, middle, high):
        return jnp.concatenate([low, middle, high], axis=0)

    def near(low, middle, high):
        return joined(low, middle, high)[WIDE - NEAR : own_rows + WIDE + NEAR]

    for i in range(n):
        layers.put(message_ref, 0, i, joined(low_ref[i], design_in[i], high_ref[i]))
        layers.put(
            message_ref, 1, i, near(roll_rows(low_ref[i], -3), free_in[i], roll_rows(high_ref[n + i], -4))
        )
        layers.put(message_ref, 2, i, near(low_ref[n + i], rhs_in[i], high_ref[n + i]))
        warmth = near(roll_rows(low_ref[n + i], -1), warmth_in[i], roll_rows(high_ref[i], -5))
        warmth_ref[i] = warmth
        if i == 0:
            layers.put(message_ref, 3, 0, warmth)


def neighbours(n, own_rows, z, own_ref, same_ref, next_ref):
    layers = Layers(n, own_rows, z)
    even = lax.axis_index("gx") % 2 == 0

    def at(which, i):
        if 0 <= i < n:
            return layers.get(own_ref, which, i)
        same, other = (layers.get(ref, which, i % n) for ref in (same_ref, next_ref))
        return jnp.where(even, other, same) if i < 0 else jnp.where(even, same, other)

    return at


def basis_kernel(
    n, own_rows, layers, rows,
    own_ref, same_ref, next_ref,
    moments_ref, basis_ref, solid_ref,
    conduct_s, free_s, inverse_s, u0_s, u1_s,
):
    first_layer = lax.axis_index("gx") * n
    first_row = lax.axis_index("gy") * own_rows
    wide_rows = own_rows + 2 * WIDE
    near_rows = own_rows + 2 * NEAR
    z = own_ref.shape[-1]
    layer_at = neighbours(n, own_rows, z, own_ref, same_ref, next_ref)

    below, here = layer_at(0, -n), layer_at(0, 1 - n)
    for i in range(1 - n, 2 * n - 1):
        above = layer_at(0, i + 1)
        valid, weight = filter_weight(i, layers, first_layer, first_row - WIDE, rows, (wide_rows, z))
        solid = 1.0 - filtered(below, here, above) / weight
        below, here = here, above
        solid = solid[WIDE - NEAR : wide_rows - WIDE + NEAR]
        valid = valid[WIDE - NEAR : wide_rows - WIDE + NEAR]
        conduct_s[i + n - 1] = jnp.where(valid > 0, KMIN + (1.0 - KMIN) * (solid * solid * solid), 0.0)
        if 0 <= i < n:
            solid_ref[i] = solid

    def conduct_at(i):
        return conduct_s[i + n - 1]

    def free_at(i):
        return free_s[i + n - 2]

    for i in range(2 - n, 2 * n - 1):
        pair = conduct_at(i) + conduct_at(i - 1)
        pair = pair + down(pair, 0)
        pair = pair + lower_z(pair)
        free = layer_at(1, i)
        inverse = 1.0 / (free * (pair * (1.0 / 3.0)) + (1.0 - free))
        free_s[i + n - 2] = free
        inverse_s[i + n - 2] = inverse
        u0_s[i + n - 2] = layer_at(2, i) * inverse

    row = lax.broadcasted_iota(jnp.int32, (near_rows, z), 0)
    own = (row >= NEAR) & (row < NEAR + own_rows)
    sums = [jnp.zeros((8, 128), jnp.float32) for _ in range(MOMENTS)]

    def gather(which, product):
        sums[which] = sums[which] + tile_sum(jnp.where(own, product, 0.0))

    def step(previous, first, count):
        for i, image in apply_layers(lambda i: free_at(i) * previous(i), conduct_at, first, count):
            free, start = free_at(i), previous(i)
            image = free * image + (1.0 - free) * start
            yield i, start, image, image * inverse_s[i + n - 2] - start

    for i, start, image, later in step(lambda i: u0_s[i + n - 2], 3 - n, 3 * n - 5):
        u1_s[i + n - 3] = later
        if 0 <= i <= n:
            basis_ref[0, i] = start
        if 0 <= i < n:
            rhs = layer_at(2, i)
            gather(0, start * image)
            gather(1, later * image)
            gather(5, rhs * start)
            gather(6, rhs * later)
    for i, start, image, later in step(lambda i: u1_s[i + n - 3], 0, n + 1):
        basis_ref[1, i] = start
        basis_ref[2, i] = later
        if i < n:
            gather(2, start * image)
            gather(3, later * image)
            gather(7, layer_at(2, i) * later)
    low = yz_modes(free_at(0) * basis_ref[2, 0])
    for i in range(n):
        high = yz_modes(free_at(i + 1) * basis_ref[2, i + 1])
        square = sum(order * value * value for order, value in element_modes(low, high).values())
        last = basis_ref[2, i]
        gather(4, square * (conduct_at(i) * (1.0 / 48.0)) + (1.0 - free_at(i)) * last * last)
        low = high

    lane = lax.broadcasted_iota(jnp.int32, (1, 128), 1)
    total = jnp.zeros((1, 128), jnp.float32)
    for k in range(MOMENTS):
        total = total + jnp.where(lane == k, jnp.sum(sums[k], axis=(0, 1), keepdims=True), 0.0)
    moments_ref[...] = jnp.broadcast_to(total, moments_ref.shape)


def integrand_kernel(
    n, own_rows, layers, rows,
    basis_ref, solid_ref, warmth_ref, same_ref, next_ref,
    scaled_ref, to_same_ref, to_next_ref,
):
    even = lax.axis_index("gx") % 2 == 0
    first_layer = lax.axis_index("gx") * n
    first_row = lax.axis_index("gy") * own_rows
    shape = solid_ref.shape[1:]
    places = Layers(n, own_rows, shape[1])
    warm_low = yz_modes(warmth_ref[0])
    lows = [yz_modes(basis_ref[k, 0]) for k in range(BASIS)]
    for i in range(n):
        if i + 1 < n:
            warm = warmth_ref[i + 1]
        else:
            warm = jnp.where(even, places.get(same_ref, 3, 0), places.get(next_ref, 3, 0))
        warm_high = yz_modes(warm)
        valid, weight = filter_weight(i, layers, first_layer, first_row - NEAR, rows, shape)
        solid = solid_ref[i]
        share = jnp.where(valid > 0, 3.0 * solid * solid / weight, 0.0)
        load = {
            key: (order / 48.0) * value for key, (order, value) in element_modes(warm_low, warm_high).items()
        }
        for k in range(BASIS):
            high = yz_modes(basis_ref[k, i + 1])
            modes = element_modes(lows[k], high)
            energy = sum(load[key] * value for key, (_, value) in modes.items())
            total = lows[k][0] + high[0]
            scaled_ref[k, i] = share * ((1.0 - KMIN) * energy - (QZERO / 8.0) * total)
            lows[k] = high
        warm_low = warm_high
    for k in range(BASIS):
        first, last = scaled_ref[k, 0], scaled_ref[k, n - 1]
        to_same_ref[k] = jnp.where(even, last, first)
        to_next_ref[k] = jnp.where(even, first, last)


def spread_kernel(moments_ref, total_ref):
    total = jnp.sum(moments_ref[...], axis=0, keepdims=True)
    total_ref[...] = jnp.broadcast_to(total, total_ref.shape)


def solve_kernel(moments_ref, coefs_ref):
    total = jnp.sum(moments_ref[...], axis=0, keepdims=True)
    a0, a1, a2, a3, a4, b0, b1, b2 = (
        jnp.broadcast_to(total[:, k : k + 1], (1, 128)) for k in range(MOMENTS)
    )
    l10 = a1 / a0
    l20 = a2 / a0
    d1 = a2 - l10 * a1
    t21 = a3 - l20 * a1
    l21 = t21 / d1
    d2 = a4 - l20 * a2 - l21 * t21
    z1 = b1 - l10 * b0
    z2 = b2 - l20 * b0 - l21 * z1
    y2 = z2 / d2
    y1 = z1 / d1 - l21 * y2
    y0 = b0 / a0 - l10 * y1 - l20 * y2
    for k, y in enumerate((y0, y1, y2)):
        coefs_ref[k] = jnp.broadcast_to(y, coefs_ref.shape[1:])


def final_kernel(n, own_rows, coefs_ref, basis_ref, scaled_ref, same_ref, next_ref, dual_ref, sens_ref):
    even = lax.axis_index("gx") % 2 == 0
    z = dual_ref.shape[-1]
    near_rows = own_rows + 2 * NEAR
    coefs = [
        jnp.broadcast_to(jnp.concatenate([coefs_ref[k, :1]] * (z // 128), axis=1), (near_rows, z))
        for k in range(BASIS)
    ]

    def combined(layers):
        return sum(coef * layer for coef, layer in zip(coefs, layers))

    for i in range(n):
        dual_ref[i] = combined([basis_ref[k, i] for k in range(BASIS)])[NEAR : NEAR + own_rows]
    same = combined([same_ref[k] for k in range(BASIS)])
    other = combined([next_ref[k] for k in range(BASIS)])
    layers = [combined([scaled_ref[k, i] for k in range(BASIS)]) for i in range(n)]
    layers = [jnp.where(even, other, same)] + layers + [jnp.where(even, same, other)]
    for i in range(n):
        sens_ref[i] = filtered(*layers[i : i + 3])[NEAR : NEAR + own_rows]


def shifted(arr, axis, step):
    count = lax.axis_size(axis)
    return lax.ppermute(arr, axis, [(i, i + step) for i in range(count) if 0 <= i + step < count])


def swapped(arr, axis, start):
    pairs = [(i, i + 1) for i in range(start, lax.axis_size(axis) - 1, 2)]
    return lax.ppermute(arr, axis, pairs + [(j, i) for i, j in pairs])


def body(gx, gy, material_fraction, primal_warmth, empty_region_flags, dirichlet_flags):
    n, own_rows, z = material_fraction.shape
    sizes = (n, own_rows, gx * n, gy * own_rows)
    near = own_rows + 2 * NEAR

    def call(name, kernel, outs, *operands, scratch=(), space=pltpu.VMEM, limit=VMEM_LIMIT, flops=0):
        return pl.pallas_call(
            kernel,
            out_shape=[jax.ShapeDtypeStruct(shape, jnp.float32) for shape in outs],
            in_specs=[pl.BlockSpec(memory_space=space)] * len(operands),
            out_specs=[pl.BlockSpec(memory_space=pltpu.VMEM)] * len(outs),
            scratch_shapes=list(scratch),
            compiler_params=pltpu.CompilerParams(vmem_limit_bytes=limit),
            cost_estimate=pl.CostEstimate(flops=flops, bytes_accessed=1 << 20, transcendentals=0),
            name=name,
        )(*operands)

    def floats(*shape):
        return pltpu.VMEM(shape, jnp.float32)

    brick_shape = (n, own_rows, z)
    *own, y_up, y_down = call(
        "load",
        functools.partial(load_kernel, n),
        [brick_shape] * 4 + [(2 * n, 8, z)] * 2,
        material_fraction, primal_warmth, empty_region_flags, dirichlet_flags,
        scratch=[
            floats(*brick_shape),
            pltpu.VMEM(brick_shape, jnp.int32),
            pltpu.VMEM(brick_shape, jnp.int32),
            pltpu.SemaphoreType.DMA((4,)),
        ],
        space=pltpu.HBM,
        limit=LOAD_LIMIT,
    )
    y_low = shifted(y_up, "gy", 1)
    y_high = shifted(y_down, "gy", -1)
    places = Layers(n, own_rows, z)
    message, warmth = call(
        "extend",
        functools.partial(extend_kernel, n, own_rows),
        [(places.tiles, 8, z), (n, near, z)],
        *own, y_low, y_high,
    )
    same, other = swapped(message, "gx", 0), swapped(message, "gx", 1)

    pairs = 2 if gx % 2 == 0 else 1
    inner, outer = pairs * gy, gx // pairs
    moments, basis, solid = call(
        "basis",
        functools.partial(basis_kernel, *sizes),
        [(inner, 128), (BASIS, n + 1, near, z), (n, near, z)],
        message, same, other,
        scratch=[floats(count, near, z) for count in (3 * n - 2, 3 * n - 3, 3 * n - 3, 3 * n - 3, 3 * n - 5)],
    )
    scaled, to_same, to_next = call(
        "integrand",
        functools.partial(integrand_kernel, *sizes),
        [(BASIS, n, near, z), (BASIS, near, z), (BASIS, near, z)],
        basis, solid, warmth, same, other,
    )

    near_groups = [
        [(g * pairs + c) * gy + y for c in range(pairs) for y in range(gy)] for g in range(outer)
    ]
    far_groups = [
        [(g * pairs + c) * gy + y for g in range(outer)] for c in range(pairs) for y in range(gy)
    ]
    moments = lax.all_to_all(moments, ("gx", "gy"), 0, 0, axis_index_groups=near_groups, tiled=True)
    (moments,) = call("spread", spread_kernel, [(outer, 128)], moments, flops=FAR_WORK)
    from_same, from_next = swapped(to_same, "gx", 0), swapped(to_next, "gx", 1)
    moments = lax.all_to_all(moments, ("gx", "gy"), 0, 0, axis_index_groups=far_groups, tiled=True)
    (coefs,) = call("solve", solve_kernel, [(BASIS, 8, 128)], moments, flops=1000)
    return tuple(
        call(
            "combine",
            functools.partial(final_kernel, n, own_rows),
            [brick_shape, brick_shape],
            coefs, basis, scaled, from_same, from_next,
        )
    )


def solution(mesh):
    placed = P("gx", "gy", None)
    return jax.shard_map(
        functools.partial(body, mesh.shape["gx"], mesh.shape["gy"]),
        mesh=mesh,
        in_specs=(placed,) * 4,
        out_specs=(placed, placed),
        check_vma=False,
    )
```

time: 69.7 us -> 62 us (0.89)
  waiting for transfers between devices: 16.9 us -> 6.23 us
  blocking collectives: 14.8 us -> 23 us
  starting transfers between devices: 31.1 us -> 26.6 us
    ppermute x0 -> x4, starting transfers between devices: none -> 13.8 us  [swapped(): return lax.ppermute(arr, axis, pairs + [(j, i) for i, j in pairs])]
    ppermute x6 -> x2, starting transfers between devices: 17 us -> 5.33 us  [shifted(): lax.ppermute(arr, axis, [(i, i + step) for i in range(count) if 0 <= i +...]
    all_to_all x1, waiting for transfers between devices: 9.79 us -> 0.28 us  [body(): lax.all_to_all(moments, ('gx', 'gy'), 0, 0, axis_index_groups=near_groups...]
    all_to_all x1, blocking collectives: 14.8 us -> 23 us  [body(): lax.all_to_all(moments, ('gx', 'gy'), 0, 0, axis_index_groups=far_groups,...]
    all_to_all x1, starting transfers between devices: 14.1 us -> 7.43 us  [body(): lax.all_to_all(moments, ('gx', 'gy'), 0, 0, axis_index_groups=near_groups...]
    ppermute x6 -> x2, waiting for transfers between devices: 7.07 us -> 3.71 us  [shifted(): lax.ppermute(arr, axis, [(i, i + step) for i in range(count) if 0 <= i +...]
    ppermute x0 -> x4, waiting for transfers between devices: none -> 2.24 us  [swapped(): return lax.ppermute(arr, axis, pairs + [(j, i) for i, j in pairs])]
    pallas_call x5 -> x7, Pallas kernels: 5.12 us -> 5.04 us  [call(): pl.pallas_call(kernel, out_shape=[jax.ShapeDtypeStruct(shape, jnp.float32...]
  transfers between devices with their start and end apart: 7 -> 7, of which waited for: 4 -> 3; matrix products, arithmetic and copies ran while one was open for 0% -> 0% of each run, Pallas kernels for 2% -> 1%
where the time goes in v5:
time: 62 us; the launch traced here: 61.6 us
  starting transfers between devices  26.6 us (43%)
  blocking collectives  23 us (37%)
  waiting for transfers between devices  6.23 us (10%)
  Pallas kernels  5.04 us (8%)
  between operations  0.72 us (1%)
    all_to_all x1, blocking collectives, body(): lax.all_to_all(moments, ('gx', 'gy'), 0, 0, axis_index_groups=far_groups,...  23 us
    ppermute x4, starting transfers between devices, swapped(): return lax.ppermute(arr, axis, pairs + [(j, i) for i, j in pairs])  13.8 us
    all_to_all x1, starting transfers between devices, body(): lax.all_to_all(moments, ('gx', 'gy'), 0, 0, axis_index_groups=near_groups...  7.43 us
    ppermute x2, starting transfers between devices, shifted(): lax.ppermute(arr, axis, [(i, i + step) for i in range(count) if 0 <= i +...  5.33 us
    pallas_call x7, Pallas kernels, call(): pl.pallas_call(kernel, out_shape=[jax.ShapeDtypeStruct(shape, jnp.float32...  5.04 us
    ppermute x2, waiting for transfers between devices, shifted(): lax.ppermute(arr, axis, [(i, i + step) for i in range(count) if 0 <= i +...  3.71 us
    ppermute x4, waiting for transfers between devices, swapped(): return lax.ppermute(arr, axis, pairs + [(j, i) for i, j in pairs])  2.24 us
  transfers between devices with their start and end apart: 7, of which 3 were waited for; matrix products, arithmetic and copies ran while one was open for 0% of the time, Pallas kernels for 1%

profile of v5, /device:TPU:1, one launch (start us, length us, event | category | flops | bytes accessed | tf_op | source)
XLA Modules:
  0.0 61.6 jit_solution(15691295252697112111)
XLA Ops:
  0.6 1.0 %load.1 = (f32[4,16,256]{2,1,0:T(8,128)S(1)}, f32[4,16,256]{2,1,0:T(8,128)S(1)}, f32[4,16,256]{2,1,0:T(8,128)S(1)}, f32[4,16,256]{2,1,0:T(8,128)S(1)}, f32[8,8,2...) custom-call(f32[4,16,256]{2,1,0:T(8,128)} %material_hbm.1, f32[4,16,256]{2,1,0:T(8,128)} %primal_hbm.1, ...), custom_call_target="tpu_custom_call" | custom-call | bytes 1048576 | tf_op jit(solution)/shard_map/load/pallas_call | solution.py:418
  1.6 4.0 %collective-permute-start = (f32[8,8,256]{2,1,0:T(8,128)S(1)}, f32[8,8,256]{2,1,0:T(8,128)S(1)}, u32[]{:S(2)}, u32[]{:S(2)}) collective-permute-start(f32[8,8,256]{2,1,0:T(8,128)S(1)} %get-tuple-element.20), channel_id=1, source_target_pairs={{0,1},{1,2},{2,3},{3,4},{4,5},{5,6},{6,7},{8,9},{9,10},{10,11},{11... | collective-permute-start | bytes 196616 | tf_op jit(solution)/shard_map/ppermute | solution.py:404
  5.7 1.3 %collective-permute-start.1 = (f32[8,8,256]{2,1,0:T(8,128)S(1)}, f32[8,8,256]{2,1,0:T(8,128)S(1)}, u32[]{:S(2)}, u32[]{:S(2)}) collective-permute-start(f32[8,8,256]{2,1,0:T(8,128)S(1)} %get-tuple-element.21), channel_id=1, source_target_pairs={{1,0},{2,1},{3,2},{4,3},{5,4},{6,5},{7,6},{9,8},{10,9},{11,10},{12... | collective-permute-start | bytes 196616 | tf_op jit(solution)/shard_map/ppermute | solution.py:404
  7.0 0.0 collective-permute-done.low_ref
  7.0 3.7 %collective-permute-done.1.high_ref = f32[8,8,256]{2,1,0:T(8,128)S(1)} collective-permute-done((f32[8,8,256]{2,1,0:T(8,128)S(1)}, f32[8,8,256]{2,1,0:T(8,128)S(1)}, u32[]{:S(2)}, u32[]{:S(2)}) %collective-permute-start.1) | collective-permute-done | bytes 65568 | tf_op jit(solution)/shard_map/ppermute | solution.py:404
  10.7 5.1 %collective-permute-start.3 = (f32[43,8,256]{2,1,0:T(8,128)S(1)}, f32[43,8,256]{2,1,0:T(8,128)S(1)}, u32[]{:S(2)}, u32[]{:S(2)}) collective-permute-start(f32[43,8,256]{2,1,0:T(8,128)S(1)} %get-tuple-element.22.own_ref), channel_id=1, source_target_pairs={{8,16},{24,32},{40,48},{56,64},{72,80},{88,96},{104,112},{120,128}... | collective-permute-start | bytes 1056776 | tf_op jit(solution)/shard_map/ppermute | solution.py:409
  15.8 2.8 %collective-permute-start.2 = (f32[43,8,256]{2,1,0:T(8,128)S(1)}, f32[43,8,256]{2,1,0:T(8,128)S(1)}, u32[]{:S(2)}, u32[]{:S(2)}) collective-permute-start(f32[43,8,256]{2,1,0:T(8,128)S(1)} %get-tuple-element.22.own_ref), channel_id=1, source_target_pairs={{0,8},{16,24},{32,40},{48,56},{64,72},{80,88},{96,104},{112,120},{... | collective-permute-start | bytes 1056776 | tf_op jit(solution)/shard_map/ppermute | solution.py:409
  18.6 2.2 %collective-permute-done.3.next_ref = f32[43,8,256]{2,1,0:T(8,128)S(1)} collective-permute-done((f32[43,8,256]{2,1,0:T(8,128)S(1)}, f32[43,8,256]{2,1,0:T(8,128)S(1)}, u32[]{:S(2)}, u32[]{:S(2)}) %collective-permute-start.3) | collective-permute-done | bytes 352288 | tf_op jit(solution)/shard_map/ppermute | solution.py:409
  20.8 0.0 collective-permute-done.2.same_ref
  20.8 2.5 %basis.1 = (f32[16,128]{1,0:T(8,128)}, f32[3,5,24,256]{3,2,1,0:T(8,128)S(1)}, f32[4,24,256]{2,1,0:T(8,128)S(1)}) custom-call(f32[43,8,256]{2,1,0:T(8,128)S(1)} %get-tuple-element.22.own_ref, f32[43,8,256]{2,1,0:T(8,128)S(1)} %collective-permute-done.2.same_ref, f32[43,8,256]{2,1,0:T(8,128)S(1)} %collective-permute-done.3.next_ref), custom_call_target="tpu_custom_call" | custom-call | bytes 1048576 | tf_op jit(solution)/shard_map/basis/pallas_call | solution.py:418
  23.3 7.4 %all-to-all-start = ((f32[16,1,128]{2,1,0:T(1,128)}), f32[16,1,128]{2,1,0:T(1,128)S(1)}, u32[]{:S(2)}, u32[]{:S(2)}) async-start(f32[16,1,128]{2,1,0:T(1,128)} %bitcast.1), calls=%async_computation | async-start | bytes 16384 | tf_op jit(solution)/shard_map/all_to_all | solution.py:480
  30.8 0.6 %integrand.1 = (f32[3,4,24,256]{3,2,1,0:T(8,128)S(1)}, f32[3,24,256]{2,1,0:T(8,128)S(1)}, f32[3,24,256]{2,1,0:T(8,128)S(1)}) custom-call(f32[3,5,24,256]{3,2,1,0:T(8,128)S(1)} %get-tuple-element.24.basis_ref, f32[4,24,256]{2,1,0:T(8,128)S(1)} %get-tuple-element.25.solid_ref, f32[4,24,256]{2,1,0:T(8,128)S(1)} %get-tuple-element.26.warmth_ref, ...), custom_call_target="tpu_custom_call" | custom-call | bytes 1048576 | tf_op jit(solution)/shard_map/integrand/pallas_call | solution.py:418
  31.4 2.0 %collective-permute-start.4 = (f32[3,24,256]{2,1,0:T(8,128)S(1)}, f32[3,24,256]{2,1,0:T(8,128)S(1)}, u32[]{:S(2)}, u32[]{:S(2)}) collective-permute-start(f32[3,24,256]{2,1,0:T(8,128)S(1)} %get-tuple-element.28), channel_id=1, source_target_pairs={{0,8},{16,24},{32,40},{48,56},{64,72},{80,88},{96,104},{112,120},{... | collective-permute-start | bytes 221192 | tf_op jit(solution)/shard_map/ppermute | solution.py:409
  33.4 3.9 %collective-permute-start.5 = (f32[3,24,256]{2,1,0:T(8,128)S(1)}, f32[3,24,256]{2,1,0:T(8,128)S(1)}, u32[]{:S(2)}, u32[]{:S(2)}) collective-permute-start(f32[3,24,256]{2,1,0:T(8,128)S(1)} %get-tuple-element.29), channel_id=1, source_target_pairs={{8,16},{24,32},{40,48},{56,64},{72,80},{88,96},{104,112},{120,128}... | collective-permute-start | bytes 221192 | tf_op jit(solution)/shard_map/ppermute | solution.py:409
  37.4 0.3 all-to-all-done
  37.7 23.0 %all_to_all.22 = f32[32,1,128]{2,1,0:T(1,128)S(1)} all-to-all(f32[32,1,128]{2,1,0:T(1,128)S(1)} %bitcast.9), channel_id=1, replica_groups={{0,16,32,48,64,80,96,112,128,144,160,176,192,208,224,240,256,272,288,30..., dimensions={0} | all-to-all | bytes 32768 | tf_op jit(solution)/shard_map/all_to_all | solution.py:483
  60.7 0.1 solve.1.coefs_ref
  60.8 0.0 collective-permute-done.4.same_ref
  60.8 0.0 collective-permute-done.5.next_ref
  60.8 0.8 %combine.1 = (f32[4,16,256]{2,1,0:T(8,128)}, f32[4,16,256]{2,1,0:T(8,128)}) custom-call(f32[3,8,128]{2,1,0:T(8,128)S(1)} %solve.1.coefs_ref, f32[3,5,24,256]{3,2,1,0:T(8,128)S(1)} %get-tuple-element.24.basis_ref, f32[3,4,24,256]{3,2,1,0:T(8,128)S(1)} %get-tuple-element.27.scaled_ref, f32[3,24,256]{2,1,0:T(8,128)S(1)} %collective-permute-done.4.same_ref, ...), custom_call_target="tpu_custom_call" | custom-call | bytes 1048576 | tf_op jit(solution)/shard_map/combine/pallas_call | solution.py:418
  (2 shorter events, 0.0 us)
Async XLA Ops:
  1.6 5.4 %collective-permute-start = (f32[8,8,256]{2,1,0:T(8,128)S(1)}, f32[8,8,256]{2,1,0:T(8,128)S(1)}, u32[]{:S(2)}, u32[]{:S(2)}) collective-permute-start(f32[8,8,256]{2,1,0:T(8,128)S(1)} %get-tuple-element.20), channel_id=1, source_target_pairs={{0,1},{1,2},{2,3},{3,4},{4,5},{5,6},{6,7},{8,9},{9,10},{10,11},{11... | collective-permute-start | bytes 196616 | tf_op jit(solution)/shard_map/ppermute | solution.py:404
  5.7 5.0 %collective-permute-start.1 = (f32[8,8,256]{2,1,0:T(8,128)S(1)}, f32[8,8,256]{2,1,0:T(8,128)S(1)}, u32[]{:S(2)}, u32[]{:S(2)}) collective-permute-start(f32[8,8,256]{2,1,0:T(8,128)S(1)} %get-tuple-element.21), channel_id=1, source_target_pairs={{1,0},{2,1},{3,2},{4,3},{5,4},{6,5},{7,6},{9,8},{10,9},{11,10},{12... | collective-permute-start | bytes 196616 | tf_op jit(solution)/shard_map/ppermute | solution.py:404
  10.7 10.1 %collective-permute-start.3 = (f32[43,8,256]{2,1,0:T(8,128)S(1)}, f32[43,8,256]{2,1,0:T(8,128)S(1)}, u32[]{:S(2)}, u32[]{:S(2)}) collective-permute-start(f32[43,8,256]{2,1,0:T(8,128)S(1)} %get-tuple-element.22.own_ref), channel_id=1, source_target_pairs={{8,16},{24,32},{40,48},{56,64},{72,80},{88,96},{104,112},{120,128}... | collective-permute-start | bytes 1056776 | tf_op jit(solution)/shard_map/ppermute | solution.py:409
  15.8 5.0 %collective-permute-start.2 = (f32[43,8,256]{2,1,0:T(8,128)S(1)}, f32[43,8,256]{2,1,0:T(8,128)S(1)}, u32[]{:S(2)}, u32[]{:S(2)}) collective-permute-start(f32[43,8,256]{2,1,0:T(8,128)S(1)} %get-tuple-element.22.own_ref), channel_id=1, source_target_pairs={{0,8},{16,24},{32,40},{48,56},{64,72},{80,88},{96,104},{112,120},{... | collective-permute-start | bytes 1056776 | tf_op jit(solution)/shard_map/ppermute | solution.py:409
  23.3 14.3 %all-to-all-start = ((f32[16,1,128]{2,1,0:T(1,128)}), f32[16,1,128]{2,1,0:T(1,128)S(1)}, u32[]{:S(2)}, u32[]{:S(2)}) async-start(f32[16,1,128]{2,1,0:T(1,128)} %bitcast.1), calls=%async_computation | async-start | bytes 16384 | tf_op jit(solution)/shard_map/all_to_all | solution.py:480
  31.4 29.4 %collective-permute-start.4 = (f32[3,24,256]{2,1,0:T(8,128)S(1)}, f32[3,24,256]{2,1,0:T(8,128)S(1)}, u32[]{:S(2)}, u32[]{:S(2)}) collective-permute-start(f32[3,24,256]{2,1,0:T(8,128)S(1)} %get-tuple-element.28), channel_id=1, source_target_pairs={{0,8},{16,24},{32,40},{48,56},{64,72},{80,88},{96,104},{112,120},{... | collective-permute-start | bytes 221192 | tf_op jit(solution)/shard_map/ppermute | solution.py:409
  33.4 27.4 %collective-permute-start.5 = (f32[3,24,256]{2,1,0:T(8,128)S(1)}, f32[3,24,256]{2,1,0:T(8,128)S(1)}, u32[]{:S(2)}, u32[]{:S(2)}) collective-permute-start(f32[3,24,256]{2,1,0:T(8,128)S(1)} %get-tuple-element.29), channel_id=1, source_target_pairs={{8,16},{24,32},{40,48},{56,64},{72,80},{88,96},{104,112},{120,128}... | collective-permute-start | bytes 221192 | tf_op jit(solution)/shard_map/ppermute | solution.py:409

commit v6 on v5

--- a/solution.py
+++ b/solution.py
@@ -42,38 +42,43 @@
     return jnp.where(z_index(arr) == 0, 0.0, down(arr, 1))
 
 
+def with_rim(layer):
+    return layer, up(layer, 0) + down(layer, 0)
+
+
 def filtered(below, here, above):
-    beside = below + above
-    rim = up(here, 0) + down(here, 0)
-    corner = up(beside, 0) + down(beside, 0)
-    flat = 1.5 * here + EDGE * (beside + rim) + DIAGONAL * corner
-    slanted = EDGE * here + DIAGONAL * (beside + rim)
+    beside = below[0] + above[0]
+    around = beside + here[1]
+    flat = 1.5 * here[0] + EDGE * around + DIAGONAL * (below[1] + above[1])
+    slanted = EDGE * here[0] + DIAGONAL * around
     return flat + lift(slanted) + lower_z(slanted)
 
 
-def grid_flags(layer, layers, first_layer, first_row, rows, shape):
-    def inside(at):
-        return ((at >= 0) & (at < layers)).astype(jnp.float32)
-
-    at = first_layer + layer
+def layer_inside(at, layers):
+    return ((at >= 0) & (at < layers)).astype(jnp.float32)
+
+
+def row_inside(first_row, rows, shape):
     row = first_row + lax.broadcasted_iota(jnp.int32, shape, 0)
-
-    def row_inside(offset):
-        return ((row + offset >= 0) & (row + offset < rows)).astype(jnp.float32)
-
-    return inside(at), inside(at - 1) + inside(at + 1), row_inside(0), row_inside(-1) + row_inside(1)
-
-
-def filter_weight(layer, layers, first_layer, first_row, rows, shape):
-    here, beside, row_here, row_beside = grid_flags(
-        layer, layers, first_layer, first_row, rows, shape
-    )
+    return [((row + step >= 0) & (row + step < rows)).astype(jnp.float32) for step in (0, -1, 1)]
+
+
+def inverse_weights(first_row, rows, shape):
+    here, before, after = row_inside(first_row, rows, shape)
     z = lax.broadcasted_iota(jnp.int32, shape, 1)
     z_beside = (z > 0).astype(jnp.float32) + (z < shape[1] - 1).astype(jnp.float32)
-    flat = (1.5 + EDGE * beside) * row_here + (EDGE + DIAGONAL * beside) * row_beside
-    slanted = (EDGE + DIAGONAL * beside) * row_here + DIAGONAL * row_beside
-    valid = here * row_here
-    return valid, jnp.where(valid > 0, flat + z_beside * slanted, 1.0)
+    inverses = []
+    for beside in (2.0, 1.0):
+        flat = (1.5 + EDGE * beside) * here + (EDGE + DIAGONAL * beside) * (before + after)
+        slanted = (EDGE + DIAGONAL * beside) * here + DIAGONAL * (before + after)
+        weight = flat + z_beside * slanted
+        inverses.append(jnp.where(here > 0, 1.0 / jnp.where(here > 0, weight, 1.0), 0.0))
+    return here > 0, inverses
+
+
+def inverse_at(inverses, at, layers):
+    inner = (at > 0) & (at < layers - 1)
+    return jnp.where(inner, *inverses)
 
 
 def yz_modes(node):
@@ -176,11 +181,11 @@
     def __init__(self, n, own_rows, z):
         self.n, self.z = n, z
         self.wide, self.near = own_rows + 2 * WIDE, own_rows + 2 * NEAR
-        self.tiles = (n * self.wide + (2 * n + 1) * self.near) // 8
+        self.tiles = (n * self.wide + (2 * n - 1) * self.near) // 8
 
     def place(self, which, layer):
         rows = self.near if which else self.wide
-        start = layer * rows if which == 0 else self.n * self.wide + ((which - 1) * self.n + layer) * self.near
+        start = layer * rows if which == 0 else self.n * self.wide + ((which - 1) * (self.n - 1) + layer) * self.near
         return slice(start // 8, (start + rows) // 8), rows
 
     def put(self, ref, which, layer, value):
@@ -193,8 +198,10 @@
 
 
 def extend_kernel(
-    n, own_rows, design_in, free_in, rhs_in, warmth_in, low_ref, high_ref, message_ref, warmth_ref
+    n, own_rows, design_in, free_in, rhs_in, warmth_in, low_ref, high_ref,
+    free_ref, rhs_ref, warmth_ref, to_same_ref, to_next_ref,
 ):
+    even = lax.axis_index("gx") % 2 == 0
     layers = Layers(n, own_rows, design_in.shape[-1])
 
     def joined(low, middle, high):
@@ -203,26 +210,33 @@
     def near(low, middle, high):
         return joined(low, middle, high)[WIDE - NEAR : own_rows + WIDE + NEAR]
 
+    free, rhs = [], []
     for i in range(n):
-        layers.put(message_ref, 0, i, joined(low_ref[i], design_in[i], high_ref[i]))
-        layers.put(
-            message_ref, 1, i, near(roll_rows(low_ref[i], -3), free_in[i], roll_rows(high_ref[n + i], -4))
-        )
-        layers.put(message_ref, 2, i, near(low_ref[n + i], rhs_in[i], high_ref[n + i]))
+        design = joined(low_ref[i], design_in[i], high_ref[i])
+        layers.put(to_same_ref, 0, i, design)
+        layers.put(to_next_ref, 0, i, design)
+        free.append(near(roll_rows(low_ref[i], -3), free_in[i], roll_rows(high_ref[n + i], -4)))
+        rhs.append(near(low_ref[n + i], rhs_in[i], high_ref[n + i]))
         warmth = near(roll_rows(low_ref[n + i], -1), warmth_in[i], roll_rows(high_ref[i], -5))
-        warmth_ref[i] = warmth
+        free_ref[i], rhs_ref[i], warmth_ref[i] = free[i], rhs[i], warmth
         if i == 0:
-            layers.put(message_ref, 3, 0, warmth)
-
-
-def neighbours(n, own_rows, z, own_ref, same_ref, next_ref):
+            layers.put(to_same_ref, 3, 0, warmth)
+            layers.put(to_next_ref, 3, 0, warmth)
+    for which, values in ((1, free), (2, rhs)):
+        for i in range(n - 1):
+            layers.put(to_same_ref, which, i, jnp.where(even, values[i + 1], values[i]))
+            layers.put(to_next_ref, which, i, jnp.where(even, values[i], values[i + 1]))
+
+
+def neighbours(n, own_rows, z, own_ref, free_ref, rhs_ref, same_ref, next_ref):
     layers = Layers(n, own_rows, z)
     even = lax.axis_index("gx") % 2 == 0
 
     def at(which, i):
         if 0 <= i < n:
-            return layers.get(own_ref, which, i)
-        same, other = (layers.get(ref, which, i % n) for ref in (same_ref, next_ref))
+            return (free_ref, rhs_ref)[which - 1][i] if which else layers.get(own_ref, 0, i)
+        slot = i % n - (1 if which and i < 0 else 0)
+        same, other = (layers.get(ref, which, slot) for ref in (same_ref, next_ref))
         return jnp.where(even, other, same) if i < 0 else jnp.where(even, same, other)
 
     return at
@@ -230,26 +244,32 @@
 
 def basis_kernel(
     n, own_rows, layers, rows,
-    own_ref, same_ref, next_ref,
+    own_ref, free_ref, rhs_ref, same_ref, next_ref,
     moments_ref, basis_ref, solid_ref,
     conduct_s, free_s, inverse_s, u0_s, u1_s,
 ):
     first_layer = lax.axis_index("gx") * n
     first_row = lax.axis_index("gy") * own_rows
-    wide_rows = own_rows + 2 * WIDE
     near_rows = own_rows + 2 * NEAR
     z = own_ref.shape[-1]
-    layer_at = neighbours(n, own_rows, z, own_ref, same_ref, next_ref)
-
-    below, here = layer_at(0, -n), layer_at(0, 1 - n)
+    layer_at = neighbours(n, own_rows, z, own_ref, free_ref, rhs_ref, same_ref, next_ref)
+
+    def design_at(i):
+        layer = layer_at(0, i)
+        before, here, after = (
+            layer[WIDE - NEAR + step : WIDE - NEAR + step + near_rows] for step in (-1, 0, 1)
+        )
+        return here, before + after
+
+    valid, inverses = inverse_weights(first_row - NEAR, rows, (near_rows, z))
+    below, here = design_at(-n), design_at(1 - n)
     for i in range(1 - n, 2 * n - 1):
-        above = layer_at(0, i + 1)
-        valid, weight = filter_weight(i, layers, first_layer, first_row - WIDE, rows, (wide_rows, z))
-        solid = 1.0 - filtered(below, here, above) / weight
+        above = design_at(i + 1)
+        at = first_layer + i
+        solid = 1.0 - filtered(below, here, above) * inverse_at(inverses, at, layers)
         below, here = here, above
-        solid = solid[WIDE - NEAR : wide_rows - WIDE + NEAR]
-        valid = valid[WIDE - NEAR : wide_rows - WIDE + NEAR]
-        conduct_s[i + n - 1] = jnp.where(valid > 0, KMIN + (1.0 - KMIN) * (solid * solid * solid), 0.0)
+        conduct = KMIN + (1.0 - KMIN) * (solid * solid * solid)
+        conduct_s[i + n - 1] = jnp.where(valid & (at >= 0) & (at < layers), conduct, 0.0)
         if 0 <= i < n:
             solid_ref[i] = solid
 
@@ -307,10 +327,10 @@
         gather(4, square * (conduct_at(i) * (1.0 / 48.0)) + (1.0 - free_at(i)) * last * last)
         low = high
 
-    lane = lax.broadcasted_iota(jnp.int32, (1, 128), 1)
-    total = jnp.zeros((1, 128), jnp.float32)
-    for k in range(MOMENTS):
-        total = total + jnp.where(lane == k, jnp.sum(sums[k], axis=(0, 1), keepdims=True), 0.0)
+    table = jnp.concatenate([jnp.sum(partial, axis=0, keepdims=True) for partial in sums], axis=0)
+    column = jnp.sum(table, axis=1, keepdims=True)
+    diagonal = lax.broadcasted_iota(jnp.int32, (8, 128), 0) == lax.broadcasted_iota(jnp.int32, (8, 128), 1)
+    total = jnp.sum(jnp.where(diagonal, column, 0.0), axis=0, keepdims=True)
     moments_ref[...] = jnp.broadcast_to(total, moments_ref.shape)
 
 
@@ -324,6 +344,7 @@
     first_row = lax.axis_index("gy") * own_rows
     shape = solid_ref.shape[1:]
     places = Layers(n, own_rows, shape[1])
+    _, inverses = inverse_weights(first_row - NEAR, rows, shape)
     warm_low = yz_modes(warmth_ref[0])
     lows = [yz_modes(basis_ref[k, 0]) for k in range(BASIS)]
     for i in range(n):
@@ -332,9 +353,8 @@
         else:
             warm = jnp.where(even, places.get(same_ref, 3, 0), places.get(next_ref, 3, 0))
         warm_high = yz_modes(warm)
-        valid, weight = filter_weight(i, layers, first_layer, first_row - NEAR, rows, shape)
         solid = solid_ref[i]
-        share = jnp.where(valid > 0, 3.0 * solid * solid / weight, 0.0)
+        share = (3.0 * solid * solid) * inverse_at(inverses, first_layer + i, layers)
         load = {
             key: (order / 48.0) * value for key, (order, value) in element_modes(warm_low, warm_high).items()
         }
@@ -357,8 +377,7 @@
     total_ref[...] = jnp.broadcast_to(total, total_ref.shape)
 
 
-def solve_kernel(moments_ref, coefs_ref):
-    total = jnp.sum(moments_ref[...], axis=0, keepdims=True)
+def coefficients(total):
     a0, a1, a2, a3, a4, b0, b1, b2 = (
         jnp.broadcast_to(total[:, k : k + 1], (1, 128)) for k in range(MOMENTS)
     )
@@ -373,17 +392,16 @@
     y2 = z2 / d2
     y1 = z1 / d1 - l21 * y2
     y0 = b0 / a0 - l10 * y1 - l20 * y2
-    for k, y in enumerate((y0, y1, y2)):
-        coefs_ref[k] = jnp.broadcast_to(y, coefs_ref.shape[1:])
-
-
-def final_kernel(n, own_rows, coefs_ref, basis_ref, scaled_ref, same_ref, next_ref, dual_ref, sens_ref):
+    return y0, y1, y2
+
+
+def final_kernel(n, own_rows, moments_ref, basis_ref, scaled_ref, same_ref, next_ref, dual_ref, sens_ref):
     even = lax.axis_index("gx") % 2 == 0
     z = dual_ref.shape[-1]
     near_rows = own_rows + 2 * NEAR
     coefs = [
-        jnp.broadcast_to(jnp.concatenate([coefs_ref[k, :1]] * (z // 128), axis=1), (near_rows, z))
-        for k in range(BASIS)
+        jnp.broadcast_to(jnp.concatenate([y] * (z // 128), axis=1), (near_rows, z))
+        for y in coefficients(jnp.sum(moments_ref[...], axis=0, keepdims=True))
     ]
 
     def combined(layers):
@@ -395,6 +413,7 @@
     other = combined([next_ref[k] for k in range(BASIS)])
     layers = [combined([scaled_ref[k, i] for k in range(BASIS)]) for i in range(n)]
     layers = [jnp.where(even, other, same)] + layers + [jnp.where(even, same, other)]
+    layers = [with_rim(layer) for layer in layers]
     for i in range(n):
         sens_ref[i] = filtered(*layers[i : i + 3])[NEAR : NEAR + own_rows]
 
@@ -447,13 +466,13 @@
     y_low = shifted(y_up, "gy", 1)
     y_high = shifted(y_down, "gy", -1)
     places = Layers(n, own_rows, z)
-    message, warmth = call(
+    free, rhs, warmth, to_same, to_next = call(
         "extend",
         functools.partial(extend_kernel, n, own_rows),
-        [(places.tiles, 8, z), (n, near, z)],
+        [(n, near, z)] * 3 + [(places.tiles, 8, z)] * 2,
         *own, y_low, y_high,
     )
-    same, other = swapped(message, "gx", 0), swapped(message, "gx", 1)
+    same, other = swapped(to_same, "gx", 0), swapped(to_next, "gx", 1)
 
     pairs = 2 if gx % 2 == 0 else 1
     inner, outer = pairs * gy, gx // pairs
@@ -461,7 +480,7 @@
         "basis",
         functools.partial(basis_kernel, *sizes),
         [(inner, 128), (BASIS, n + 1, near, z), (n, near, z)],
-        message, same, other,
+        to_same, free, rhs, same, other,
         scratch=[floats(count, near, z) for count in (3 * n - 2, 3 * n - 3, 3 * n - 3, 3 * n - 3, 3 * n - 5)],
     )
     scaled, to_same, to_next = call(
@@ -481,13 +500,12 @@
     (moments,) = call("spread", spread_kernel, [(outer, 128)], moments, flops=FAR_WORK)
     from_same, from_next = swapped(to_same, "gx", 0), swapped(to_next, "gx", 1)
     moments = lax.all_to_all(moments, ("gx", "gy"), 0, 0, axis_index_groups=far_groups, tiled=True)
-    (coefs,) = call("solve", solve_kernel, [(BASIS, 8, 128)], moments, flops=1000)
     return tuple(
         call(
             "combine",
             functools.partial(final_kernel, n, own_rows),
             [brick_shape, brick_shape],
-            coefs, basis, scaled, from_same, from_next,
+            moments, basis, scaled, from_same, from_next,
         )
     )
 

time: 62 us -> 61.4 us (level)
    pallas_call x7 -> x6, Pallas kernels: 5.04 us -> 5.01 us  [call(): pl.pallas_call(kernel, out_shape=[jax.ShapeDtypeStruct(shape, jnp.float32...]
where the time goes in v6:
time: 61.4 us; the launch traced here: 61 us
  starting transfers between devices  26.6 us (43%)
  blocking collectives  23 us (37%)
  waiting for transfers between devices  5.72 us (9%)
  Pallas kernels  5.01 us (8%)
  between operations  0.7 us (1%)
    all_to_all x1, blocking collectives, body(): lax.all_to_all(moments, ('gx', 'gy'), 0, 0, axis_index_groups=far_groups,...  23 us
    ppermute x4, starting transfers between devices, swapped(): return lax.ppermute(arr, axis, pairs + [(j, i) for i, j in pairs])  13.8 us
    all_to_all x1, starting transfers between devices, body(): lax.all_to_all(moments, ('gx', 'gy'), 0, 0, axis_index_groups=near_groups...  7.43 us
    ppermute x2, starting transfers between devices, shifted(): lax.ppermute(arr, axis, [(i, i + step) for i in range(count) if 0 <= i +...  5.33 us
    pallas_call x6, Pallas kernels, call(): pl.pallas_call(kernel, out_shape=[jax.ShapeDtypeStruct(shape, jnp.float32...  5.01 us
    ppermute x2, waiting for transfers between devices, shifted(): lax.ppermute(arr, axis, [(i, i + step) for i in range(count) if 0 <= i +...  3.71 us
    ppermute x4, waiting for transfers between devices, swapped(): return lax.ppermute(arr, axis, pairs + [(j, i) for i, j in pairs])  1.71 us
  transfers between devices with their start and end apart: 7, of which 3 were waited for; matrix products, arithmetic and copies ran while one was open for 0% of the time, Pallas kernels for 1%

profile of v6, /device:TPU:1, one launch (start us, length us, event | category | flops | bytes accessed | tf_op | source)
XLA Modules:
  0.0 61.0 jit_solution(16661154102386726920)
XLA Ops:
  0.6 1.0 %load.1 = (f32[4,16,256]{2,1,0:T(8,128)S(1)}, f32[4,16,256]{2,1,0:T(8,128)S(1)}, f32[4,16,256]{2,1,0:T(8,128)S(1)}, f32[4,16,256]{2,1,0:T(8,128)S(1)}, f32[8,8,2...) custom-call(f32[4,16,256]{2,1,0:T(8,128)} %material_hbm.1, f32[4,16,256]{2,1,0:T(8,128)} %primal_hbm.1, ...), custom_call_target="tpu_custom_call" | custom-call | bytes 1048576 | tf_op jit(solution)/shard_map/load/pallas_call | solution.py:437
  1.6 4.0 %collective-permute-start = (f32[8,8,256]{2,1,0:T(8,128)S(1)}, f32[8,8,256]{2,1,0:T(8,128)S(1)}, u32[]{:S(2)}, u32[]{:S(2)}) collective-permute-start(f32[8,8,256]{2,1,0:T(8,128)S(1)} %get-tuple-element.23), channel_id=1, source_target_pairs={{0,1},{1,2},{2,3},{3,4},{4,5},{5,6},{6,7},{8,9},{9,10},{10,11},{11... | collective-permute-start | bytes 196616 | tf_op jit(solution)/shard_map/ppermute | solution.py:423
  5.7 1.3 %collective-permute-start.1 = (f32[8,8,256]{2,1,0:T(8,128)S(1)}, f32[8,8,256]{2,1,0:T(8,128)S(1)}, u32[]{:S(2)}, u32[]{:S(2)}) collective-permute-start(f32[8,8,256]{2,1,0:T(8,128)S(1)} %get-tuple-element.24), channel_id=1, source_target_pairs={{1,0},{2,1},{3,2},{4,3},{5,4},{6,5},{7,6},{9,8},{10,9},{11,10},{12... | collective-permute-start | bytes 196616 | tf_op jit(solution)/shard_map/ppermute | solution.py:423
  7.0 0.0 collective-permute-done.low_ref
  7.0 3.7 %collective-permute-done.1.high_ref = f32[8,8,256]{2,1,0:T(8,128)S(1)} collective-permute-done((f32[8,8,256]{2,1,0:T(8,128)S(1)}, f32[8,8,256]{2,1,0:T(8,128)S(1)}, u32[]{:S(2)}, u32[]{:S(2)}) %collective-permute-start.1) | collective-permute-done | bytes 65568 | tf_op jit(solution)/shard_map/ppermute | solution.py:423
  10.7 0.1 extend.1
  10.8 5.1 %collective-permute-start.3 = (f32[37,8,256]{2,1,0:T(8,128)S(1)}, f32[37,8,256]{2,1,0:T(8,128)S(1)}, u32[]{:S(2)}, u32[]{:S(2)}) collective-permute-start(f32[37,8,256]{2,1,0:T(8,128)S(1)} %get-tuple-element.28), channel_id=1, source_target_pairs={{8,16},{24,32},{40,48},{56,64},{72,80},{88,96},{104,112},{120,128}... | collective-permute-start | bytes 909320 | tf_op jit(solution)/shard_map/ppermute | solution.py:428
  15.9 2.8 %collective-permute-start.2 = (f32[37,8,256]{2,1,0:T(8,128)S(1)}, f32[37,8,256]{2,1,0:T(8,128)S(1)}, u32[]{:S(2)}, u32[]{:S(2)}) collective-permute-start(f32[37,8,256]{2,1,0:T(8,128)S(1)} %get-tuple-element.25.own_ref), channel_id=1, source_target_pairs={{0,8},{16,24},{32,40},{48,56},{64,72},{80,88},{96,104},{112,120},{... | collective-permute-start | bytes 909320 | tf_op jit(solution)/shard_map/ppermute | solution.py:428
  18.7 1.7 %collective-permute-done.3.next_ref = f32[37,8,256]{2,1,0:T(8,128)S(1)} collective-permute-done((f32[37,8,256]{2,1,0:T(8,128)S(1)}, f32[37,8,256]{2,1,0:T(8,128)S(1)}, u32[]{:S(2)}, u32[]{:S(2)}) %collective-permute-start.3) | collective-permute-done | bytes 303136 | tf_op jit(solution)/shard_map/ppermute | solution.py:428
  20.4 0.0 collective-permute-done.2.same_ref
  20.4 2.4 %basis.1 = (f32[16,128]{1,0:T(8,128)}, f32[3,5,24,256]{3,2,1,0:T(8,128)S(1)}, f32[4,24,256]{2,1,0:T(8,128)S(1)}) custom-call(f32[37,8,256]{2,1,0:T(8,128)S(1)} %get-tuple-element.25.own_ref, f32[4,24,256]{2,1,0:T(8,128)S(1)} %get-tuple-element.26.free_ref, f32[4,24,256]{2,1,0:T(8,128)S(1)} %get-tuple-element.27.rhs_ref, ...), custom_call_target="tpu_custom_call" | custom-call | bytes 1048576 | tf_op jit(solution)/shard_map/basis/pallas_call | solution.py:437
  22.8 7.4 %all-to-all-start = ((f32[16,1,128]{2,1,0:T(1,128)}), f32[16,1,128]{2,1,0:T(1,128)S(1)}, u32[]{:S(2)}, u32[]{:S(2)}) async-start(f32[16,1,128]{2,1,0:T(1,128)} %bitcast.1), calls=%async_computation | async-start | bytes 16384 | tf_op jit(solution)/shard_map/all_to_all | solution.py:499
  30.2 0.6 %integrand.1 = (f32[3,4,24,256]{3,2,1,0:T(8,128)S(1)}, f32[3,24,256]{2,1,0:T(8,128)S(1)}, f32[3,24,256]{2,1,0:T(8,128)S(1)}) custom-call(f32[3,5,24,256]{3,2,1,0:T(8,128)S(1)} %get-tuple-element.30.basis_ref, f32[4,24,256]{2,1,0:T(8,128)S(1)} %get-tuple-element.31.solid_ref, f32[4,24,256]{2,1,0:T(8,128)S(1)} %get-tuple-element.32.warmth_ref, ...), custom_call_target="tpu_custom_call" | custom-call | bytes 1048576 | tf_op jit(solution)/shard_map/integrand/pallas_call | solution.py:437
  30.8 2.0 %collective-permute-start.4 = (f32[3,24,256]{2,1,0:T(8,128)S(1)}, f32[3,24,256]{2,1,0:T(8,128)S(1)}, u32[]{:S(2)}, u32[]{:S(2)}) collective-permute-start(f32[3,24,256]{2,1,0:T(8,128)S(1)} %get-tuple-element.34), channel_id=1, source_target_pairs={{0,8},{16,24},{32,40},{48,56},{64,72},{80,88},{96,104},{112,120},{... | collective-permute-start | bytes 221192 | tf_op jit(solution)/shard_map/ppermute | solution.py:428
  32.9 3.9 %collective-permute-start.5 = (f32[3,24,256]{2,1,0:T(8,128)S(1)}, f32[3,24,256]{2,1,0:T(8,128)S(1)}, u32[]{:S(2)}, u32[]{:S(2)}) collective-permute-start(f32[3,24,256]{2,1,0:T(8,128)S(1)} %get-tuple-element.35), channel_id=1, source_target_pairs={{8,16},{24,32},{40,48},{56,64},{72,80},{88,96},{104,112},{120,128}... | collective-permute-start | bytes 221192 | tf_op jit(solution)/shard_map/ppermute | solution.py:428
  36.8 0.3 all-to-all-done
  37.1 23.0 %all_to_all.22 = f32[32,1,128]{2,1,0:T(1,128)S(1)} all-to-all(f32[32,1,128]{2,1,0:T(1,128)S(1)} %bitcast.9), channel_id=1, replica_groups={{0,16,32,48,64,80,96,112,128,144,160,176,192,208,224,240,256,272,288,30..., dimensions={0} | all-to-all | bytes 32768 | tf_op jit(solution)/shard_map/all_to_all | solution.py:502
  60.1 0.0 collective-permute-done.4.same_ref
  60.1 0.0 collective-permute-done.5.next_ref
  60.1 0.9 %combine.1 = (f32[4,16,256]{2,1,0:T(8,128)}, f32[4,16,256]{2,1,0:T(8,128)}) custom-call(f32[32,128]{1,0:T(8,128)S(1)} %bitcast.8, f32[3,5,24,256]{3,2,1,0:T(8,128)S(1)} %get-tuple-element.30.basis_ref, f32[3,4,24,256]{3,2,1,0:T(8,128)S(1)} %get-tuple-element.33.scaled_ref, f32[3,24,256]{2,1,0:T(8,128)S(1)} %collective-permute-done.4.same_ref, ...), custom_call_target="tpu_custom_call" | custom-call | bytes 1048576 | tf_op jit(solution)/shard_map/combine/pallas_call | solution.py:437
  (1 shorter events, 0.0 us)
Async XLA Ops:
  1.6 5.4 %collective-permute-start = (f32[8,8,256]{2,1,0:T(8,128)S(1)}, f32[8,8,256]{2,1,0:T(8,128)S(1)}, u32[]{:S(2)}, u32[]{:S(2)}) collective-permute-start(f32[8,8,256]{2,1,0:T(8,128)S(1)} %get-tuple-element.23), channel_id=1, source_target_pairs={{0,1},{1,2},{2,3},{3,4},{4,5},{5,6},{6,7},{8,9},{9,10},{10,11},{11... | collective-permute-start | bytes 196616 | tf_op jit(solution)/shard_map/ppermute | solution.py:423
  5.7 5.0 %collective-permute-start.1 = (f32[8,8,256]{2,1,0:T(8,128)S(1)}, f32[8,8,256]{2,1,0:T(8,128)S(1)}, u32[]{:S(2)}, u32[]{:S(2)}) collective-permute-start(f32[8,8,256]{2,1,0:T(8,128)S(1)} %get-tuple-element.24), channel_id=1, source_target_pairs={{1,0},{2,1},{3,2},{4,3},{5,4},{6,5},{7,6},{9,8},{10,9},{11,10},{12... | collective-permute-start | bytes 196616 | tf_op jit(solution)/shard_map/ppermute | solution.py:423
  10.8 9.6 %collective-permute-start.3 = (f32[37,8,256]{2,1,0:T(8,128)S(1)}, f32[37,8,256]{2,1,0:T(8,128)S(1)}, u32[]{:S(2)}, u32[]{:S(2)}) collective-permute-start(f32[37,8,256]{2,1,0:T(8,128)S(1)} %get-tuple-element.28), channel_id=1, source_target_pairs={{8,16},{24,32},{40,48},{56,64},{72,80},{88,96},{104,112},{120,128}... | collective-permute-start | bytes 909320 | tf_op jit(solution)/shard_map/ppermute | solution.py:428
  15.9 4.5 %collective-permute-start.2 = (f32[37,8,256]{2,1,0:T(8,128)S(1)}, f32[37,8,256]{2,1,0:T(8,128)S(1)}, u32[]{:S(2)}, u32[]{:S(2)}) collective-permute-start(f32[37,8,256]{2,1,0:T(8,128)S(1)} %get-tuple-element.25.own_ref), channel_id=1, source_target_pairs={{0,8},{16,24},{32,40},{48,56},{64,72},{80,88},{96,104},{112,120},{... | collective-permute-start | bytes 909320 | tf_op jit(solution)/shard_map/ppermute | solution.py:428
  22.8 14.3 %all-to-all-start = ((f32[16,1,128]{2,1,0:T(1,128)}), f32[16,1,128]{2,1,0:T(1,128)S(1)}, u32[]{:S(2)}, u32[]{:S(2)}) async-start(f32[16,1,128]{2,1,0:T(1,128)} %bitcast.1), calls=%async_computation | async-start | bytes 16384 | tf_op jit(solution)/shard_map/all_to_all | solution.py:499
  30.8 29.3 %collective-permute-start.4 = (f32[3,24,256]{2,1,0:T(8,128)S(1)}, f32[3,24,256]{2,1,0:T(8,128)S(1)}, u32[]{:S(2)}, u32[]{:S(2)}) collective-permute-start(f32[3,24,256]{2,1,0:T(8,128)S(1)} %get-tuple-element.34), channel_id=1, source_target_pairs={{0,8},{16,24},{32,40},{48,56},{64,72},{80,88},{96,104},{112,120},{... | collective-permute-start | bytes 221192 | tf_op jit(solution)/shard_map/ppermute | solution.py:428
  32.9 27.3 %collective-permute-start.5 = (f32[3,24,256]{2,1,0:T(8,128)S(1)}, f32[3,24,256]{2,1,0:T(8,128)S(1)}, u32[]{:S(2)}, u32[]{:S(2)}) collective-permute-start(f32[3,24,256]{2,1,0:T(8,128)S(1)} %get-tuple-element.35), channel_id=1, source_target_pairs={{8,16},{24,32},{40,48},{56,64},{72,80},{88,96},{104,112},{120,128}... | collective-permute-start | bytes 221192 | tf_op jit(solution)/shard_map/ppermute | solution.py:428

commit v7 on v6

--- a/solution.py
+++ b/solution.py
@@ -16,6 +16,7 @@
 WIDE = 8
 NEAR = 4
 BASIS = 3
+SPARE = 3
 MOMENTS = 8
 VMEM_LIMIT = 12 << 20
 FAR_WORK = 10**10
@@ -181,7 +182,7 @@
     def __init__(self, n, own_rows, z):
         self.n, self.z = n, z
         self.wide, self.near = own_rows + 2 * WIDE, own_rows + 2 * NEAR
-        self.tiles = (n * self.wide + (2 * n - 1) * self.near) // 8
+        self.tiles = (n * self.wide + (2 * n - 2) * self.near) // 8
 
     def place(self, which, layer):
         rows = self.near if which else self.wide
@@ -195,6 +196,18 @@
     def get(self, ref, which, layer):
         place, rows = self.place(which, layer)
         return ref[place].reshape(rows, self.z)
+
+
+def with_spare(design, carried):
+    return jnp.concatenate([carried[:SPARE], design[SPARE:-SPARE], carried[SPARE:]], axis=0)
+
+
+def spare_rows(layers, ref):
+    pieces = []
+    for i in range(layers.n):
+        design = layers.get(ref, 0, i)
+        pieces += [design[:SPARE], design[-SPARE:]]
+    return jnp.concatenate(pieces, axis=0)
 
 
 def extend_kernel(
@@ -212,16 +225,16 @@
 
     free, rhs = [], []
     for i in range(n):
-        design = joined(low_ref[i], design_in[i], high_ref[i])
-        layers.put(to_same_ref, 0, i, design)
-        layers.put(to_next_ref, 0, i, design)
         free.append(near(roll_rows(low_ref[i], -3), free_in[i], roll_rows(high_ref[n + i], -4)))
         rhs.append(near(low_ref[n + i], rhs_in[i], high_ref[n + i]))
         warmth = near(roll_rows(low_ref[n + i], -1), warmth_in[i], roll_rows(high_ref[i], -5))
         free_ref[i], rhs_ref[i], warmth_ref[i] = free[i], rhs[i], warmth
         if i == 0:
-            layers.put(to_same_ref, 3, 0, warmth)
-            layers.put(to_next_ref, 3, 0, warmth)
+            carried = warmth
+        design = joined(low_ref[i], design_in[i], high_ref[i])
+        design = with_spare(design, carried[2 * SPARE * i : 2 * SPARE * (i + 1)])
+        layers.put(to_same_ref, 0, i, design)
+        layers.put(to_next_ref, 0, i, design)
     for which, values in ((1, free), (2, rhs)):
         for i in range(n - 1):
             layers.put(to_same_ref, which, i, jnp.where(even, values[i + 1], values[i]))
@@ -351,7 +364,7 @@
         if i + 1 < n:
             warm = warmth_ref[i + 1]
         else:
-            warm = jnp.where(even, places.get(same_ref, 3, 0), places.get(next_ref, 3, 0))
+            warm = jnp.where(even, spare_rows(places, same_ref), spare_rows(places, next_ref))
         warm_high = yz_modes(warm)
         solid = solid_ref[i]
         share = (3.0 * solid * solid) * inverse_at(inverses, first_layer + i, layers)

time: 61.4 us -> 61.1 us (level)
  no operation moved by 1% of the time
where the time goes in v7:
time: 61.1 us; the launch traced here: 60.7 us
  starting transfers between devices  26.6 us (44%)
  blocking collectives  23 us (38%)
  waiting for transfers between devices  5.46 us (9%)
  Pallas kernels  5.01 us (8%)
  between operations  0.7 us (1%)
    all_to_all x1, blocking collectives, body(): lax.all_to_all(moments, ('gx', 'gy'), 0, 0, axis_index_groups=far_groups,...  23 us
    ppermute x4, starting transfers between devices, swapped(): return lax.ppermute(arr, axis, pairs + [(j, i) for i, j in pairs])  13.8 us
    all_to_all x1, starting transfers between devices, body(): lax.all_to_all(moments, ('gx', 'gy'), 0, 0, axis_index_groups=near_groups...  7.43 us
    ppermute x2, starting transfers between devices, shifted(): lax.ppermute(arr, axis, [(i, i + step) for i in range(count) if 0 <= i +...  5.33 us
    pallas_call x6, Pallas kernels, call(): pl.pallas_call(kernel, out_shape=[jax.ShapeDtypeStruct(shape, jnp.float32...  5.01 us
    ppermute x2, waiting for transfers between devices, shifted(): lax.ppermute(arr, axis, [(i, i + step) for i in range(count) if 0 <= i +...  3.71 us
    ppermute x4, waiting for transfers between devices, swapped(): return lax.ppermute(arr, axis, pairs + [(j, i) for i, j in pairs])  1.45 us
  transfers between devices with their start and end apart: 7, of which 3 were waited for; matrix products, arithmetic and copies ran while one was open for 0% of the time, Pallas kernels for 1%

profile of v7, /device:TPU:1, one launch (start us, length us, event | category | flops | bytes accessed | tf_op | source)
XLA Modules:
  0.0 60.7 jit_solution(10013883271150374126)
XLA Ops:
  0.6 1.0 %load.1 = (f32[4,16,256]{2,1,0:T(8,128)S(1)}, f32[4,16,256]{2,1,0:T(8,128)S(1)}, f32[4,16,256]{2,1,0:T(8,128)S(1)}, f32[4,16,256]{2,1,0:T(8,128)S(1)}, f32[8,8,2...) custom-call(f32[4,16,256]{2,1,0:T(8,128)} %material_hbm.1, f32[4,16,256]{2,1,0:T(8,128)} %primal_hbm.1, ...), custom_call_target="tpu_custom_call" | custom-call | bytes 1048576 | tf_op jit(solution)/shard_map/load/pallas_call | solution.py:450
  1.6 4.0 %collective-permute-start = (f32[8,8,256]{2,1,0:T(8,128)S(1)}, f32[8,8,256]{2,1,0:T(8,128)S(1)}, u32[]{:S(2)}, u32[]{:S(2)}) collective-permute-start(f32[8,8,256]{2,1,0:T(8,128)S(1)} %get-tuple-element.23), channel_id=1, source_target_pairs={{0,1},{1,2},{2,3},{3,4},{4,5},{5,6},{6,7},{8,9},{9,10},{10,11},{11... | collective-permute-start | bytes 196616 | tf_op jit(solution)/shard_map/ppermute | solution.py:436
  5.7 1.3 %collective-permute-start.1 = (f32[8,8,256]{2,1,0:T(8,128)S(1)}, f32[8,8,256]{2,1,0:T(8,128)S(1)}, u32[]{:S(2)}, u32[]{:S(2)}) collective-permute-start(f32[8,8,256]{2,1,0:T(8,128)S(1)} %get-tuple-element.24), channel_id=1, source_target_pairs={{1,0},{2,1},{3,2},{4,3},{5,4},{6,5},{7,6},{9,8},{10,9},{11,10},{12... | collective-permute-start | bytes 196616 | tf_op jit(solution)/shard_map/ppermute | solution.py:436
  7.0 0.0 collective-permute-done.low_ref
  7.0 3.7 %collective-permute-done.1.high_ref = f32[8,8,256]{2,1,0:T(8,128)S(1)} collective-permute-done((f32[8,8,256]{2,1,0:T(8,128)S(1)}, f32[8,8,256]{2,1,0:T(8,128)S(1)}, u32[]{:S(2)}, u32[]{:S(2)}) %collective-permute-start.1) | collective-permute-done | bytes 65568 | tf_op jit(solution)/shard_map/ppermute | solution.py:436
  10.7 0.1 extend.1
  10.8 5.1 %collective-permute-start.3 = (f32[34,8,256]{2,1,0:T(8,128)S(1)}, f32[34,8,256]{2,1,0:T(8,128)S(1)}, u32[]{:S(2)}, u32[]{:S(2)}) collective-permute-start(f32[34,8,256]{2,1,0:T(8,128)S(1)} %get-tuple-element.28), channel_id=1, source_target_pairs={{8,16},{24,32},{40,48},{56,64},{72,80},{88,96},{104,112},{120,128}... | collective-permute-start | bytes 835592 | tf_op jit(solution)/shard_map/ppermute | solution.py:441
  15.9 2.8 %collective-permute-start.2 = (f32[34,8,256]{2,1,0:T(8,128)S(1)}, f32[34,8,256]{2,1,0:T(8,128)S(1)}, u32[]{:S(2)}, u32[]{:S(2)}) collective-permute-start(f32[34,8,256]{2,1,0:T(8,128)S(1)} %get-tuple-element.25.own_ref), channel_id=1, source_target_pairs={{0,8},{16,24},{32,40},{48,56},{64,72},{80,88},{96,104},{112,120},{... | collective-permute-start | bytes 835592 | tf_op jit(solution)/shard_map/ppermute | solution.py:441
  18.7 1.4 %collective-permute-done.3.next_ref = f32[34,8,256]{2,1,0:T(8,128)S(1)} collective-permute-done((f32[34,8,256]{2,1,0:T(8,128)S(1)}, f32[34,8,256]{2,1,0:T(8,128)S(1)}, u32[]{:S(2)}, u32[]{:S(2)}) %collective-permute-start.3) | collective-permute-done | bytes 278560 | tf_op jit(solution)/shard_map/ppermute | solution.py:441
  20.1 0.0 collective-permute-done.2.same_ref
  20.1 2.4 %basis.1 = (f32[16,128]{1,0:T(8,128)}, f32[3,5,24,256]{3,2,1,0:T(8,128)S(1)}, f32[4,24,256]{2,1,0:T(8,128)S(1)}) custom-call(f32[34,8,256]{2,1,0:T(8,128)S(1)} %get-tuple-element.25.own_ref, f32[4,24,256]{2,1,0:T(8,128)S(1)} %get-tuple-element.26.free_ref, f32[4,24,256]{2,1,0:T(8,128)S(1)} %get-tuple-element.27.rhs_ref, ...), custom_call_target="tpu_custom_call" | custom-call | bytes 1048576 | tf_op jit(solution)/shard_map/basis/pallas_call | solution.py:450
  22.5 7.4 %all-to-all-start = ((f32[16,1,128]{2,1,0:T(1,128)}), f32[16,1,128]{2,1,0:T(1,128)S(1)}, u32[]{:S(2)}, u32[]{:S(2)}) async-start(f32[16,1,128]{2,1,0:T(1,128)} %bitcast.1), calls=%async_computation | async-start | bytes 16384 | tf_op jit(solution)/shard_map/all_to_all | solution.py:512
  29.9 0.6 %integrand.1 = (f32[3,4,24,256]{3,2,1,0:T(8,128)S(1)}, f32[3,24,256]{2,1,0:T(8,128)S(1)}, f32[3,24,256]{2,1,0:T(8,128)S(1)}) custom-call(f32[3,5,24,256]{3,2,1,0:T(8,128)S(1)} %get-tuple-element.30.basis_ref, f32[4,24,256]{2,1,0:T(8,128)S(1)} %get-tuple-element.31.solid_ref, f32[4,24,256]{2,1,0:T(8,128)S(1)} %get-tuple-element.32.warmth_ref, ...), custom_call_target="tpu_custom_call" | custom-call | bytes 1048576 | tf_op jit(solution)/shard_map/integrand/pallas_call | solution.py:450
  30.6 2.0 %collective-permute-start.4 = (f32[3,24,256]{2,1,0:T(8,128)S(1)}, f32[3,24,256]{2,1,0:T(8,128)S(1)}, u32[]{:S(2)}, u32[]{:S(2)}) collective-permute-start(f32[3,24,256]{2,1,0:T(8,128)S(1)} %get-tuple-element.34), channel_id=1, source_target_pairs={{0,8},{16,24},{32,40},{48,56},{64,72},{80,88},{96,104},{112,120},{... | collective-permute-start | bytes 221192 | tf_op jit(solution)/shard_map/ppermute | solution.py:441
  32.6 3.9 %collective-permute-start.5 = (f32[3,24,256]{2,1,0:T(8,128)S(1)}, f32[3,24,256]{2,1,0:T(8,128)S(1)}, u32[]{:S(2)}, u32[]{:S(2)}) collective-permute-start(f32[3,24,256]{2,1,0:T(8,128)S(1)} %get-tuple-element.35), channel_id=1, source_target_pairs={{8,16},{24,32},{40,48},{56,64},{72,80},{88,96},{104,112},{120,128}... | collective-permute-start | bytes 221192 | tf_op jit(solution)/shard_map/ppermute | solution.py:441
  36.5 0.3 all-to-all-done
  36.8 23.0 %all_to_all.22 = f32[32,1,128]{2,1,0:T(1,128)S(1)} all-to-all(f32[32,1,128]{2,1,0:T(1,128)S(1)} %bitcast.9), channel_id=1, replica_groups={{0,16,32,48,64,80,96,112,128,144,160,176,192,208,224,240,256,272,288,30..., dimensions={0} | all-to-all | bytes 32768 | tf_op jit(solution)/shard_map/all_to_all | solution.py:515
  59.8 0.0 collective-permute-done.4.same_ref
  59.8 0.0 collective-permute-done.5.next_ref
  59.9 0.9 %combine.1 = (f32[4,16,256]{2,1,0:T(8,128)}, f32[4,16,256]{2,1,0:T(8,128)}) custom-call(f32[32,128]{1,0:T(8,128)S(1)} %bitcast.8, f32[3,5,24,256]{3,2,1,0:T(8,128)S(1)} %get-tuple-element.30.basis_ref, f32[3,4,24,256]{3,2,1,0:T(8,128)S(1)} %get-tuple-element.33.scaled_ref, f32[3,24,256]{2,1,0:T(8,128)S(1)} %collective-permute-done.4.same_ref, ...), custom_call_target="tpu_custom_call" | custom-call | bytes 1048576 | tf_op jit(solution)/shard_map/combine/pallas_call | solution.py:450
  (1 shorter events, 0.0 us)
Async XLA Ops:
  1.6 5.4 %collective-permute-start = (f32[8,8,256]{2,1,0:T(8,128)S(1)}, f32[8,8,256]{2,1,0:T(8,128)S(1)}, u32[]{:S(2)}, u32[]{:S(2)}) collective-permute-start(f32[8,8,256]{2,1,0:T(8,128)S(1)} %get-tuple-element.23), channel_id=1, source_target_pairs={{0,1},{1,2},{2,3},{3,4},{4,5},{5,6},{6,7},{8,9},{9,10},{10,11},{11... | collective-permute-start | bytes 196616 | tf_op jit(solution)/shard_map/ppermute | solution.py:436
  5.7 5.0 %collective-permute-start.1 = (f32[8,8,256]{2,1,0:T(8,128)S(1)}, f32[8,8,256]{2,1,0:T(8,128)S(1)}, u32[]{:S(2)}, u32[]{:S(2)}) collective-permute-start(f32[8,8,256]{2,1,0:T(8,128)S(1)} %get-tuple-element.24), channel_id=1, source_target_pairs={{1,0},{2,1},{3,2},{4,3},{5,4},{6,5},{7,6},{9,8},{10,9},{11,10},{12... | collective-permute-start | bytes 196616 | tf_op jit(solution)/shard_map/ppermute | solution.py:436
  10.8 9.3 %collective-permute-start.3 = (f32[34,8,256]{2,1,0:T(8,128)S(1)}, f32[34,8,256]{2,1,0:T(8,128)S(1)}, u32[]{:S(2)}, u32[]{:S(2)}) collective-permute-start(f32[34,8,256]{2,1,0:T(8,128)S(1)} %get-tuple-element.28), channel_id=1, source_target_pairs={{8,16},{24,32},{40,48},{56,64},{72,80},{88,96},{104,112},{120,128}... | collective-permute-start | bytes 835592 | tf_op jit(solution)/shard_map/ppermute | solution.py:441
  15.9 4.2 %collective-permute-start.2 = (f32[34,8,256]{2,1,0:T(8,128)S(1)}, f32[34,8,256]{2,1,0:T(8,128)S(1)}, u32[]{:S(2)}, u32[]{:S(2)}) collective-permute-start(f32[34,8,256]{2,1,0:T(8,128)S(1)} %get-tuple-element.25.own_ref), channel_id=1, source_target_pairs={{0,8},{16,24},{32,40},{48,56},{64,72},{80,88},{96,104},{112,120},{... | collective-permute-start | bytes 835592 | tf_op jit(solution)/shard_map/ppermute | solution.py:441
  22.5 14.3 %all-to-all-start = ((f32[16,1,128]{2,1,0:T(1,128)}), f32[16,1,128]{2,1,0:T(1,128)S(1)}, u32[]{:S(2)}, u32[]{:S(2)}) async-start(f32[16,1,128]{2,1,0:T(1,128)} %bitcast.1), calls=%async_computation | async-start | bytes 16384 | tf_op jit(solution)/shard_map/all_to_all | solution.py:512
  30.6 29.3 %collective-permute-start.4 = (f32[3,24,256]{2,1,0:T(8,128)S(1)}, f32[3,24,256]{2,1,0:T(8,128)S(1)}, u32[]{:S(2)}, u32[]{:S(2)}) collective-permute-start(f32[3,24,256]{2,1,0:T(8,128)S(1)} %get-tuple-element.34), channel_id=1, source_target_pairs={{0,8},{16,24},{32,40},{48,56},{64,72},{80,88},{96,104},{112,120},{... | collective-permute-start | bytes 221192 | tf_op jit(solution)/shard_map/ppermute | solution.py:441
  32.6 27.3 %collective-permute-start.5 = (f32[3,24,256]{2,1,0:T(8,128)S(1)}, f32[3,24,256]{2,1,0:T(8,128)S(1)}, u32[]{:S(2)}, u32[]{:S(2)}) collective-permute-start(f32[3,24,256]{2,1,0:T(8,128)S(1)} %get-tuple-element.35), channel_id=1, source_target_pairs={{8,16},{24,32},{40,48},{56,64},{72,80},{88,96},{104,112},{120,128}... | collective-permute-start | bytes 221192 | tf_op jit(solution)/shard_map/ppermute | solution.py:441
